TPU v7x, 256 devices: a whole 4x4x8 slice. The times are simulated.
256 devices in a mesh: fsdp: 64 (over y, z, core), rep: 4 (over x).
Axes of the slice: x: 4, y: 4, z: 8, core: 2. Of those that a mesh axis runs over, the one named last changes fastest.
Arguments:
- grad_parts: bfloat16 [4, 80, 1024, 1024], P('rep', None, 'fsdp'), may hold values from -6 to 6
- moment: float32 [80, 1024, 1024], P(None, 'fsdp', 'rep'), may hold values from 0.001 to 3000, as said below
- owner: int32 [80], replicated, may hold values from 0 to 63, as said below
- left_root: bfloat16 [64, 3, 1024, 1024], P('fsdp'), may hold values from -0.5 to 2.02, as said below
- right_root: bfloat16 [64, 3, 1024, 1024], P('fsdp', None, None, 'rep'), may hold values from -0.5 to 2.02, as said below
Outputs:
- update: float32 [80, 1024, 1024], P(None, 'fsdp', 'rep')
Inputs may be any that keep to these rules, and one draw needn't show every extreme that they name: `owner`: no fsdp index owns more than 3 blocks, and in every draw one index owns exactly 3. `left_root`: positive on the diagonal. Slot s of owner o holds the factor of the s-th block (in increasing block order) that o owns; other slots are unused. `right_root`: positive on the diagonal. Slots as for left_root. `moment`: Positive.
All inputs are finite; a program needn't handle non-finite values.
Results may differ from a plain program's by a relative error of at most 0.017.
Values may be sent and summed in bfloat16 or wider, within the bound.
No kernel may reach another device: no remote copies, remote signals or barrier semaphores. Data moves between devices by JAX's collectives and lax.ppermute only.
A program may use at most 128 MiB of HBM per device.

v0:
```python
import jax
import jax.numpy as jnp
from jax import lax
from jax.sharding import PartitionSpec as P

second_decay = 0.99
adam_epsilon = 1e-08
norm_epsilon = 1e-06


def block_slots(owner):
    count = owner.shape[0]
    numbers = jnp.arange(count, dtype=jnp.int32)
    same = owner[:, None] == owner[None, :]
    earlier = numbers[None, :] < numbers[:, None]
    return jnp.sum(jnp.where(same & earlier, 1, 0), axis=1).astype(jnp.int32)


def pack_blocks(pieces, owner, slot, owners, slots_each):
    count = pieces.shape[0]
    numbers = jnp.arange(count, dtype=jnp.int32)
    target = slot * owners + owner
    places = jnp.arange(owners * slots_each, dtype=jnp.int32)
    matched = places[:, None] == target[None, :]
    source = jnp.sum(jnp.where(matched, numbers[None, :], 0), axis=1) + jnp.where(
        jnp.any(matched, axis=1), 0, count
    )
    padded = jnp.concatenate([pieces, jnp.zeros((1,) + pieces.shape[1:], pieces.dtype)], axis=0)
    taken = jnp.take(padded, source, axis=0)
    return taken.reshape(slots_each, owners * pieces.shape[1], pieces.shape[2])


def shards(grad_parts, moment, owner, left_root, right_root):
    owners = lax.axis_size("fsdp")
    slots_each = left_root.shape[1]
    gradient = lax.psum_scatter(
        grad_parts[0].astype(jnp.float32).astype(jnp.bfloat16),
        "rep",
        scatter_dimension=2,
        tiled=True,
    ).astype(jnp.float32)
    second = second_decay * moment + (1.0 - second_decay) * gradient * gradient
    adam_direction = gradient / (jnp.sqrt(second) + adam_epsilon)
    adam_part = jnp.sum(adam_direction * adam_direction, axis=(1, 2))
    adam_total = lax.psum(adam_part, ("fsdp", "rep"))
    gradient_low = gradient.astype(jnp.bfloat16)
    slot = block_slots(owner)
    left = left_root[0]
    right = right_root[0]
    full_rows = lax.all_gather(gradient_low, "rep", axis=2, tiled=True)
    owned = lax.all_to_all(
        pack_blocks(full_rows, owner, slot, owners, slots_each),
        "fsdp",
        split_axis=1,
        concat_axis=1,
        tiled=True,
    )
    inner_sum = jnp.einsum("sij,sjk->sik", owned, right, preferred_element_type=jnp.float32)
    inner = inner_sum.astype(jnp.bfloat16)
    shampoo = jnp.einsum("sij,sjk->sik", left, inner, preferred_element_type=jnp.float32).astype(
        jnp.bfloat16
    )
    returned = lax.all_to_all(shampoo, "fsdp", split_axis=1, concat_axis=0, tiled=True)
    direction = jnp.take(returned, owner * slots_each + slot, axis=0)
    direction_wide = direction.astype(jnp.float32)
    shampoo_part = jnp.sum(direction_wide * direction_wide, axis=(1, 2))
    shampoo_total = lax.psum(shampoo_part, ("fsdp", "rep"))
    ratio = jnp.sqrt(adam_total) / (jnp.sqrt(shampoo_total) + norm_epsilon)
    return direction_wide * ratio[:, None, None]


def solution(mesh):
    in_specs = (
        P("rep", None, "fsdp", None),
        P(None, "fsdp", "rep"),
        P(),
        P("fsdp", None, None, None),
        P("fsdp", None, None, "rep"),
    )
    out_specs = P(None, "fsdp", "rep")
    return jax.shard_map(shards, mesh=mesh, in_specs=in_specs, out_specs=out_specs, check_vma=False)
```

profile of v0, /device:TPU:1, one launch (start us, length us, event | category | flops | bytes accessed | tf_op | source)
XLA Modules:
  0.0 480.2 jit_solution(2318982923702803209)
XLA Ops:
  6.5 0.0 copy-start
  6.5 0.0 reduce-scatter.2.cloned.1.call-start
  6.5 0.7 reduce-scatter.2.cloned.1.call-update
  7.3 0.0 all-gather.2.cloned.1.call-start
  7.3 43.0 %reduce-scatter.2.cloned.1.call-done = bf16[80,16,256]{2,1,0:T(8,128)(2,1)} async-done(((bf16[80,16,1024]{2,1,0:T(8,128)(2,1)}), bf16[80,16,256]{2,1,0:T(8,128)(2,1)}) %reduce-scatter.2.cloned.1.call-update) | async-done | bytes 655376 | tf_op jit(solution)/shard_map/reduce_scatter | solution.py:36
  50.3 0.0 all-gather.2.cloned.1.call-update
  50.3 0.0 copy-done.3
  50.3 0.2 select_reduce_fusion.1
  50.5 0.1 fusion.24
  50.6 0.1 select_reduce_fusion
  50.7 0.1 add.83
  50.8 0.1 broadcast_in_dim.78
  50.9 0.1 broadcast_in_dim.79
  51.1 41.3 %all-gather.2.cloned.1.call-done = bf16[80,16,1024]{2,1,0:T(8,128)(2,1)} async-done(((bf16[80,16,256]{2,1,0:T(8,128)(2,1)}), bf16[80,16,1024]{2,1,0:T(8,128)(2,1)}) %all-gather.2.cloned.1.call-update) | async-done | bytes 2621456 | tf_op jit(solution)/shard_map/all_gather | solution.py:50
  92.3 3.7 concatenate.3
  96.1 9.6 %gather_fusion = bf16[192,16,1024]{2,1,0:T(8,128)(2,1)} fusion(bf16[81,16,1024]{2,1,0:T(8,128)(2,1)} %concatenate.3, s32[1024]{0:T(1024)S(1)} %pad_clamp_fusion.1), kind=kCustom, calls=%fused_computation | custom fusion | bytes 12583680 | tf_op jit(solution)/shard_map/jit(_take)/gather | solution.py:29
  105.7 6.7 %bitcast_select_fusion = bf16[3,1024,1024]{2,1,0:T(8,128)(2,1)} fusion(pred[3,1024]{1,0:T(4,128)(4,1)S(1)} %broadcast_in_dim.79, bf16[3,1024,1024]{2,1,0:T(8,128)(2,1)} %bitcast.24), kind=kLoop, calls=%fused_computation.4 | loop fusion | flops 3145728 | bytes 12585984 | tf_op jit(solution)/shard_map/jit(_take)/select_n | solution.py:29
  112.4 11.4 %copy.20 = bf16[3,1024,1024]{2,0,1:T(4,128)(2,1)} copy(bf16[3,1024,1024]{2,1,0:T(8,128)(2,1)} %bitcast_select_fusion) | data formatting | bytes 12582912 | tf_op jit(solution)/shard_map/jit(_take)/select_n | solution.py:29
  123.8 197.7 %all_to_all.23 = bf16[3,1024,1024]{2,0,1:T(4,128)(2,1)} all-to-all(bf16[3,1024,1024]{2,0,1:T(4,128)(2,1)} %copy.20), channel_id=1, replica_groups=mesh['fsdp'=64,'rep'=4] {'fsdp'}, dimensions={1} | all-to-all | bytes 12582912 | tf_op jit(solution)/shard_map/all_to_all | solution.py:51
  321.6 0.0 copy-done
  321.6 9.5 %fusion.11 = bf16[3,1024,256]{1,2,0:T(8,128)(2,1)S(1)} fusion(bf16[1,3,1024,1024]{3,2,1,0:T(8,128)(2,1)} %param.8, bf16[3,1024,1024]{2,0,1:T(4,128)(2,1)} %all_to_all.23, bf16[1,3,1024,256]{3,2,1,0:T(8,128)(2,1)S(1)} %copy-done), kind=kOutput, calls=%fused_computation.14 | convolution fusion | flops 3222798336 | bytes 15728640 | tf_op jit(solution)/shard_map/sij,sjk->sik/dot_general | solution.py:60
  331.0 2.6 copy.23
  333.6 6.1 %all-to-all-start.1 = ((bf16[3,1024,256]{2,0,1:T(4,128)(2,1)}), bf16[3,1024,256]{2,0,1:T(4,128)(2,1)}, u32[]{:S(2)}, u32[]{:S(2)}) async-start(bf16[3,1024,256]{2,0,1:T(4,128)(2,1)} %copy.23), calls=%async_computation.2 | async-start | bytes 4194304 | tf_op jit(solution)/shard_map/all_to_all | solution.py:63
  339.8 0.0 copy-done.1
  339.8 1.0 fusion.19
  340.8 50.1 %all-to-all-done.1 = bf16[3,1024,256]{2,0,1:T(4,128)(2,1)} async-done(((bf16[3,1024,256]{2,0,1:T(4,128)(2,1)}), bf16[3,1024,256]{2,0,1:T(4,128)(2,1)}, u32[]{:S(2)}, u32[]{:S(2)}) %all-to-all-start.1) | async-done | bytes 1572896 | tf_op jit(solution)/shard_map/all_to_all | solution.py:63
  390.9 1.8 copy.24
  392.7 1.3 copy.25
  394.0 2.0 gather_fusion.1
  396.0 1.2 fusion.14
  397.2 74.8 %all-reduce.1 = (f32[80]{0:T(128)S(1)}, f32[80]{0:T(128)S(1)}) all-reduce(f32[80]{0:T(128)S(1)} %fusion.14, f32[80]{0:T(128)S(1)} %fusion.19), channel_id=1, replica_groups=mesh['fsdp'=64,'rep'=4] {'fsdp','rep'}, use_global_device_ids=true, to_apply=%region_7.8 | all-reduce | flops 160 | bytes 1280 | tf_op jit(solution)/shard_map/psum | solution.py:67
  472.1 1.3 convert_multiply_fusion
  (12 shorter events, 0.1 us)
Async XLA Ops:
  6.5 315.0 %copy-start = (bf16[1,3,1024,256]{3,2,1,0:T(8,128)(2,1)S(1)}, bf16[1,3,1024,256]{3,2,1,0:T(8,128)(2,1)}, u32[]{:S(2)}) copy-start(bf16[1,3,1024,256]{3,2,1,0:T(8,128)(2,1)} %param.9) | copy-start | bytes 4718596
  6.5 43.8 %reduce-scatter.2.cloned.1.call-start = ((), (), s32[]{:S(2)}) async-start(), calls=%async_computation.3 | async-start | bytes 3276800 | tf_op jit(solution)/shard_map/reduce_scatter | solution.py:36
  6.5 43.8 %copy-start.3 = (s32[80]{0:T(128)S(1)}, s32[80]{0:T(128)}, u32[]{:S(2)}) copy-start(s32[80]{0:T(128)} %param.7) | copy-start | bytes 964
  7.3 85.1 %all-gather.2.cloned.1.call-start = ((), (), s32[]{:S(2)}) async-start(), calls=%async_computation.4 | async-start | bytes 3276800 | tf_op jit(solution)/shard_map/all_gather | solution.py:50
  333.6 6.2 %copy-start.1 = (bf16[80,16,256]{2,1,0:T(8,128)(2,1)S(1)}, bf16[80,16,256]{2,1,0:T(8,128)(2,1)}, u32[]{:S(2)}) copy-start(bf16[80,16,256]{2,1,0:T(8,128)(2,1)} %reduce-scatter.2.cloned.1.call-done) | copy-start | bytes 1966084
  333.6 6.2 %copy-start.2 = (f32[80,16,256]{2,1,0:T(8,128)S(1)}, f32[80,16,256]{2,1,0:T(8,128)}, u32[]{:S(2)}) copy-start(f32[80,16,256]{2,1,0:T(8,128)} %param.6) | copy-start | bytes 3932164
  333.6 57.3 %all-to-all-start.1 = ((bf16[3,1024,256]{2,0,1:T(4,128)(2,1)}), bf16[3,1024,256]{2,0,1:T(4,128)(2,1)}, u32[]{:S(2)}, u32[]{:S(2)}) async-start(bf16[3,1024,256]{2,0,1:T(4,128)(2,1)} %copy.23), calls=%async_computation.2 | async-start | bytes 4194304 | tf_op jit(solution)/shard_map/all_to_all | solution.py:63
Sparse Core Ops, SparseCore 0:
  9.9 40.3 reduce-scatter.1
  52.1 40.2 all-gather.1
where the time goes:
time: 481 us; the launch traced here: 480 us
  blocking collectives  273 us (57%)
  waiting for transfers between devices  135 us (28%)
  local copies, waits for them, and re-layouts  32.7 us (7%)
  between operations  13.5 us (3%)
  other arithmetic  10.6 us (2%)
  matrix products  9.46 us (2%)
  starting transfers between devices  6.18 us (1%)
    all_to_all x1, blocking collectives, shards(): lax.all_to_all(pack_blocks(full_rows, owner, slot, owners, slots_each), '...  198 us
    psum x1, blocking collectives, shards(): shampoo_total = lax.psum(shampoo_part, ('fsdp', 'rep'))  74.8 us
    all_to_all x1, waiting for transfers between devices, shards(): lax.all_to_all(shampoo, 'fsdp', split_axis=1, concat_axis=0, tiled=True)  50.1 us
    reduce_scatter x1, waiting for transfers between devices, shards(): lax.psum_scatter(grad_parts[0].astype(jnp.float32).astype(jnp.bfloat16),...  43 us
    all_gather x1, waiting for transfers between devices, shards(): full_rows = lax.all_gather(gradient_low, 'rep', axis=2, tiled=True)  41.3 us
    select_n x1, local copies, waits for them, and re-layouts, pack_blocks(): taken = jnp.take(padded, source, axis=0)  11.4 us
    gather x1, local copies, waits for them, and re-layouts, pack_blocks(): taken = jnp.take(padded, source, axis=0)  9.65 us
  transfers between devices with their start and end apart: 3, of which 3 were waited for; matrix products, arithmetic and copies ran while one was open for 0% of the time, Pallas kernels for 0%

commit v1 on v0

v1 whole, which is shorter than its diff:
```python
import jax
import jax.numpy as jnp
from jax import lax
from jax.experimental import pallas as pl
from jax.experimental.pallas import tpu as pltpu
from jax.sharding import PartitionSpec as P

second_decay = 0.99
adam_epsilon = 1e-08
norm_epsilon = 1e-06

REP = 4
OWNERS = 64
CAP = 3
VMEM = pl.BlockSpec(memory_space=pltpu.VMEM)
SMEM = pl.BlockSpec(memory_space=pltpu.SMEM)
ROOM = 48 * 1024 * 1024


def block_slots(owner):
    count = owner.shape[0]
    numbers = jnp.arange(count, dtype=jnp.int32)
    same = owner[:, None] == owner[None, :]
    earlier = numbers[None, :] < numbers[:, None]
    return jnp.sum(jnp.where(same & earlier, 1, 0), axis=1).astype(jnp.int32)


def shift(value, step):
    return lax.ppermute(value, "rep", [(i, (i + step) % REP) for i in range(REP)])


def wide(value):
    return value.astype(jnp.float32)


def sum_over_rep(pieces):
    middle = pieces[0].shape[0] // 2
    top, bottom = slice(0, middle), slice(middle, None)
    far_right = shift(pieces[2][top], 1)
    far_left = shift(pieces[2][bottom], 3)
    near_right = shift(pieces[1][bottom], 1)
    near_left = shift(pieces[3][top], 3)
    on_right = (wide(pieces[1][top]) + wide(far_right)).astype(jnp.bfloat16)
    on_left = (wide(pieces[3][bottom]) + wide(far_left)).astype(jnp.bfloat16)
    last_right = shift(on_right, 1)
    last_left = shift(on_left, 3)
    return (pieces[0], near_left, last_right, near_right, last_left), (on_right, on_left)


def gather_over_rep(value):
    middle = value.shape[1] // 2
    top, bottom = value[:, :middle], value[:, middle:]
    left_top = shift(top, 1)
    right_bottom = shift(bottom, 3)
    left_bottom = shift(bottom, 1)
    right_top = shift(top, 3)
    far_top = shift(left_top, 1)
    far_bottom = shift(right_bottom, 3)
    return value, left_top, left_bottom, far_top, far_bottom, right_top, right_bottom


def sum_pack_kernel(source, own, near_left, last_right, near_right, last_left, low, out):
    middle = near_left.shape[0]

    @pl.loop(0, middle)
    def _(b):
        low[b] = (wide(own[b]) + (wide(near_left[b]) + wide(last_right[b]))).astype(jnp.bfloat16)
        c = middle + b
        low[c] = (wide(own[c]) + (wide(near_right[b]) + wide(last_left[b]))).astype(jnp.bfloat16)

    @pl.loop(0, OWNERS)
    def _(o):
        for s in range(CAP):
            out[o, s] = low[source[s * OWNERS + o]]


def sum_pack(source, terms):
    blocks, rows, columns = terms[0].shape
    return pl.pallas_call(
        sum_pack_kernel,
        out_shape=[
            jax.ShapeDtypeStruct((blocks, rows, columns), jnp.bfloat16),
            jax.ShapeDtypeStruct((OWNERS, CAP, rows, columns), jnp.bfloat16),
        ],
        in_specs=[SMEM] + [VMEM] * 5,
        out_specs=[VMEM, VMEM],
        compiler_params=pltpu.CompilerParams(vmem_limit_bytes=ROOM),
        name="sum_pack",
    )(source, *terms)


def left_kernel(first, place, gradient, left, out, wide_rows):
    halves, size, half = wide_rows.shape
    width = halves * half
    rows = gradient.shape[2]
    part = rows // REP
    s = pl.program_id(0)
    low = gradient[:, first + s].reshape(size, width)
    tile = size // 4
    for i in range(4):
        at = slice(i * tile, (i + 1) * tile)
        product = jnp.dot(left[0, at, :], low, preferred_element_type=jnp.float32)
        for h in range(halves):
            wide_rows[h, at, :] = product[:, h * half : (h + 1) * half]
    for target in range(REP):
        k = lax.rem(target + REP - place[0], REP)
        for j in range(part):
            for h in range(halves):
                strided = wide_rows[h, pl.ds(target * part + j, OWNERS, stride=rows), :]
                at = slice(j * OWNERS, (j + 1) * OWNERS), slice(h * half, (h + 1) * half)
                out[(k, 0) + at] = strided.astype(jnp.bfloat16)


def left_multiply(place, gradient, left, first, count):
    size, width = left.shape[1], gradient.shape[3]
    return pl.pallas_call(
        lambda *refs: left_kernel(first, *refs),
        grid=(count,),
        out_shape=jax.ShapeDtypeStruct((REP, count, size // REP, width), jnp.bfloat16),
        in_specs=[SMEM, VMEM, pl.BlockSpec((1, size, size), lambda i: (first + i, 0, 0))],
        out_specs=pl.BlockSpec((REP, 1, size // REP, width), lambda i: (0, i, 0, 0)),
        scratch_shapes=[pltpu.VMEM((width // 128, size, 128), jnp.float32)],
        compiler_params=pltpu.CompilerParams(vmem_limit_bytes=ROOM),
        cost_estimate=pl.CostEstimate(
            flops=count * 2 * size * size * width,
            bytes_accessed=count * 4 * size * size,
            transcendentals=0,
        ),
        name="left_multiply",
    )(place, gradient, left)


def right_kernel(place, *refs):
    pieces, rights = refs[:REP], refs[REP : REP + 7]
    out, total, full, wide_rows = refs[REP + 7 :]
    height, size = full.shape
    width = size // REP
    halves, _, half = wide_rows.shape
    rows = out.shape[2]
    part = rows // REP
    for k, piece in enumerate(pieces):
        at = pl.multiple_of(lax.rem(place[0] + (REP - k), REP) * width, width)
        full[:, pl.ds(at, width)] = piece[0]
    squares = jnp.zeros((8, width), jnp.float32)
    middle = size // 2
    for k in range(REP):
        if k == 0:
            product = jnp.dot(full[...], rights[0][0], preferred_element_type=jnp.float32)
        else:
            top, bottom = rights[2 * k - 1], rights[2 * k]
            product = jnp.dot(full[:, :middle], top[0], preferred_element_type=jnp.float32)
            product = product + jnp.dot(
                full[:, middle:], bottom[0], preferred_element_type=jnp.float32
            )
        squares = squares + jnp.sum((product * product).reshape(height // 8, 8, width), axis=0)
        for j in range(part):
            for h in range(halves):
                wide_rows[h, pl.ds(k * part + j, OWNERS, stride=rows), :] = product[
                    j * OWNERS : (j + 1) * OWNERS, h * half : (h + 1) * half
                ]
    for h in range(halves):
        low = wide_rows[h].astype(jnp.bfloat16).reshape(OWNERS, rows, half)
        out[:, 0, :, h * half : (h + 1) * half] = low
    total[0] = jnp.sum(squares, axis=0, keepdims=True)


def right_multiply(place, pieces, rights):
    count, height, width = pieces[0].shape
    size = rights[0].shape[1]
    rows = size // OWNERS
    return pl.pallas_call(
        right_kernel,
        grid=(count,),
        out_shape=[
            jax.ShapeDtypeStruct((OWNERS, count, rows, width), jnp.bfloat16),
            jax.ShapeDtypeStruct((count, 1, width), jnp.float32),
        ],
        in_specs=[SMEM]
        + [pl.BlockSpec((1, height, width), lambda i: (i, 0, 0))] * 4
        + [pl.BlockSpec((1,) + r.shape[1:], lambda i: (i, 0, 0)) for r in rights],
        out_specs=[
            pl.BlockSpec((OWNERS, 1, rows, width), lambda i: (0, i, 0, 0)),
            pl.BlockSpec((1, 1, width), lambda i: (i, 0, 0)),
        ],
        scratch_shapes=[
            pltpu.VMEM((height, size), jnp.bfloat16),
            pltpu.VMEM((width // 128, size, 128), jnp.float32),
        ],
        compiler_params=pltpu.CompilerParams(vmem_limit_bytes=ROOM),
        cost_estimate=pl.CostEstimate(
            flops=count * 2 * size * size * width,
            bytes_accessed=count * 4 * size * size,
            transcendentals=0,
        ),
        name="right_multiply",
    )(place, *pieces, *rights)


def split_kernel(owner, slot, back01, back2, out, held):
    _, groups, rows, _ = out.shape
    part = rows // REP

    held[:, :2] = back01[...]
    held[:, 2] = back2[:, 0]

    @pl.loop(0, groups)
    def _(g):
        parts = []
        for i in range(REP):
            b = g * REP + i
            parts.append(wide(held[owner[b], slot[b]]))
        for k in range(REP):
            joined = [p[k * part : (k + 1) * part] for p in parts]
            out[(REP - k) % REP, g] = jnp.concatenate(joined, axis=0).astype(jnp.bfloat16)


def split_blocks(owner, slot, back01, back2):
    blocks = owner.shape[0]
    _, _, rows, width = back01.shape
    return pl.pallas_call(
        split_kernel,
        out_shape=jax.ShapeDtypeStruct((REP, blocks // REP, rows, width), jnp.bfloat16),
        in_specs=[SMEM] * 2 + [VMEM] * 2,
        out_specs=VMEM,
        scratch_shapes=[pltpu.VMEM((OWNERS, CAP, rows, width), jnp.bfloat16)],
        compiler_params=pltpu.CompilerParams(vmem_limit_bytes=ROOM),
        name="split_blocks",
    )(owner, slot, back01, back2)


def join_kernel(place, ratio, own, first, second, third, out, held):
    groups, rows, _ = own.shape
    part = rows // REP
    for k, piece in enumerate((own, first, second, third)):
        held[lax.rem(place[0] + (REP - k), REP)] = piece[...]

    @pl.loop(0, groups)
    def _(g):
        parts = [wide(held[q, g]) for q in range(REP)]
        for i in range(REP):
            joined = [p[i * part : (i + 1) * part] for p in parts]
            out[g * REP + i] = jnp.concatenate(joined, axis=0) * ratio[g * REP + i]


def join_blocks(place, ratio, pieces):
    groups, rows, width = pieces[0].shape
    return pl.pallas_call(
        join_kernel,
        out_shape=jax.ShapeDtypeStruct((groups * REP, rows, width), jnp.float32),
        in_specs=[SMEM] * 2 + [VMEM] * 4,
        out_specs=VMEM,
        scratch_shapes=[pltpu.VMEM((REP, groups, rows, width), jnp.bfloat16)],
        compiler_params=pltpu.CompilerParams(vmem_limit_bytes=ROOM),
        name="join_blocks",
    )(place, ratio, *pieces)


def adam_squares(low, moment):
    gradient = wide(low)
    second = second_decay * moment + (1.0 - second_decay) * gradient * gradient
    direction = gradient / (jnp.sqrt(second) + adam_epsilon)
    return jnp.sum(direction * direction, axis=(1, 2))


def exchange(value):
    return lax.all_to_all(value, "fsdp", split_axis=0, concat_axis=0)


def after(value, *others):
    return lax.optimization_barrier((value, *others))[0]


def shards(grad_parts, moment, owner, left_root, right_root):
    place = lax.axis_index("rep")
    place_ref = place.astype(jnp.int32).reshape(1)
    blocks, rows, columns = moment.shape
    slot = block_slots(owner)
    numbers = jnp.arange(blocks, dtype=jnp.int32)
    target = slot * OWNERS + owner
    places = jnp.arange(OWNERS * CAP, dtype=jnp.int32)
    matched = places[:, None] == target[None, :]
    source = jnp.sum(jnp.where(matched, numbers[None, :], 0), axis=1)
    gradient = grad_parts[0]
    pieces = [
        lax.dynamic_slice(
            gradient, (0, 0, lax.rem(place + k, REP) * columns), (blocks, rows, columns)
        )
        for k in range(REP)
    ]
    terms, passing = sum_over_rep(pieces)
    rights01 = gather_over_rep(after(right_root[0, :2], *passing))
    low, packed = sum_pack(source, terms)
    owned = exchange(packed)
    adam = lax.psum(adam_squares(low, moment), "rep")

    def spread(sent):
        return [sent[0]] + [shift(sent[k], k) for k in (1, 2, 3)]

    sent01 = left_multiply(after(place_ref, *rights01), owned, left_root[0], 0, 2)
    held01 = spread(sent01)
    result01, square01 = right_multiply(place_ref, held01, rights01)
    back01 = exchange(result01)
    rights2 = gather_over_rep(after(right_root[0, 2:], *held01))
    sent2 = left_multiply(after(place_ref, *held01), owned, left_root[0], 2, 1)
    held2 = spread(sent2)
    result2, square2 = right_multiply(place_ref, held2, rights2)
    back2 = exchange(after(result2, back01))
    squares = lax.psum(jnp.sum(jnp.concatenate([square01, square2]), axis=(1, 2)), "rep")
    known = jnp.concatenate([adam, squares, jnp.zeros((128 - blocks - CAP,), jnp.float32)])
    known = jnp.broadcast_to(known[None, None, :], (OWNERS, 1, 128))
    sent = split_blocks(owner, slot, back01, back2)
    known = exchange(after(known, sent))[:, 0]
    adam_norm = jnp.sqrt(jnp.sum(known[:, :blocks], axis=0))
    by_place = jnp.transpose(known[:, blocks : blocks + CAP]).reshape(OWNERS * CAP, 1)
    shampoo_norm = jnp.sqrt(jnp.sum(jnp.where(matched, by_place, 0.0), axis=0))
    ratio = adam_norm / (shampoo_norm + norm_epsilon)
    held = spread(sent)
    return join_blocks(place_ref, ratio, held)


def solution(mesh):
    in_specs = (
        P("rep", None, "fsdp", None),
        P(None, "fsdp", "rep"),
        P(),
        P("fsdp", None, None, None),
        P("fsdp", None, None, "rep"),
    )
    out_specs = P(None, "fsdp", "rep")
    return jax.shard_map(shards, mesh=mesh, in_specs=in_specs, out_specs=out_specs, check_vma=False)
```

time: 481 us -> 199 us (0.41)
  blocking collectives: 273 us -> 7.17 us
  starting transfers between devices: 6.18 us -> 69.3 us
  waiting for transfers between devices: 135 us -> 90 us
  local copies, waits for them, and re-layouts: 32.7 us -> 10.2 us
  Pallas kernels: 0 us -> 17.3 us
  between operations: 13.5 us -> 0.27 us
  matrix products: 9.46 us -> 0 us
  other arithmetic: 10.6 us -> 4.26 us
    all_to_all x1 -> x0, blocking collectives: 198 us -> none  [shards(): lax.all_to_all(pack_blocks(full_rows, owner, slot, owners, slots_each), '...]
    ppermute x0 -> x27, waiting for transfers between devices: none -> 75.1 us  [shift(): lax.ppermute(value, 'rep', [(i, (i + step) % REP) for i in range(REP)])]
    psum x1, blocking collectives: 74.8 us -> 7.17 us  [shards(): lax.psum(jnp.sum(jnp.concatenate([square01, square2]), axis=(1, 2)), 'rep')]
    reduce_scatter x1 -> x0, waiting for transfers between devices: 43 us -> none  [shards(): lax.psum_scatter(grad_parts[0].astype(jnp.float32).astype(jnp.bfloat16),...]
    all_gather x1 -> x0, waiting for transfers between devices: 41.3 us -> none  [shards(): full_rows = lax.all_gather(gradient_low, 'rep', axis=2, tiled=True)]
    all_to_all x1 -> x4, starting transfers between devices: 6.13 us -> 41.3 us  [exchange(): return lax.all_to_all(value, 'fsdp', split_axis=0, concat_axis=0)]
    all_to_all x1 -> x4, waiting for transfers between devices: 50.1 us -> 14.9 us  [exchange(): return lax.all_to_all(value, 'fsdp', split_axis=0, concat_axis=0)]
    ppermute x0 -> x27, starting transfers between devices: none -> 27.9 us  [shift(): lax.ppermute(value, 'rep', [(i, (i + step) % REP) for i in range(REP)])]
  transfers between devices with their start and end apart: 3 -> 31, of which waited for: 3 -> 17; matrix products, arithmetic and copies ran while one was open for 0% -> 4% of each run, Pallas kernels for 0% -> 2%
where the time goes in v1:
time: 199 us; the launch traced here: 198 us
  waiting for transfers between devices  90 us (45%)
  starting transfers between devices  69.3 us (35%)
  Pallas kernels  17.3 us (9%)
  local copies, waits for them, and re-layouts  10.2 us (5%)
  blocking collectives  7.17 us (4%)
  other arithmetic  4.26 us (2%)
    ppermute x27, waiting for transfers between devices, shift(): lax.ppermute(value, 'rep', [(i, (i + step) % REP) for i in range(REP)])  75.1 us
    all_to_all x4, starting transfers between devices, exchange(): return lax.all_to_all(value, 'fsdp', split_axis=0, concat_axis=0)  41.3 us
    ppermute x27, starting transfers between devices, shift(): lax.ppermute(value, 'rep', [(i, (i + step) % REP) for i in range(REP)])  27.9 us
    all_to_all x4, waiting for transfers between devices, exchange(): return lax.all_to_all(value, 'fsdp', split_axis=0, concat_axis=0)  14.9 us
    psum x1, blocking collectives, shards(): lax.psum(jnp.sum(jnp.concatenate([square01, square2]), axis=(1, 2)), 'rep')  7.17 us
    pallas_call x2, Pallas kernels, left_multiply(): pl.pallas_call(lambda *refs: left_kernel(first, *refs), grid=(count,), ou...  6.44 us
    pallas_call x2, Pallas kernels, right_multiply(): pl.pallas_call(right_kernel, grid=(count,), out_shape=[jax.ShapeDtypeStru...  5.29 us
    unnamed x22, local copies, waits for them, and re-layouts  4.16 us
  transfers between devices with their start and end apart: 31, of which 17 were waited for; matrix products, arithmetic and copies ran while one was open for 4% of the time, Pallas kernels for 2%

profile of v1, /device:TPU:1, one launch (start us, length us, event | category | flops | bytes accessed | tf_op | source)
XLA Modules:
  0.0 198.4 jit_solution(9573671983014135410)
XLA Ops:
  1.4 2.1 %collective-permute-start.1 = (bf16[40,16,256]{2,1,0:T(8,128)(2,1)S(1)}, bf16[40,16,256]{2,1,0:T(8,128)(2,1)S(1)}, u32[]{:S(2)}, u32[]{:S(2)}) collective-permute-start(bf16[40,16,256]{2,1,0:T(8,128)(2,1)S(1)} %get-tuple-element.32), channel_id=1, source_target_pairs={{0,1},{1,2},{2,3},{3,0},{4,5},{5,6},{6,7},{7,4},{8,9},{9,10},{10,1... | collective-permute-start | bytes 983048 | tf_op jit(solution)/shard_map/ppermute | solution.py:29
  5.0 2.6 %collective-permute-start = (bf16[40,16,256]{2,1,0:T(8,128)(2,1)S(1)}, bf16[40,16,256]{2,1,0:T(8,128)(2,1)S(1)}, u32[]{:S(2)}, u32[]{:S(2)}) collective-permute-start(bf16[40,16,256]{2,1,0:T(8,128)(2,1)S(1)} %get-tuple-element.33), channel_id=1, source_target_pairs={{0,3},{1,0},{2,1},{3,2},{4,7},{5,4},{6,5},{7,6},{8,11},{9,8},{10,9... | collective-permute-start | bytes 983048 | tf_op jit(solution)/shard_map/ppermute | solution.py:29
  7.7 2.2 %collective-permute-done.1 = bf16[40,16,256]{2,1,0:T(8,128)(2,1)S(1)} collective-permute-done((bf16[40,16,256]{2,1,0:T(8,128)(2,1)S(1)}, bf16[40,16,256]{2,1,0:T(8,128)(2,1)S(1)}, u32[]{:S(2)}, u32[]{:S(2)}) %collective-permute-start.1) | collective-permute-done | bytes 327712 | tf_op jit(solution)/shard_map/ppermute | solution.py:29
  12.7 2.0 %collective-permute-start.5 = (bf16[40,16,256]{2,1,0:T(8,128)(2,1)S(1)}, bf16[40,16,256]{2,1,0:T(8,128)(2,1)S(1)}, u32[]{:S(2)}, u32[]{:S(2)}) collective-permute-start(bf16[40,16,256]{2,1,0:T(8,128)(2,1)S(1)} %get-tuple-element.35), channel_id=1, source_target_pairs={{0,3},{1,0},{2,1},{3,2},{4,7},{5,4},{6,5},{7,6},{8,11},{9,8},{10,9... | collective-permute-start | bytes 983048 | tf_op jit(solution)/shard_map/ppermute | solution.py:29
  18.4 7.0 %collective-permute-done.5.last_left = bf16[40,16,256]{2,1,0:T(8,128)(2,1)S(1)} collective-permute-done((bf16[40,16,256]{2,1,0:T(8,128)(2,1)S(1)}, bf16[40,16,256]{2,1,0:T(8,128)(2,1)S(1)}, u32[]{:S(2)}, u32[]{:S(2)}) %collective-permute-start.5) | collective-permute-done | bytes 327712 | tf_op jit(solution)/shard_map/ppermute | solution.py:29
  25.5 2.6 %sum_pack.1 = (bf16[80,16,256]{2,1,0:T(8,128)(2,1)S(1)}, bf16[64,3,16,256]{3,2,1,0:T(8,128)(2,1)}) custom-call(s32[192]{0:T(256)S(1)} %select_reduce_fusion.1.source, bf16[80,16,256]{2,1,0:T(8,128)(2,1)S(1)} %dynamic-slice_bitcast_fusion.own, bf16[40,16,256]{2,1,0:T(8,128)(2,1)S(1)} %collective-permute-done.near_left, ...), custom_call_target="tpu_custom_call" | custom-call | tf_op jit(solution)/shard_map/sum_pack/pallas_call | solution.py:79
  28.1 13.9 %all-to-all-start = ((bf16[64,3,16,256]{3,2,1,0:T(8,128)(2,1)}), bf16[64,3,16,256]{3,2,1,0:T(8,128)(2,1)S(1)}, u32[]{:S(2)}, u32[]{:S(2)}) async-start(bf16[64,3,16,256]{3,2,1,0:T(8,128)(2,1)} %get-tuple-element.20), calls=%async_computation | async-start | bytes 3145728 | tf_op jit(solution)/shard_map/all_to_all | solution.py:266
  43.4 2.8 %collective-permute-start.9 = (bf16[2,512,256]{2,1,0:T(8,128)(2,1)S(1)}, bf16[2,512,256]{2,1,0:T(8,128)(2,1)S(1)}, u32[]{:S(2)}, u32[]{:S(2)}) collective-permute-start(bf16[2,512,256]{2,1,0:T(8,128)(2,1)S(1)} %get-tuple-element.41), channel_id=1, source_target_pairs={{0,3},{1,0},{2,1},{3,2},{4,7},{5,4},{6,5},{7,6},{8,11},{9,8},{10,9... | collective-permute-start | bytes 1572872 | tf_op jit(solution)/shard_map/ppermute | solution.py:29
  46.1 2.7 %collective-permute-start.11 = (bf16[2,512,256]{2,1,0:T(8,128)(2,1)S(1)}, bf16[2,512,256]{2,1,0:T(8,128)(2,1)S(1)}, u32[]{:S(2)}, u32[]{:S(2)}) collective-permute-start(bf16[2,512,256]{2,1,0:T(8,128)(2,1)S(1)} %get-tuple-element.42), channel_id=1, source_target_pairs={{0,3},{1,0},{2,1},{3,2},{4,7},{5,4},{6,5},{7,6},{8,11},{9,8},{10,9... | collective-permute-start | bytes 1572872 | tf_op jit(solution)/shard_map/ppermute | solution.py:29
  48.8 8.1 %collective-permute-done.9.refs_10_ = bf16[2,512,256]{2,1,0:T(8,128)(2,1)S(1)} collective-permute-done((bf16[2,512,256]{2,1,0:T(8,128)(2,1)S(1)}, bf16[2,512,256]{2,1,0:T(8,128)(2,1)S(1)}, u32[]{:S(2)}, u32[]{:S(2)}) %collective-permute-start.9) | collective-permute-done | bytes 524320 | tf_op jit(solution)/shard_map/ppermute | solution.py:29
  57.0 3.4 %collective-permute-start.10 = (bf16[2,512,256]{2,1,0:T(8,128)(2,1)S(1)}, bf16[2,512,256]{2,1,0:T(8,128)(2,1)S(1)}, u32[]{:S(2)}, u32[]{:S(2)}) collective-permute-start(bf16[2,512,256]{2,1,0:T(8,128)(2,1)S(1)} %collective-permute-done.9.refs_10_), channel_id=1, source_target_pairs={{0,3},{1,0},{2,1},{3,2},{4,7},{5,4},{6,5},{7,6},{8,11},{9,8},{10,9... | collective-permute-start | bytes 1572872 | tf_op jit(solution)/shard_map/ppermute | solution.py:29
  60.4 10.9 %collective-permute-done.7.refs_6_ = bf16[2,512,256]{2,1,0:T(8,128)(2,1)S(1)} collective-permute-done((bf16[2,512,256]{2,1,0:T(8,128)(2,1)S(1)}, bf16[2,512,256]{2,1,0:T(8,128)(2,1)S(1)}, u32[]{:S(2)}, u32[]{:S(2)}) %collective-permute-start.7) | collective-permute-done | bytes 524320 | tf_op jit(solution)/shard_map/ppermute | solution.py:29
  72.9 6.6 %collective-permute-done.10.refs_8_ = bf16[2,512,256]{2,1,0:T(8,128)(2,1)S(1)} collective-permute-done((bf16[2,512,256]{2,1,0:T(8,128)(2,1)S(1)}, bf16[2,512,256]{2,1,0:T(8,128)(2,1)S(1)}, u32[]{:S(2)}, u32[]{:S(2)}) %collective-permute-start.10) | collective-permute-done | bytes 524320 | tf_op jit(solution)/shard_map/ppermute | solution.py:29
  80.2 2.3 %collective-permute-done.8.refs_7_ = bf16[2,512,256]{2,1,0:T(8,128)(2,1)S(1)} collective-permute-done((bf16[2,512,256]{2,1,0:T(8,128)(2,1)S(1)}, bf16[2,512,256]{2,1,0:T(8,128)(2,1)S(1)}, u32[]{:S(2)}, u32[]{:S(2)}) %collective-permute-start.8) | collective-permute-done | bytes 524320 | tf_op jit(solution)/shard_map/ppermute | solution.py:29
  83.3 3.8 %left_multiply.2 = bf16[4,2,256,256]{3,2,1,0:T(8,128)(2,1)S(1)} custom-call(s32[1]{0:T(128)} %bitcast.refs_0_.place, bf16[64,3,16,256]{3,2,1,0:T(8,128)(2,1)S(1)} %all-to-all-done.refs_1_, bf16[3,1024,1024]{2,1,0:T(8,128)(2,1)} %bitcast.53), custom_call_target="tpu_custom_call" | custom-call | flops 1073741824 | bytes 8388608 | tf_op jit(solution)/shard_map/left_multiply/pallas_call | solution.py:116
  89.3 4.4 %collective-permute-done.14.refs_3_ = bf16[2,256,256]{2,1,0:T(8,128)(2,1)S(1)} collective-permute-done((bf16[2,256,256]{2,1,0:T(8,128)(2,1)S(1)}, bf16[2,256,256]{2,1,0:T(8,128)(2,1)S(1)}, u32[]{:S(2)}, u32[]{:S(2)}) %collective-permute-start.14) | collective-permute-done | bytes 262176 | tf_op jit(solution)/shard_map/ppermute | solution.py:29
  93.7 2.7 %collective-permute-done.13.refs_2_ = bf16[2,256,256]{2,1,0:T(8,128)(2,1)S(1)} collective-permute-done((bf16[2,256,256]{2,1,0:T(8,128)(2,1)S(1)}, bf16[2,256,256]{2,1,0:T(8,128)(2,1)S(1)}, u32[]{:S(2)}, u32[]{:S(2)}) %collective-permute-start.13) | collective-permute-done | bytes 262176 | tf_op jit(solution)/shard_map/ppermute | solution.py:29
  96.4 7.5 %collective-permute-done.12.refs_1_ = bf16[2,256,256]{2,1,0:T(8,128)(2,1)S(1)} collective-permute-done((bf16[2,256,256]{2,1,0:T(8,128)(2,1)S(1)}, bf16[2,256,256]{2,1,0:T(8,128)(2,1)S(1)}, u32[]{:S(2)}, u32[]{:S(2)}) %collective-permute-start.12) | collective-permute-done | bytes 262176 | tf_op jit(solution)/shard_map/ppermute | solution.py:29
  104.0 3.4 %right_multiply.2 = (bf16[64,2,16,256]{3,2,1,0:T(8,128)(2,1)S(1)}, f32[2,1,256]{2,1,0:T(1,128)S(1)}) custom-call(s32[1]{0:T(128)} %bitcast.refs_0_.place, bf16[2,256,256]{2,1,0:T(8,128)(2,1)S(1)} %get-tuple-element.40.refs_0_, bf16[2,256,256]{2,1,0:T(8,128)(2,1)S(1)} %collective-permute-done.12.refs_1_, ...), custom_call_target="tpu_custom_call" | custom-call | flops 1073741824 | bytes 8388608 | tf_op jit(solution)/shard_map/right_multiply/pallas_call | solution.py:171
  108.4 10.4 %all-to-all-start.1 = ((bf16[64,2,16,256]{3,2,1,0:T(8,128)(2,1)}), bf16[64,2,16,256]{3,2,1,0:T(8,128)(2,1)S(1)}, u32[]{:S(2)}, u32[]{:S(2)}) async-start(bf16[64,2,16,256]{3,2,1,0:T(8,128)(2,1)} %copy-done), calls=%async_computation.1 | async-start | bytes 2097152 | tf_op jit(solution)/shard_map/all_to_all | solution.py:266
  121.4 2.7 %left_multiply.3 = bf16[4,1,256,256]{3,2,1,0:T(8,128)(2,1)S(1)} custom-call(s32[1]{0:T(128)} %bitcast.refs_0_.place, bf16[64,3,16,256]{3,2,1,0:T(8,128)(2,1)S(1)} %all-to-all-done.refs_1_, bf16[3,1024,1024]{2,1,0:T(8,128)(2,1)} %bitcast.54), custom_call_target="tpu_custom_call" | custom-call | flops 536870912 | bytes 4194304 | tf_op jit(solution)/shard_map/left_multiply/pallas_call | solution.py:116
  126.6 3.6 %collective-permute-done.17.refs_3_ = bf16[1,256,256]{2,1,0:T(8,128)(2,1)S(1)} collective-permute-done((bf16[1,256,256]{2,1,0:T(8,128)(2,1)S(1)}, bf16[1,256,256]{2,1,0:T(8,128)(2,1)S(1)}, u32[]{:S(2)}, u32[]{:S(2)}) %collective-permute-start.17) | collective-permute-done | bytes 131104 | tf_op jit(solution)/shard_map/ppermute | solution.py:29
  133.1 13.5 %collective-permute-done.15.refs_1_ = bf16[1,256,256]{2,1,0:T(8,128)(2,1)S(1)} collective-permute-done((bf16[1,256,256]{2,1,0:T(8,128)(2,1)S(1)}, bf16[1,256,256]{2,1,0:T(8,128)(2,1)S(1)}, u32[]{:S(2)}, u32[]{:S(2)}) %collective-permute-start.15) | collective-permute-done | bytes 131104 | tf_op jit(solution)/shard_map/ppermute | solution.py:29
  146.6 1.9 right_multiply.3
  148.5 10.8 %all-to-all-start.2 = ((bf16[64,1,16,256]{3,2,1,0:T(8,128)(2,1)}), bf16[64,1,16,256]{3,2,1,0:T(8,128)(2,1)S(1)}, u32[]{:S(2)}, u32[]{:S(2)}) async-start(bf16[64,1,16,256]{3,2,1,0:T(8,128)(2,1)} %get-tuple-element.27), calls=%async_computation.2 | async-start | bytes 1048576 | tf_op jit(solution)/shard_map/all_to_all | solution.py:266
  159.4 2.3 %fusion.4 = f32[80]{0:T(128)S(1)} fusion(f32[80,16,256]{2,1,0:T(8,128)} %param.6, bf16[80,16,256]{2,1,0:T(8,128)(2,1)S(1)} %get-tuple-element.17), kind=kLoop, calls=%fused_computation.6 | loop fusion | flops 2949040 | bytes 1966400 | tf_op jit(solution)/shard_map/reduce_sum | solution.py:262
  161.8 7.2 %all-reduce = (f32[3]{0:T(128)S(1)}, f32[80]{0:T(128)S(1)}) all-reduce(f32[3]{0:T(128)S(1)} %maximum_reduce_fusion, f32[80]{0:T(128)S(1)} %fusion.4), channel_id=1, replica_groups=mesh['fsdp'=64,'rep'=4] {'rep'}, use_global_device_ids=true, to_apply=%region_5.6 | all-reduce | flops 83 | bytes 664 | tf_op jit(solution)/shard_map/psum | solution.py:308
  169.0 7.6 %all-to-all-done.2.back2 = bf16[64,1,16,256]{3,2,1,0:T(8,128)(2,1)S(1)} async-done(((bf16[64,1,16,256]{3,2,1,0:T(8,128)(2,1)}), bf16[64,1,16,256]{3,2,1,0:T(8,128)(2,1)S(1)}, u32[]{:S(2)}, u32[]{:S(2)}) %all-to-all-start.2) | async-done | bytes 524320 | tf_op jit(solution)/shard_map/all_to_all | solution.py:266
  178.3 6.3 %all-to-all-start.3 = ((f32[64,1,128]{2,1,0:T(1,128)}), f32[64,1,128]{2,1,0:T(1,128)S(1)}, u32[]{:S(2)}, u32[]{:S(2)}) async-start(f32[64,1,128]{2,1,0:T(1,128)} %broadcast_in_dim.55), calls=%async_computation.3 | async-start | bytes 65536 | tf_op jit(solution)/shard_map/all_to_all | solution.py:266
  186.5 7.3 %all-to-all-done.3 = f32[64,1,128]{2,1,0:T(1,128)S(1)} async-done(((f32[64,1,128]{2,1,0:T(1,128)}), f32[64,1,128]{2,1,0:T(1,128)S(1)}, u32[]{:S(2)}, u32[]{:S(2)}) %all-to-all-start.3) | async-done | bytes 32800 | tf_op jit(solution)/shard_map/all_to_all | solution.py:266
  194.3 2.2 %collective-permute-done.24.first = bf16[20,16,256]{2,1,0:T(8,128)(2,1)S(1)} collective-permute-done((bf16[20,16,256]{2,1,0:T(8,128)(2,1)S(1)}, bf16[20,16,256]{2,1,0:T(8,128)(2,1)S(1)}, u32[]{:S(2)}, u32[]{:S(2)}) %collective-permute-start.24) | collective-permute-done | bytes 163872 | tf_op jit(solution)/shard_map/ppermute | solution.py:29
  196.5 2.0 join_blocks.1
  (84 shorter events, 29.5 us)
Async XLA Ops:
  1.4 8.5 %collective-permute-start.1 = (bf16[40,16,256]{2,1,0:T(8,128)(2,1)S(1)}, bf16[40,16,256]{2,1,0:T(8,128)(2,1)S(1)}, u32[]{:S(2)}, u32[]{:S(2)}) collective-permute-start(bf16[40,16,256]{2,1,0:T(8,128)(2,1)S(1)} %get-tuple-element.32), channel_id=1, source_target_pairs={{0,1},{1,2},{2,3},{3,0},{4,5},{5,6},{6,7},{7,4},{8,9},{9,10},{10,1... | collective-permute-start | bytes 983048 | tf_op jit(solution)/shard_map/ppermute | solution.py:29
  3.5 7.9 %collective-permute-start.4 = (bf16[40,16,256]{2,1,0:T(8,128)(2,1)S(1)}, bf16[40,16,256]{2,1,0:T(8,128)(2,1)S(1)}, u32[]{:S(2)}, u32[]{:S(2)}) collective-permute-start(bf16[40,16,256]{2,1,0:T(8,128)(2,1)S(1)} %get-tuple-element.34), channel_id=1, source_target_pairs={{0,3},{1,0},{2,1},{3,2},{4,7},{5,4},{6,5},{7,6},{8,11},{9,8},{10,9... | collective-permute-start | bytes 983048 | tf_op jit(solution)/shard_map/ppermute | solution.py:29
  4.9 12.1 %collective-permute-start.3 = (bf16[40,16,256]{2,1,0:T(8,128)(2,1)S(1)}, bf16[40,16,256]{2,1,0:T(8,128)(2,1)S(1)}, u32[]{:S(2)}, u32[]{:S(2)}) collective-permute-start(bf16[40,16,256]{2,1,0:T(8,128)(2,1)S(1)} %get-tuple-element.31), channel_id=1, source_target_pairs={{0,1},{1,2},{2,3},{3,0},{4,5},{5,6},{6,7},{7,4},{8,9},{9,10},{10,1... | collective-permute-start | bytes 983048 | tf_op jit(solution)/shard_map/ppermute | solution.py:29
  5.0 13.5 %collective-permute-start = (bf16[40,16,256]{2,1,0:T(8,128)(2,1)S(1)}, bf16[40,16,256]{2,1,0:T(8,128)(2,1)S(1)}, u32[]{:S(2)}, u32[]{:S(2)}) collective-permute-start(bf16[40,16,256]{2,1,0:T(8,128)(2,1)S(1)} %get-tuple-element.33), channel_id=1, source_target_pairs={{0,3},{1,0},{2,1},{3,2},{4,7},{5,4},{6,5},{7,6},{8,11},{9,8},{10,9... | collective-permute-start | bytes 983048 | tf_op jit(solution)/shard_map/ppermute | solution.py:29
  12.7 12.8 %collective-permute-start.5 = (bf16[40,16,256]{2,1,0:T(8,128)(2,1)S(1)}, bf16[40,16,256]{2,1,0:T(8,128)(2,1)S(1)}, u32[]{:S(2)}, u32[]{:S(2)}) collective-permute-start(bf16[40,16,256]{2,1,0:T(8,128)(2,1)S(1)} %get-tuple-element.35), channel_id=1, source_target_pairs={{0,3},{1,0},{2,1},{3,2},{4,7},{5,4},{6,5},{7,6},{8,11},{9,8},{10,9... | collective-permute-start | bytes 983048 | tf_op jit(solution)/shard_map/ppermute | solution.py:29
  14.7 10.8 %collective-permute-start.2 = (bf16[40,16,256]{2,1,0:T(8,128)(2,1)S(1)}, bf16[40,16,256]{2,1,0:T(8,128)(2,1)S(1)}, u32[]{:S(2)}, u32[]{:S(2)}) collective-permute-start(bf16[40,16,256]{2,1,0:T(8,128)(2,1)S(1)} %get-tuple-element.36), channel_id=1, source_target_pairs={{0,1},{1,2},{2,3},{3,0},{4,5},{5,6},{6,7},{7,4},{8,9},{9,10},{10,1... | collective-permute-start | bytes 983048 | tf_op jit(solution)/shard_map/ppermute | solution.py:29
  28.1 55.2 %all-to-all-start = ((bf16[64,3,16,256]{3,2,1,0:T(8,128)(2,1)}), bf16[64,3,16,256]{3,2,1,0:T(8,128)(2,1)S(1)}, u32[]{:S(2)}, u32[]{:S(2)}) async-start(bf16[64,3,16,256]{3,2,1,0:T(8,128)(2,1)} %get-tuple-element.20), calls=%async_computation | async-start | bytes 3145728 | tf_op jit(solution)/shard_map/all_to_all | solution.py:266
  43.3 39.2 %copy-start.10 = (bf16[2,1024,256]{2,1,0:T(8,128)(2,1)}, bf16[2,1024,256]{2,1,0:T(8,128)(2,1)S(1)}, u32[]{:S(2)}) copy-start(bf16[2,1024,256]{2,1,0:T(8,128)(2,1)S(1)} %slice_bitcast_fusion.refs_4_) | copy-start | bytes 3145732
  43.4 13.6 %collective-permute-start.9 = (bf16[2,512,256]{2,1,0:T(8,128)(2,1)S(1)}, bf16[2,512,256]{2,1,0:T(8,128)(2,1)S(1)}, u32[]{:S(2)}, u32[]{:S(2)}) collective-permute-start(bf16[2,512,256]{2,1,0:T(8,128)(2,1)S(1)} %get-tuple-element.41), channel_id=1, source_target_pairs={{0,3},{1,0},{2,1},{3,2},{4,7},{5,4},{6,5},{7,6},{8,11},{9,8},{10,9... | collective-permute-start | bytes 1572872 | tf_op jit(solution)/shard_map/ppermute | solution.py:29
  46.1 14.3 %collective-permute-start.6 = (bf16[2,512,256]{2,1,0:T(8,128)(2,1)S(1)}, bf16[2,512,256]{2,1,0:T(8,128)(2,1)S(1)}, u32[]{:S(2)}, u32[]{:S(2)}) collective-permute-start(bf16[2,512,256]{2,1,0:T(8,128)(2,1)S(1)} %get-tuple-element.42), channel_id=1, source_target_pairs={{0,1},{1,2},{2,3},{3,0},{4,5},{5,6},{6,7},{7,4},{8,9},{9,10},{10,1... | collective-permute-start | bytes 1572872 | tf_op jit(solution)/shard_map/ppermute | solution.py:29
  46.1 25.2 %collective-permute-start.7 = (bf16[2,512,256]{2,1,0:T(8,128)(2,1)S(1)}, bf16[2,512,256]{2,1,0:T(8,128)(2,1)S(1)}, u32[]{:S(2)}, u32[]{:S(2)}) collective-permute-start(bf16[2,512,256]{2,1,0:T(8,128)(2,1)S(1)} %get-tuple-element.41), channel_id=1, source_target_pairs={{0,1},{1,2},{2,3},{3,0},{4,5},{5,6},{6,7},{7,4},{8,9},{9,10},{10,1... | collective-permute-start | bytes 1572872 | tf_op jit(solution)/shard_map/ppermute | solution.py:29
  46.1 26.0 %collective-permute-start.11 = (bf16[2,512,256]{2,1,0:T(8,128)(2,1)S(1)}, bf16[2,512,256]{2,1,0:T(8,128)(2,1)S(1)}, u32[]{:S(2)}, u32[]{:S(2)}) collective-permute-start(bf16[2,512,256]{2,1,0:T(8,128)(2,1)S(1)} %get-tuple-element.42), channel_id=1, source_target_pairs={{0,3},{1,0},{2,1},{3,2},{4,7},{5,4},{6,5},{7,6},{8,11},{9,8},{10,9... | collective-permute-start | bytes 1572872 | tf_op jit(solution)/shard_map/ppermute | solution.py:29
  57.0 22.5 %collective-permute-start.10 = (bf16[2,512,256]{2,1,0:T(8,128)(2,1)S(1)}, bf16[2,512,256]{2,1,0:T(8,128)(2,1)S(1)}, u32[]{:S(2)}, u32[]{:S(2)}) collective-permute-start(bf16[2,512,256]{2,1,0:T(8,128)(2,1)S(1)} %collective-permute-done.9.refs_10_), channel_id=1, source_target_pairs={{0,3},{1,0},{2,1},{3,2},{4,7},{5,4},{6,5},{7,6},{8,11},{9,8},{10,9... | collective-permute-start | bytes 1572872 | tf_op jit(solution)/shard_map/ppermute | solution.py:29
  60.4 22.1 %collective-permute-start.8 = (bf16[2,512,256]{2,1,0:T(8,128)(2,1)S(1)}, bf16[2,512,256]{2,1,0:T(8,128)(2,1)S(1)}, u32[]{:S(2)}, u32[]{:S(2)}) collective-permute-start(bf16[2,512,256]{2,1,0:T(8,128)(2,1)S(1)} %collective-permute-done.6.refs_5_), channel_id=1, source_target_pairs={{0,1},{1,2},{2,3},{3,0},{4,5},{5,6},{6,7},{7,4},{8,9},{9,10},{10,1... | collective-permute-start | bytes 1572872 | tf_op jit(solution)/shard_map/ppermute | solution.py:29
  87.2 6.4 %collective-permute-start.14 = (bf16[2,256,256]{2,1,0:T(8,128)(2,1)S(1)}, bf16[2,256,256]{2,1,0:T(8,128)(2,1)S(1)}, u32[]{:S(2)}, u32[]{:S(2)}) collective-permute-start(bf16[2,256,256]{2,1,0:T(8,128)(2,1)S(1)} %get-tuple-element.37), channel_id=1, source_target_pairs={{0,3},{1,0},{2,1},{3,2},{4,7},{5,4},{6,5},{7,6},{8,11},{9,8},{10,9... | collective-permute-start | bytes 786440 | tf_op jit(solution)/shard_map/ppermute | solution.py:29
  88.6 7.8 %collective-permute-start.13 = (bf16[2,256,256]{2,1,0:T(8,128)(2,1)S(1)}, bf16[2,256,256]{2,1,0:T(8,128)(2,1)S(1)}, u32[]{:S(2)}, u32[]{:S(2)}) collective-permute-start(bf16[2,256,256]{2,1,0:T(8,128)(2,1)S(1)} %get-tuple-element.38), channel_id=1, source_target_pairs={{0,2},{1,3},{2,0},{3,1},{4,6},{5,7},{6,4},{7,5},{8,10},{9,11},{10,... | collective-permute-start | bytes 786440 | tf_op jit(solution)/shard_map/ppermute | solution.py:29
  88.9 15.0 %collective-permute-start.12 = (bf16[2,256,256]{2,1,0:T(8,128)(2,1)S(1)}, bf16[2,256,256]{2,1,0:T(8,128)(2,1)S(1)}, u32[]{:S(2)}, u32[]{:S(2)}) collective-permute-start(bf16[2,256,256]{2,1,0:T(8,128)(2,1)S(1)} %get-tuple-element.39), channel_id=1, source_target_pairs={{0,1},{1,2},{2,3},{3,0},{4,5},{5,6},{6,7},{7,4},{8,9},{9,10},{10,1... | collective-permute-start | bytes 786440 | tf_op jit(solution)/shard_map/ppermute | solution.py:29
  108.4 40.2 %all-to-all-start.1 = ((bf16[64,2,16,256]{3,2,1,0:T(8,128)(2,1)}), bf16[64,2,16,256]{3,2,1,0:T(8,128)(2,1)S(1)}, u32[]{:S(2)}, u32[]{:S(2)}) async-start(bf16[64,2,16,256]{3,2,1,0:T(8,128)(2,1)} %copy-done), calls=%async_computation.1 | async-start | bytes 2097152 | tf_op jit(solution)/shard_map/all_to_all | solution.py:266
  119.8 11.6 %collective-permute-start.21 = (bf16[1,512,256]{2,1,0:T(8,128)(2,1)S(1)}, bf16[1,512,256]{2,1,0:T(8,128)(2,1)S(1)}, u32[]{:S(2)}, u32[]{:S(2)}) collective-permute-start(bf16[1,512,256]{2,1,0:T(8,128)(2,1)S(1)} %get-tuple-element.47), channel_id=1, source_target_pairs={{0,3},{1,0},{2,1},{3,2},{4,7},{5,4},{6,5},{7,6},{8,11},{9,8},{10,9... | collective-permute-start | bytes 786440 | tf_op jit(solution)/shard_map/ppermute | solution.py:29
  120.5 11.0 %collective-permute-start.18 = (bf16[1,512,256]{2,1,0:T(8,128)(2,1)S(1)}, bf16[1,512,256]{2,1,0:T(8,128)(2,1)S(1)}, u32[]{:S(2)}, u32[]{:S(2)}) collective-permute-start(bf16[1,512,256]{2,1,0:T(8,128)(2,1)S(1)} %get-tuple-element.48), channel_id=1, source_target_pairs={{0,1},{1,2},{2,3},{3,0},{4,5},{5,6},{6,7},{7,4},{8,9},{9,10},{10,1... | collective-permute-start | bytes 786440 | tf_op jit(solution)/shard_map/ppermute | solution.py:29
  124.1 6.1 %collective-permute-start.17 = (bf16[1,256,256]{2,1,0:T(8,128)(2,1)S(1)}, bf16[1,256,256]{2,1,0:T(8,128)(2,1)S(1)}, u32[]{:S(2)}, u32[]{:S(2)}) collective-permute-start(bf16[1,256,256]{2,1,0:T(8,128)(2,1)S(1)} %get-tuple-element.49), channel_id=1, source_target_pairs={{0,3},{1,0},{2,1},{3,2},{4,7},{5,4},{6,5},{7,6},{8,11},{9,8},{10,9... | collective-permute-start | bytes 393224 | tf_op jit(solution)/shard_map/ppermute | solution.py:29
  125.9 7.0 %collective-permute-start.16 = (bf16[1,256,256]{2,1,0:T(8,128)(2,1)S(1)}, bf16[1,256,256]{2,1,0:T(8,128)(2,1)S(1)}, u32[]{:S(2)}, u32[]{:S(2)}) collective-permute-start(bf16[1,256,256]{2,1,0:T(8,128)(2,1)S(1)} %get-tuple-element.50), channel_id=1, source_target_pairs={{0,2},{1,3},{2,0},{3,1},{4,6},{5,7},{6,4},{7,5},{8,10},{9,11},{10,... | collective-permute-start | bytes 393224 | tf_op jit(solution)/shard_map/ppermute | solution.py:29
  126.0 20.6 %collective-permute-start.19 = (bf16[1,512,256]{2,1,0:T(8,128)(2,1)S(1)}, bf16[1,512,256]{2,1,0:T(8,128)(2,1)S(1)}, u32[]{:S(2)}, u32[]{:S(2)}) collective-permute-start(bf16[1,512,256]{2,1,0:T(8,128)(2,1)S(1)} %get-tuple-element.47), channel_id=1, source_target_pairs={{0,1},{1,2},{2,3},{3,0},{4,5},{5,6},{6,7},{7,4},{8,9},{9,10},{10,1... | collective-permute-start | bytes 786440 | tf_op jit(solution)/shard_map/ppermute | solution.py:29
  130.2 16.5 %collective-permute-start.23 = (bf16[1,512,256]{2,1,0:T(8,128)(2,1)S(1)}, bf16[1,512,256]{2,1,0:T(8,128)(2,1)S(1)}, u32[]{:S(2)}, u32[]{:S(2)}) collective-permute-start(bf16[1,512,256]{2,1,0:T(8,128)(2,1)S(1)} %get-tuple-element.48), channel_id=1, source_target_pairs={{0,3},{1,0},{2,1},{3,2},{4,7},{5,4},{6,5},{7,6},{8,11},{9,8},{10,9... | collective-permute-start | bytes 786440 | tf_op jit(solution)/shard_map/ppermute | solution.py:29
  131.4 15.2 %collective-permute-start.22 = (bf16[1,512,256]{2,1,0:T(8,128)(2,1)S(1)}, bf16[1,512,256]{2,1,0:T(8,128)(2,1)S(1)}, u32[]{:S(2)}, u32[]{:S(2)}) collective-permute-start(bf16[1,512,256]{2,1,0:T(8,128)(2,1)S(1)} %collective-permute-done.21.refs_10_), channel_id=1, source_target_pairs={{0,3},{1,0},{2,1},{3,2},{4,7},{5,4},{6,5},{7,6},{8,11},{9,8},{10,9... | collective-permute-start | bytes 786440 | tf_op jit(solution)/shard_map/ppermute | solution.py:29
  131.4 15.2 %collective-permute-start.20 = (bf16[1,512,256]{2,1,0:T(8,128)(2,1)S(1)}, bf16[1,512,256]{2,1,0:T(8,128)(2,1)S(1)}, u32[]{:S(2)}, u32[]{:S(2)}) collective-permute-start(bf16[1,512,256]{2,1,0:T(8,128)(2,1)S(1)} %collective-permute-done.18.refs_5_), channel_id=1, source_target_pairs={{0,1},{1,2},{2,3},{3,0},{4,5},{5,6},{6,7},{7,4},{8,9},{9,10},{10,1... | collective-permute-start | bytes 786440 | tf_op jit(solution)/shard_map/ppermute | solution.py:29
  132.9 13.7 %collective-permute-start.15 = (bf16[1,256,256]{2,1,0:T(8,128)(2,1)S(1)}, bf16[1,256,256]{2,1,0:T(8,128)(2,1)S(1)}, u32[]{:S(2)}, u32[]{:S(2)}) collective-permute-start(bf16[1,256,256]{2,1,0:T(8,128)(2,1)S(1)} %get-tuple-element.51), channel_id=1, source_target_pairs={{0,1},{1,2},{2,3},{3,0},{4,5},{5,6},{6,7},{7,4},{8,9},{9,10},{10,1... | collective-permute-start | bytes 393224 | tf_op jit(solution)/shard_map/ppermute | solution.py:29
  148.5 28.2 %all-to-all-start.2 = ((bf16[64,1,16,256]{3,2,1,0:T(8,128)(2,1)}), bf16[64,1,16,256]{3,2,1,0:T(8,128)(2,1)S(1)}, u32[]{:S(2)}, u32[]{:S(2)}) async-start(bf16[64,1,16,256]{3,2,1,0:T(8,128)(2,1)} %get-tuple-element.27), calls=%async_computation.2 | async-start | bytes 1048576 | tf_op jit(solution)/shard_map/all_to_all | solution.py:266
  178.3 15.5 %all-to-all-start.3 = ((f32[64,1,128]{2,1,0:T(1,128)}), f32[64,1,128]{2,1,0:T(1,128)S(1)}, u32[]{:S(2)}, u32[]{:S(2)}) async-start(f32[64,1,128]{2,1,0:T(1,128)} %broadcast_in_dim.55), calls=%async_computation.3 | async-start | bytes 65536 | tf_op jit(solution)/shard_map/all_to_all | solution.py:266
  184.7 9.6 %collective-permute-start.26 = (bf16[20,16,256]{2,1,0:T(8,128)(2,1)S(1)}, bf16[20,16,256]{2,1,0:T(8,128)(2,1)S(1)}, u32[]{:S(2)}, u32[]{:S(2)}) collective-permute-start(bf16[20,16,256]{2,1,0:T(8,128)(2,1)S(1)} %get-tuple-element.43), channel_id=1, source_target_pairs={{0,3},{1,0},{2,1},{3,2},{4,7},{5,4},{6,5},{7,6},{8,11},{9,8},{10,9... | collective-permute-start | bytes 491528 | tf_op jit(solution)/shard_map/ppermute | solution.py:29
  185.4 8.9 %collective-permute-start.25 = (bf16[20,16,256]{2,1,0:T(8,128)(2,1)S(1)}, bf16[20,16,256]{2,1,0:T(8,128)(2,1)S(1)}, u32[]{:S(2)}, u32[]{:S(2)}) collective-permute-start(bf16[20,16,256]{2,1,0:T(8,128)(2,1)S(1)} %get-tuple-element.44), channel_id=1, source_target_pairs={{0,2},{1,3},{2,0},{3,1},{4,6},{5,7},{6,4},{7,5},{8,10},{9,11},{10,... | collective-permute-start | bytes 491528 | tf_op jit(solution)/shard_map/ppermute | solution.py:29
  186.2 10.3 %collective-permute-start.24 = (bf16[20,16,256]{2,1,0:T(8,128)(2,1)S(1)}, bf16[20,16,256]{2,1,0:T(8,128)(2,1)S(1)}, u32[]{:S(2)}, u32[]{:S(2)}) collective-permute-start(bf16[20,16,256]{2,1,0:T(8,128)(2,1)S(1)} %get-tuple-element.45), channel_id=1, source_target_pairs={{0,1},{1,2},{2,3},{3,0},{4,5},{5,6},{6,7},{7,4},{8,9},{9,10},{10,1... | collective-permute-start | bytes 491528 | tf_op jit(solution)/shard_map/ppermute | solution.py:29
  (10 other events, 79.0 us)

commit v2 on v1

--- a/solution.py
+++ b/solution.py
@@ -47,9 +47,9 @@
     return (pieces[0], near_left, last_right, near_right, last_left), (on_right, on_left)
 
 
-def gather_over_rep(value):
+def gather_over_rep(value, *others):
     middle = value.shape[1] // 2
-    top, bottom = value[:, :middle], value[:, middle:]
+    top, bottom = after((value[:, :middle], value[:, middle:]), *others)
     left_top = shift(top, 1)
     right_bottom = shift(bottom, 3)
     left_bottom = shift(bottom, 1)
@@ -59,7 +59,13 @@
     return value, left_top, left_bottom, far_top, far_bottom, right_top, right_bottom
 
 
-def sum_pack_kernel(source, own, near_left, last_right, near_right, last_left, low, out):
+def near(gathered):
+    return gathered[1], gathered[2], gathered[5], gathered[6]
+
+
+def sum_pack_kernel(
+    source, own, near_left, last_right, near_right, last_left, low, out01, out2
+):
     middle = near_left.shape[0]
 
     @pl.loop(0, middle)
@@ -70,8 +76,9 @@
 
     @pl.loop(0, OWNERS)
     def _(o):
-        for s in range(CAP):
-            out[o, s] = low[source[s * OWNERS + o]]
+        out01[o, 0] = low[source[o]]
+        out01[o, 1] = low[source[OWNERS + o]]
+        out2[o, 0] = low[source[2 * OWNERS + o]]
 
 
 def sum_pack(source, terms):
@@ -80,22 +87,23 @@
         sum_pack_kernel,
         out_shape=[
             jax.ShapeDtypeStruct((blocks, rows, columns), jnp.bfloat16),
-            jax.ShapeDtypeStruct((OWNERS, CAP, rows, columns), jnp.bfloat16),
+            jax.ShapeDtypeStruct((OWNERS, 2, rows, columns), jnp.bfloat16),
+            jax.ShapeDtypeStruct((OWNERS, 1, rows, columns), jnp.bfloat16),
         ],
         in_specs=[SMEM] + [VMEM] * 5,
-        out_specs=[VMEM, VMEM],
+        out_specs=[VMEM] * 3,
         compiler_params=pltpu.CompilerParams(vmem_limit_bytes=ROOM),
         name="sum_pack",
     )(source, *terms)
 
 
-def left_kernel(first, place, gradient, left, out, wide_rows):
+def left_kernel(place, gradient, left, out, wide_rows):
     halves, size, half = wide_rows.shape
     width = halves * half
     rows = gradient.shape[2]
     part = rows // REP
     s = pl.program_id(0)
-    low = gradient[:, first + s].reshape(size, width)
+    low = gradient[:, s].reshape(size, width)
     tile = size // 4
     for i in range(4):
         at = slice(i * tile, (i + 1) * tile)
@@ -111,10 +119,11 @@
                 out[(k, 0) + at] = strided.astype(jnp.bfloat16)
 
 
-def left_multiply(place, gradient, left, first, count):
+def left_multiply(place, gradient, left, first):
     size, width = left.shape[1], gradient.shape[3]
-    return pl.pallas_call(
-        lambda *refs: left_kernel(first, *refs),
+    count = gradient.shape[1]
+    return pl.pallas_call(
+        left_kernel,
         grid=(count,),
         out_shape=jax.ShapeDtypeStruct((REP, count, size // REP, width), jnp.bfloat16),
         in_specs=[SMEM, VMEM, pl.BlockSpec((1, size, size), lambda i: (first + i, 0, 0))],
@@ -288,28 +297,29 @@
         for k in range(REP)
     ]
     terms, passing = sum_over_rep(pieces)
-    rights01 = gather_over_rep(after(right_root[0, :2], *passing))
-    low, packed = sum_pack(source, terms)
-    owned = exchange(packed)
+    rights01 = gather_over_rep(right_root[0, :2], *passing)
+    low, packed01, packed2 = sum_pack(source, terms)
+    owned01 = exchange(packed01)
+    owned2 = exchange(after(packed2, owned01))
     adam = lax.psum(adam_squares(low, moment), "rep")
 
     def spread(sent):
         return [sent[0]] + [shift(sent[k], k) for k in (1, 2, 3)]
 
-    sent01 = left_multiply(after(place_ref, *rights01), owned, left_root[0], 0, 2)
+    sent01 = left_multiply(after(place_ref, *near(rights01)), owned01, left_root[0], 0)
     held01 = spread(sent01)
-    result01, square01 = right_multiply(place_ref, held01, rights01)
+    rights2 = gather_over_rep(right_root[0, 2:], *held01)
+    sent2 = left_multiply(after(place_ref, sent01), owned2, left_root[0], 2)
+    result01, square01 = right_multiply(after(place_ref, sent2), held01, rights01)
     back01 = exchange(result01)
-    rights2 = gather_over_rep(after(right_root[0, 2:], *held01))
-    sent2 = left_multiply(after(place_ref, *held01), owned, left_root[0], 2, 1)
     held2 = spread(sent2)
-    result2, square2 = right_multiply(place_ref, held2, rights2)
+    result2, square2 = right_multiply(after(place_ref, result01), held2, rights2)
     back2 = exchange(after(result2, back01))
     squares = lax.psum(jnp.sum(jnp.concatenate([square01, square2]), axis=(1, 2)), "rep")
     known = jnp.concatenate([adam, squares, jnp.zeros((128 - blocks - CAP,), jnp.float32)])
     known = jnp.broadcast_to(known[None, None, :], (OWNERS, 1, 128))
     sent = split_blocks(owner, slot, back01, back2)
-    known = exchange(after(known, sent))[:, 0]
+    known = exchange(after(known, back2))[:, 0]
     adam_norm = jnp.sqrt(jnp.sum(known[:, :blocks], axis=0))
     by_place = jnp.transpose(known[:, blocks : blocks + CAP]).reshape(OWNERS * CAP, 1)
     shampoo_norm = jnp.sqrt(jnp.sum(jnp.where(matched, by_place, 0.0), axis=0))

time: 199 us -> 201 us (1.010)
  starting transfers between devices: 69.3 us -> 81.5 us
  waiting for transfers between devices: 90 us -> 79.6 us
  local copies, waits for them, and re-layouts: 10.2 us -> 8.14 us
    ppermute x27, waiting for transfers between devices: 75.1 us -> 38.9 us  [shift(): lax.ppermute(value, 'rep', [(i, (i + step) % REP) for i in range(REP)])]
    all_to_all x4 -> x5, waiting for transfers between devices: 14.9 us -> 40.8 us  [exchange(): return lax.all_to_all(value, 'fsdp', split_axis=0, concat_axis=0)]
    all_to_all x4 -> x5, starting transfers between devices: 41.3 us -> 48.5 us  [exchange(): return lax.all_to_all(value, 'fsdp', split_axis=0, concat_axis=0)]
    ppermute x27, starting transfers between devices: 27.9 us -> 33 us  [shift(): lax.ppermute(value, 'rep', [(i, (i + step) % REP) for i in range(REP)])]
    unnamed x22 -> x14, local copies, waits for them, and re-layouts: 4.16 us -> 0.26 us
  transfers between devices with their start and end apart: 31 -> 32, of which waited for: 17 -> 17; matrix products, arithmetic and copies ran while one was open for 4% -> 5% of each run, Pallas kernels for 2% -> 5%
where the time goes in v2:
time: 201 us; the launch traced here: 200 us
  starting transfers between devices  81.5 us (41%)
  waiting for transfers between devices  79.6 us (40%)
  Pallas kernels  18.4 us (9%)
  blocking collectives  8.27 us (4%)
  local copies, waits for them, and re-layouts  8.14 us (4%)
  other arithmetic  3.45 us (2%)
    all_to_all x5, starting transfers between devices, exchange(): return lax.all_to_all(value, 'fsdp', split_axis=0, concat_axis=0)  48.5 us
    all_to_all x5, waiting for transfers between devices, exchange(): return lax.all_to_all(value, 'fsdp', split_axis=0, concat_axis=0)  40.8 us
    ppermute x27, waiting for transfers between devices, shift(): lax.ppermute(value, 'rep', [(i, (i + step) % REP) for i in range(REP)])  38.9 us
    ppermute x27, starting transfers between devices, shift(): lax.ppermute(value, 'rep', [(i, (i + step) % REP) for i in range(REP)])  33 us
    psum x1, blocking collectives, shards(): lax.psum(jnp.sum(jnp.concatenate([square01, square2]), axis=(1, 2)), 'rep')  8.27 us
    pallas_call x2, Pallas kernels, left_multiply(): pl.pallas_call(left_kernel, grid=(count,), out_shape=jax.ShapeDtypeStruct...  6.43 us
    pallas_call x2, Pallas kernels, right_multiply(): pl.pallas_call(right_kernel, grid=(count,), out_shape=[jax.ShapeDtypeStru...  6.35 us
  transfers between devices with their start and end apart: 32, of which 17 were waited for; matrix products, arithmetic and copies ran while one was open for 5% of the time, Pallas kernels for 5%

profile of v2, /device:TPU:1, one launch (start us, length us, event | category | flops | bytes accessed | tf_op | source)
XLA Modules:
  0.0 199.7 jit_solution(8487007064777550400)
XLA Ops:
  1.4 3.4 %collective-permute-start.4 = (bf16[40,16,256]{2,1,0:T(8,128)(2,1)S(1)}, bf16[40,16,256]{2,1,0:T(8,128)(2,1)S(1)}, u32[]{:S(2)}, u32[]{:S(2)}) collective-permute-start(bf16[40,16,256]{2,1,0:T(8,128)(2,1)S(1)} %get-tuple-element.46), channel_id=1, source_target_pairs={{0,3},{1,0},{2,1},{3,2},{4,7},{5,4},{6,5},{7,6},{8,11},{9,8},{10,9... | collective-permute-start | bytes 983048 | tf_op jit(solution)/shard_map/ppermute | solution.py:29
  4.8 2.7 %collective-permute-start = (bf16[40,16,256]{2,1,0:T(8,128)(2,1)S(1)}, bf16[40,16,256]{2,1,0:T(8,128)(2,1)S(1)}, u32[]{:S(2)}, u32[]{:S(2)}) collective-permute-start(bf16[40,16,256]{2,1,0:T(8,128)(2,1)S(1)} %get-tuple-element.45), channel_id=1, source_target_pairs={{0,3},{1,0},{2,1},{3,2},{4,7},{5,4},{6,5},{7,6},{8,11},{9,8},{10,9... | collective-permute-start | bytes 983048 | tf_op jit(solution)/shard_map/ppermute | solution.py:29
  7.6 3.5 %collective-permute-done.4 = bf16[40,16,256]{2,1,0:T(8,128)(2,1)S(1)} collective-permute-done((bf16[40,16,256]{2,1,0:T(8,128)(2,1)S(1)}, bf16[40,16,256]{2,1,0:T(8,128)(2,1)S(1)}, u32[]{:S(2)}, u32[]{:S(2)}) %collective-permute-start.4) | collective-permute-done | bytes 327712 | tf_op jit(solution)/shard_map/ppermute | solution.py:29
  11.2 3.1 %collective-permute-done.1 = bf16[40,16,256]{2,1,0:T(8,128)(2,1)S(1)} collective-permute-done((bf16[40,16,256]{2,1,0:T(8,128)(2,1)S(1)}, bf16[40,16,256]{2,1,0:T(8,128)(2,1)S(1)}, u32[]{:S(2)}, u32[]{:S(2)}) %collective-permute-start.1) | collective-permute-done | bytes 327712 | tf_op jit(solution)/shard_map/ppermute | solution.py:29
  15.6 2.7 %collective-permute-start.5 = (bf16[40,16,256]{2,1,0:T(8,128)(2,1)S(1)}, bf16[40,16,256]{2,1,0:T(8,128)(2,1)S(1)}, u32[]{:S(2)}, u32[]{:S(2)}) collective-permute-start(bf16[40,16,256]{2,1,0:T(8,128)(2,1)S(1)} %get-tuple-element.47), channel_id=1, source_target_pairs={{0,3},{1,0},{2,1},{3,2},{4,7},{5,4},{6,5},{7,6},{8,11},{9,8},{10,9... | collective-permute-start | bytes 983048 | tf_op jit(solution)/shard_map/ppermute | solution.py:29
  21.3 7.0 %collective-permute-done.2.last_right = bf16[40,16,256]{2,1,0:T(8,128)(2,1)S(1)} collective-permute-done((bf16[40,16,256]{2,1,0:T(8,128)(2,1)S(1)}, bf16[40,16,256]{2,1,0:T(8,128)(2,1)S(1)}, u32[]{:S(2)}, u32[]{:S(2)}) %collective-permute-start.2) | collective-permute-done | bytes 327712 | tf_op jit(solution)/shard_map/ppermute | solution.py:29
  28.3 2.7 %sum_pack.1 = (bf16[80,16,256]{2,1,0:T(8,128)(2,1)S(1)}, bf16[64,2,16,256]{3,2,1,0:T(8,128)(2,1)}, bf16[64,1,16,256]{3,2,1,0:T(8,128)(2,1)}) custom-call(s32[192]{0:T(256)S(1)} %select_reduce_fusion.1.source, bf16[80,16,256]{2,1,0:T(8,128)(2,1)S(1)} %dynamic-slice_bitcast_fusion.own, bf16[40,16,256]{2,1,0:T(8,128)(2,1)S(1)} %collective-permute-done.near_left, ...), custom_call_target="tpu_custom_call" | custom-call | tf_op jit(solution)/shard_map/sum_pack/pallas_call | solution.py:86
  31.0 13.5 %all-to-all-start = ((bf16[64,2,16,256]{3,2,1,0:T(8,128)(2,1)}), bf16[64,2,16,256]{3,2,1,0:T(8,128)(2,1)S(1)}, u32[]{:S(2)}, u32[]{:S(2)}) async-start(bf16[64,2,16,256]{3,2,1,0:T(8,128)(2,1)} %get-tuple-element.27), calls=%async_computation | async-start | bytes 2097152 | tf_op jit(solution)/shard_map/all_to_all | solution.py:275
  47.2 2.7 %collective-permute-start.8 = (bf16[2,512,256]{2,1,0:T(8,128)(2,1)}, bf16[2,512,256]{2,1,0:T(8,128)(2,1)}, u32[]{:S(2)}, u32[]{:S(2)}) collective-permute-start(bf16[2,512,256]{2,1,0:T(8,128)(2,1)} %get-tuple-element.24), channel_id=1, source_target_pairs={{0,3},{1,0},{2,1},{3,2},{4,7},{5,4},{6,5},{7,6},{8,11},{9,8},{10,9... | collective-permute-start | bytes 1572872 | tf_op jit(solution)/shard_map/ppermute | solution.py:29
  51.3 21.8 %all-to-all-done.gradient = bf16[64,2,16,256]{3,2,1,0:T(8,128)(2,1)S(1)} async-done(((bf16[64,2,16,256]{3,2,1,0:T(8,128)(2,1)}), bf16[64,2,16,256]{3,2,1,0:T(8,128)(2,1)S(1)}, u32[]{:S(2)}, u32[]{:S(2)}) %all-to-all-start) | async-done | bytes 1048608 | tf_op jit(solution)/shard_map/all_to_all | solution.py:275
  73.1 6.2 %all-to-all-start.1 = ((bf16[64,1,16,256]{3,2,1,0:T(8,128)(2,1)}), bf16[64,1,16,256]{3,2,1,0:T(8,128)(2,1)S(1)}, u32[]{:S(2)}, u32[]{:S(2)}) async-start(bf16[64,1,16,256]{3,2,1,0:T(8,128)(2,1)} %get-tuple-element.30), calls=%async_computation.1 | async-start | bytes 1048576 | tf_op jit(solution)/shard_map/all_to_all | solution.py:275
  79.4 2.7 %collective-permute-start.14 = (bf16[2,512,256]{2,1,0:T(8,128)(2,1)}, bf16[2,512,256]{2,1,0:T(8,128)(2,1)}, u32[]{:S(2)}, u32[]{:S(2)}) collective-permute-start(bf16[2,512,256]{2,1,0:T(8,128)(2,1)} %collective-permute-done.9.refs_10_), channel_id=1, source_target_pairs={{0,3},{1,0},{2,1},{3,2},{4,7},{5,4},{6,5},{7,6},{8,11},{9,8},{10,9... | collective-permute-start | bytes 1572872 | tf_op jit(solution)/shard_map/ppermute | solution.py:29
  82.1 3.8 %left_multiply.2 = bf16[4,2,256,256]{3,2,1,0:T(8,128)(2,1)S(1)} custom-call(s32[1]{0:T(128)} %bitcast.place, bf16[64,2,16,256]{3,2,1,0:T(8,128)(2,1)S(1)} %all-to-all-done.gradient, bf16[3,1024,1024]{2,1,0:T(8,128)(2,1)} %bitcast.53), custom_call_target="tpu_custom_call" | custom-call | flops 1073741824 | bytes 8388608 | tf_op jit(solution)/shard_map/left_multiply/pallas_call | solution.py:125
  89.5 7.1 %all-to-all-done.1.gradient = bf16[64,1,16,256]{3,2,1,0:T(8,128)(2,1)S(1)} async-done(((bf16[64,1,16,256]{3,2,1,0:T(8,128)(2,1)}), bf16[64,1,16,256]{3,2,1,0:T(8,128)(2,1)S(1)}, u32[]{:S(2)}, u32[]{:S(2)}) %all-to-all-start.1) | async-done | bytes 524320 | tf_op jit(solution)/shard_map/all_to_all | solution.py:275
  96.6 2.6 %left_multiply.3 = bf16[4,1,256,256]{3,2,1,0:T(8,128)(2,1)S(1)} custom-call(s32[1]{0:T(128)} %bitcast.place, bf16[64,1,16,256]{3,2,1,0:T(8,128)(2,1)S(1)} %all-to-all-done.1.gradient, bf16[3,1024,1024]{2,1,0:T(8,128)(2,1)} %bitcast.54), custom_call_target="tpu_custom_call" | custom-call | flops 536870912 | bytes 4194304 | tf_op jit(solution)/shard_map/left_multiply/pallas_call | solution.py:125
  99.3 5.6 %collective-permute-done.10.refs_1_ = bf16[2,256,256]{2,1,0:T(8,128)(2,1)S(1)} collective-permute-done((bf16[2,256,256]{2,1,0:T(8,128)(2,1)}, bf16[2,256,256]{2,1,0:T(8,128)(2,1)S(1)}, u32[]{:S(2)}, u32[]{:S(2)}) %collective-permute-start.10) | collective-permute-done | bytes 262176 | tf_op jit(solution)/shard_map/ppermute | solution.py:29
  104.9 4.5 %right_multiply.2 = (bf16[64,2,16,256]{3,2,1,0:T(8,128)(2,1)}, f32[2,1,256]{2,1,0:T(1,128)S(1)}) custom-call(s32[1]{0:T(128)} %bitcast.place, bf16[2,256,256]{2,1,0:T(8,128)(2,1)S(1)} %get-tuple-element.52.refs_0_, bf16[2,256,256]{2,1,0:T(8,128)(2,1)S(1)} %collective-permute-done.10.refs_1_, bf16[2,256,256]{2,1,0:T(8,128)(2,1)S(1)} %collective-permute-done.11.refs_2_, ...), custom_call_target="tpu_custom_call" | custom-call | flops 1073741824 | bytes 8388608 | tf_op jit(solution)/shard_map/right_multiply/pallas_call | solution.py:180
  109.4 11.2 %all-to-all-start.2 = ((bf16[64,2,16,256]{3,2,1,0:T(8,128)(2,1)}), bf16[64,2,16,256]{3,2,1,0:T(8,128)(2,1)S(1)}, u32[]{:S(2)}, u32[]{:S(2)}) async-start(bf16[64,2,16,256]{3,2,1,0:T(8,128)(2,1)} %get-tuple-element.33), calls=%async_computation.2 | async-start | bytes 2097152 | tf_op jit(solution)/shard_map/all_to_all | solution.py:275
  121.8 3.0 %collective-permute-start.21 = (bf16[1,512,256]{2,1,0:T(8,128)(2,1)S(1)}, bf16[1,512,256]{2,1,0:T(8,128)(2,1)S(1)}, u32[]{:S(2)}, u32[]{:S(2)}) collective-permute-start(bf16[1,512,256]{2,1,0:T(8,128)(2,1)S(1)} %get-tuple-element.36), channel_id=1, source_target_pairs={{0,3},{1,0},{2,1},{3,2},{4,7},{5,4},{6,5},{7,6},{8,11},{9,8},{10,9... | collective-permute-start | bytes 786440 | tf_op jit(solution)/shard_map/ppermute | solution.py:29
  124.9 2.7 %collective-permute-start.23 = (bf16[1,512,256]{2,1,0:T(8,128)(2,1)S(1)}, bf16[1,512,256]{2,1,0:T(8,128)(2,1)S(1)}, u32[]{:S(2)}, u32[]{:S(2)}) collective-permute-start(bf16[1,512,256]{2,1,0:T(8,128)(2,1)S(1)} %get-tuple-element.35), channel_id=1, source_target_pairs={{0,3},{1,0},{2,1},{3,2},{4,7},{5,4},{6,5},{7,6},{8,11},{9,8},{10,9... | collective-permute-start | bytes 786440 | tf_op jit(solution)/shard_map/ppermute | solution.py:29
  127.6 3.5 %collective-permute-done.18.refs_5_ = bf16[1,512,256]{2,1,0:T(8,128)(2,1)S(1)} collective-permute-done((bf16[1,512,256]{2,1,0:T(8,128)(2,1)S(1)}, bf16[1,512,256]{2,1,0:T(8,128)(2,1)S(1)}, u32[]{:S(2)}, u32[]{:S(2)}) %collective-permute-start.18) | collective-permute-done | bytes 262176 | tf_op jit(solution)/shard_map/ppermute | solution.py:29
  131.1 2.7 %collective-permute-start.22 = (bf16[1,512,256]{2,1,0:T(8,128)(2,1)S(1)}, bf16[1,512,256]{2,1,0:T(8,128)(2,1)S(1)}, u32[]{:S(2)}, u32[]{:S(2)}) collective-permute-start(bf16[1,512,256]{2,1,0:T(8,128)(2,1)S(1)} %collective-permute-done.21.refs_10_), channel_id=1, source_target_pairs={{0,3},{1,0},{2,1},{3,2},{4,7},{5,4},{6,5},{7,6},{8,11},{9,8},{10,9... | collective-permute-start | bytes 786440 | tf_op jit(solution)/shard_map/ppermute | solution.py:29
  133.9 2.8 %collective-permute-done.19.refs_6_ = bf16[1,512,256]{2,1,0:T(8,128)(2,1)S(1)} collective-permute-done((bf16[1,512,256]{2,1,0:T(8,128)(2,1)S(1)}, bf16[1,512,256]{2,1,0:T(8,128)(2,1)S(1)}, u32[]{:S(2)}, u32[]{:S(2)}) %collective-permute-start.19) | collective-permute-done | bytes 262176 | tf_op jit(solution)/shard_map/ppermute | solution.py:29
  136.8 2.3 %collective-permute-start.17 = (bf16[1,256,256]{2,1,0:T(8,128)(2,1)S(1)}, bf16[1,256,256]{2,1,0:T(8,128)(2,1)S(1)}, u32[]{:S(2)}, u32[]{:S(2)}) collective-permute-start(bf16[1,256,256]{2,1,0:T(8,128)(2,1)S(1)} %get-tuple-element.61), channel_id=1, source_target_pairs={{0,3},{1,0},{2,1},{3,2},{4,7},{5,4},{6,5},{7,6},{8,11},{9,8},{10,9... | collective-permute-start | bytes 393224 | tf_op jit(solution)/shard_map/ppermute | solution.py:29
  139.2 3.2 %collective-permute-done.20.refs_7_ = bf16[1,512,256]{2,1,0:T(8,128)(2,1)S(1)} collective-permute-done((bf16[1,512,256]{2,1,0:T(8,128)(2,1)S(1)}, bf16[1,512,256]{2,1,0:T(8,128)(2,1)S(1)}, u32[]{:S(2)}, u32[]{:S(2)}) %collective-permute-start.20) | collective-permute-done | bytes 262176 | tf_op jit(solution)/shard_map/ppermute | solution.py:29
  145.1 3.7 %collective-permute-done.16.refs_2_ = bf16[1,256,256]{2,1,0:T(8,128)(2,1)S(1)} collective-permute-done((bf16[1,256,256]{2,1,0:T(8,128)(2,1)S(1)}, bf16[1,256,256]{2,1,0:T(8,128)(2,1)S(1)}, u32[]{:S(2)}, u32[]{:S(2)}) %collective-permute-start.16) | collective-permute-done | bytes 131104 | tf_op jit(solution)/shard_map/ppermute | solution.py:29
  150.7 11.3 %all-to-all-start.3 = ((bf16[64,1,16,256]{3,2,1,0:T(8,128)(2,1)}), bf16[64,1,16,256]{3,2,1,0:T(8,128)(2,1)S(1)}, u32[]{:S(2)}, u32[]{:S(2)}) async-start(bf16[64,1,16,256]{3,2,1,0:T(8,128)(2,1)} %get-tuple-element.39), calls=%async_computation.3 | async-start | bytes 1048576 | tf_op jit(solution)/shard_map/all_to_all | solution.py:275
  163.6 8.3 %all-reduce = (f32[3]{0:T(128)S(1)}, f32[80]{0:T(128)S(1)}) all-reduce(f32[3]{0:T(128)S(1)} %maximum_reduce_fusion, f32[80]{0:T(128)} %fusion.4), channel_id=1, replica_groups=mesh['fsdp'=64,'rep'=4] {'rep'}, use_global_device_ids=true, to_apply=%region_5.6 | all-reduce | flops 83 | bytes 664 | tf_op jit(solution)/shard_map/psum | solution.py:318
  172.0 7.3 %all-to-all-done.3.back2 = bf16[64,1,16,256]{3,2,1,0:T(8,128)(2,1)S(1)} async-done(((bf16[64,1,16,256]{3,2,1,0:T(8,128)(2,1)}), bf16[64,1,16,256]{3,2,1,0:T(8,128)(2,1)S(1)}, u32[]{:S(2)}, u32[]{:S(2)}) %all-to-all-start.3) | async-done | bytes 524320 | tf_op jit(solution)/shard_map/all_to_all | solution.py:275
  179.9 6.3 %all-to-all-start.4 = ((f32[64,1,128]{2,1,0:T(1,128)}), f32[64,1,128]{2,1,0:T(1,128)S(1)}, u32[]{:S(2)}, u32[]{:S(2)}) async-start(f32[64,1,128]{2,1,0:T(1,128)} %broadcast_in_dim.55), calls=%async_computation.4 | async-start | bytes 65536 | tf_op jit(solution)/shard_map/all_to_all | solution.py:275
  187.4 2.8 %collective-permute-start.25 = (bf16[20,16,256]{2,1,0:T(8,128)(2,1)S(1)}, bf16[20,16,256]{2,1,0:T(8,128)(2,1)S(1)}, u32[]{:S(2)}, u32[]{:S(2)}) collective-permute-start(bf16[20,16,256]{2,1,0:T(8,128)(2,1)S(1)} %get-tuple-element.56), channel_id=1, source_target_pairs={{0,2},{1,3},{2,0},{3,1},{4,6},{5,7},{6,4},{7,5},{8,10},{9,11},{10,... | collective-permute-start | bytes 491528 | tf_op jit(solution)/shard_map/ppermute | solution.py:29
  190.9 4.5 %all-to-all-done.4 = f32[64,1,128]{2,1,0:T(1,128)S(1)} async-done(((f32[64,1,128]{2,1,0:T(1,128)}), f32[64,1,128]{2,1,0:T(1,128)S(1)}, u32[]{:S(2)}, u32[]{:S(2)}) %all-to-all-start.4) | async-done | bytes 32800 | tf_op jit(solution)/shard_map/all_to_all | solution.py:275
  (78 shorter events, 28.3 us)
Async XLA Ops:
  1.4 9.8 %collective-permute-start.4 = (bf16[40,16,256]{2,1,0:T(8,128)(2,1)S(1)}, bf16[40,16,256]{2,1,0:T(8,128)(2,1)S(1)}, u32[]{:S(2)}, u32[]{:S(2)}) collective-permute-start(bf16[40,16,256]{2,1,0:T(8,128)(2,1)S(1)} %get-tuple-element.46), channel_id=1, source_target_pairs={{0,3},{1,0},{2,1},{3,2},{4,7},{5,4},{6,5},{7,6},{8,11},{9,8},{10,9... | collective-permute-start | bytes 983048 | tf_op jit(solution)/shard_map/ppermute | solution.py:29
  4.8 9.5 %collective-permute-start.1 = (bf16[40,16,256]{2,1,0:T(8,128)(2,1)S(1)}, bf16[40,16,256]{2,1,0:T(8,128)(2,1)S(1)}, u32[]{:S(2)}, u32[]{:S(2)}) collective-permute-start(bf16[40,16,256]{2,1,0:T(8,128)(2,1)S(1)} %get-tuple-element.44), channel_id=1, source_target_pairs={{0,1},{1,2},{2,3},{3,0},{4,5},{5,6},{6,7},{7,4},{8,9},{9,10},{10,1... | collective-permute-start | bytes 983048 | tf_op jit(solution)/shard_map/ppermute | solution.py:29
  4.8 14.7 %collective-permute-start = (bf16[40,16,256]{2,1,0:T(8,128)(2,1)S(1)}, bf16[40,16,256]{2,1,0:T(8,128)(2,1)S(1)}, u32[]{:S(2)}, u32[]{:S(2)}) collective-permute-start(bf16[40,16,256]{2,1,0:T(8,128)(2,1)S(1)} %get-tuple-element.45), channel_id=1, source_target_pairs={{0,3},{1,0},{2,1},{3,2},{4,7},{5,4},{6,5},{7,6},{8,11},{9,8},{10,9... | collective-permute-start | bytes 983048 | tf_op jit(solution)/shard_map/ppermute | solution.py:29
  7.5 13.8 %collective-permute-start.3 = (bf16[40,16,256]{2,1,0:T(8,128)(2,1)S(1)}, bf16[40,16,256]{2,1,0:T(8,128)(2,1)S(1)}, u32[]{:S(2)}, u32[]{:S(2)}) collective-permute-start(bf16[40,16,256]{2,1,0:T(8,128)(2,1)S(1)} %get-tuple-element.43), channel_id=1, source_target_pairs={{0,1},{1,2},{2,3},{3,0},{4,5},{5,6},{6,7},{7,4},{8,9},{9,10},{10,1... | collective-permute-start | bytes 983048 | tf_op jit(solution)/shard_map/ppermute | solution.py:29
  15.5 12.8 %collective-permute-start.2 = (bf16[40,16,256]{2,1,0:T(8,128)(2,1)S(1)}, bf16[40,16,256]{2,1,0:T(8,128)(2,1)S(1)}, u32[]{:S(2)}, u32[]{:S(2)}) collective-permute-start(bf16[40,16,256]{2,1,0:T(8,128)(2,1)S(1)} %get-tuple-element.48), channel_id=1, source_target_pairs={{0,1},{1,2},{2,3},{3,0},{4,5},{5,6},{6,7},{7,4},{8,9},{9,10},{10,1... | collective-permute-start | bytes 983048 | tf_op jit(solution)/shard_map/ppermute | solution.py:29
  15.6 12.7 %collective-permute-start.5 = (bf16[40,16,256]{2,1,0:T(8,128)(2,1)S(1)}, bf16[40,16,256]{2,1,0:T(8,128)(2,1)S(1)}, u32[]{:S(2)}, u32[]{:S(2)}) collective-permute-start(bf16[40,16,256]{2,1,0:T(8,128)(2,1)S(1)} %get-tuple-element.47), channel_id=1, source_target_pairs={{0,3},{1,0},{2,1},{3,2},{4,7},{5,4},{6,5},{7,6},{8,11},{9,8},{10,9... | collective-permute-start | bytes 983048 | tf_op jit(solution)/shard_map/ppermute | solution.py:29
  31.0 42.1 %all-to-all-start = ((bf16[64,2,16,256]{3,2,1,0:T(8,128)(2,1)}), bf16[64,2,16,256]{3,2,1,0:T(8,128)(2,1)S(1)}, u32[]{:S(2)}, u32[]{:S(2)}) async-start(bf16[64,2,16,256]{3,2,1,0:T(8,128)(2,1)} %get-tuple-element.27), calls=%async_computation | async-start | bytes 2097152 | tf_op jit(solution)/shard_map/all_to_all | solution.py:275
  47.2 32.1 %collective-permute-start.6 = (bf16[2,512,256]{2,1,0:T(8,128)(2,1)}, bf16[2,512,256]{2,1,0:T(8,128)(2,1)S(1)}, u32[]{:S(2)}, u32[]{:S(2)}) collective-permute-start(bf16[2,512,256]{2,1,0:T(8,128)(2,1)} %get-tuple-element.24), channel_id=1, source_target_pairs={{0,1},{1,2},{2,3},{3,0},{4,5},{5,6},{6,7},{7,4},{8,9},{9,10},{10,1... | collective-permute-start | bytes 1572872 | tf_op jit(solution)/shard_map/ppermute | solution.py:29
  47.2 32.1 %collective-permute-start.7 = (bf16[2,512,256]{2,1,0:T(8,128)(2,1)}, bf16[2,512,256]{2,1,0:T(8,128)(2,1)S(1)}, u32[]{:S(2)}, u32[]{:S(2)}) collective-permute-start(bf16[2,512,256]{2,1,0:T(8,128)(2,1)} %get-tuple-element.25), channel_id=1, source_target_pairs={{0,1},{1,2},{2,3},{3,0},{4,5},{5,6},{6,7},{7,4},{8,9},{9,10},{10,1... | collective-permute-start | bytes 1572872 | tf_op jit(solution)/shard_map/ppermute | solution.py:29
  47.2 32.1 %collective-permute-start.8 = (bf16[2,512,256]{2,1,0:T(8,128)(2,1)}, bf16[2,512,256]{2,1,0:T(8,128)(2,1)}, u32[]{:S(2)}, u32[]{:S(2)}) collective-permute-start(bf16[2,512,256]{2,1,0:T(8,128)(2,1)} %get-tuple-element.24), channel_id=1, source_target_pairs={{0,3},{1,0},{2,1},{3,2},{4,7},{5,4},{6,5},{7,6},{8,11},{9,8},{10,9... | collective-permute-start | bytes 1572872 | tf_op jit(solution)/shard_map/ppermute | solution.py:29
  49.9 29.4 %collective-permute-start.9 = (bf16[2,512,256]{2,1,0:T(8,128)(2,1)}, bf16[2,512,256]{2,1,0:T(8,128)(2,1)}, u32[]{:S(2)}, u32[]{:S(2)}) collective-permute-start(bf16[2,512,256]{2,1,0:T(8,128)(2,1)} %get-tuple-element.25), channel_id=1, source_target_pairs={{0,3},{1,0},{2,1},{3,2},{4,7},{5,4},{6,5},{7,6},{8,11},{9,8},{10,9... | collective-permute-start | bytes 1572872 | tf_op jit(solution)/shard_map/ppermute | solution.py:29
  73.1 23.5 %all-to-all-start.1 = ((bf16[64,1,16,256]{3,2,1,0:T(8,128)(2,1)}), bf16[64,1,16,256]{3,2,1,0:T(8,128)(2,1)S(1)}, u32[]{:S(2)}, u32[]{:S(2)}) async-start(bf16[64,1,16,256]{3,2,1,0:T(8,128)(2,1)} %get-tuple-element.30), calls=%async_computation.1 | async-start | bytes 1048576 | tf_op jit(solution)/shard_map/all_to_all | solution.py:275
  79.3 19.9 %collective-permute-start.13 = (bf16[2,512,256]{2,1,0:T(8,128)(2,1)S(1)}, bf16[2,512,256]{2,1,0:T(8,128)(2,1)}, u32[]{:S(2)}, u32[]{:S(2)}) collective-permute-start(bf16[2,512,256]{2,1,0:T(8,128)(2,1)S(1)} %collective-permute-done.6.refs_5_), channel_id=1, source_target_pairs={{0,1},{1,2},{2,3},{3,0},{4,5},{5,6},{6,7},{7,4},{8,9},{9,10},{10,1... | collective-permute-start | bytes 1572872 | tf_op jit(solution)/shard_map/ppermute | solution.py:29
  79.4 19.8 %collective-permute-start.14 = (bf16[2,512,256]{2,1,0:T(8,128)(2,1)}, bf16[2,512,256]{2,1,0:T(8,128)(2,1)}, u32[]{:S(2)}, u32[]{:S(2)}) collective-permute-start(bf16[2,512,256]{2,1,0:T(8,128)(2,1)} %collective-permute-done.9.refs_10_), channel_id=1, source_target_pairs={{0,3},{1,0},{2,1},{3,2},{4,7},{5,4},{6,5},{7,6},{8,11},{9,8},{10,9... | collective-permute-start | bytes 1572872 | tf_op jit(solution)/shard_map/ppermute | solution.py:29
  86.8 18.1 %collective-permute-start.10 = (bf16[2,256,256]{2,1,0:T(8,128)(2,1)}, bf16[2,256,256]{2,1,0:T(8,128)(2,1)S(1)}, u32[]{:S(2)}, u32[]{:S(2)}) collective-permute-start(bf16[2,256,256]{2,1,0:T(8,128)(2,1)} %get-tuple-element.51), channel_id=1, source_target_pairs={{0,1},{1,2},{2,3},{3,0},{4,5},{5,6},{6,7},{7,4},{8,9},{9,10},{10,1... | collective-permute-start | bytes 786440 | tf_op jit(solution)/shard_map/ppermute | solution.py:29
  86.8 18.1 %collective-permute-start.11 = (bf16[2,256,256]{2,1,0:T(8,128)(2,1)}, bf16[2,256,256]{2,1,0:T(8,128)(2,1)S(1)}, u32[]{:S(2)}, u32[]{:S(2)}) collective-permute-start(bf16[2,256,256]{2,1,0:T(8,128)(2,1)} %get-tuple-element.50), channel_id=1, source_target_pairs={{0,2},{1,3},{2,0},{3,1},{4,6},{5,7},{6,4},{7,5},{8,10},{9,11},{10,... | collective-permute-start | bytes 786440 | tf_op jit(solution)/shard_map/ppermute | solution.py:29
  88.0 16.9 %collective-permute-start.12 = (bf16[2,256,256]{2,1,0:T(8,128)(2,1)}, bf16[2,256,256]{2,1,0:T(8,128)(2,1)}, u32[]{:S(2)}, u32[]{:S(2)}) collective-permute-start(bf16[2,256,256]{2,1,0:T(8,128)(2,1)} %get-tuple-element.49), channel_id=1, source_target_pairs={{0,3},{1,0},{2,1},{3,2},{4,7},{5,4},{6,5},{7,6},{8,11},{9,8},{10,9... | collective-permute-start | bytes 786440 | tf_op jit(solution)/shard_map/ppermute | solution.py:29
  109.4 41.3 %all-to-all-start.2 = ((bf16[64,2,16,256]{3,2,1,0:T(8,128)(2,1)}), bf16[64,2,16,256]{3,2,1,0:T(8,128)(2,1)S(1)}, u32[]{:S(2)}, u32[]{:S(2)}) async-start(bf16[64,2,16,256]{3,2,1,0:T(8,128)(2,1)} %get-tuple-element.33), calls=%async_computation.2 | async-start | bytes 2097152 | tf_op jit(solution)/shard_map/all_to_all | solution.py:275
  121.8 9.3 %collective-permute-start.18 = (bf16[1,512,256]{2,1,0:T(8,128)(2,1)S(1)}, bf16[1,512,256]{2,1,0:T(8,128)(2,1)S(1)}, u32[]{:S(2)}, u32[]{:S(2)}) collective-permute-start(bf16[1,512,256]{2,1,0:T(8,128)(2,1)S(1)} %get-tuple-element.35), channel_id=1, source_target_pairs={{0,1},{1,2},{2,3},{3,0},{4,5},{5,6},{6,7},{7,4},{8,9},{9,10},{10,1... | collective-permute-start | bytes 786440 | tf_op jit(solution)/shard_map/ppermute | solution.py:29
  121.8 9.2 %collective-permute-start.21 = (bf16[1,512,256]{2,1,0:T(8,128)(2,1)S(1)}, bf16[1,512,256]{2,1,0:T(8,128)(2,1)S(1)}, u32[]{:S(2)}, u32[]{:S(2)}) collective-permute-start(bf16[1,512,256]{2,1,0:T(8,128)(2,1)S(1)} %get-tuple-element.36), channel_id=1, source_target_pairs={{0,3},{1,0},{2,1},{3,2},{4,7},{5,4},{6,5},{7,6},{8,11},{9,8},{10,9... | collective-permute-start | bytes 786440 | tf_op jit(solution)/shard_map/ppermute | solution.py:29
  124.9 11.8 %collective-permute-start.19 = (bf16[1,512,256]{2,1,0:T(8,128)(2,1)S(1)}, bf16[1,512,256]{2,1,0:T(8,128)(2,1)S(1)}, u32[]{:S(2)}, u32[]{:S(2)}) collective-permute-start(bf16[1,512,256]{2,1,0:T(8,128)(2,1)S(1)} %get-tuple-element.36), channel_id=1, source_target_pairs={{0,1},{1,2},{2,3},{3,0},{4,5},{5,6},{6,7},{7,4},{8,9},{9,10},{10,1... | collective-permute-start | bytes 786440 | tf_op jit(solution)/shard_map/ppermute | solution.py:29
  124.9 11.9 %collective-permute-start.23 = (bf16[1,512,256]{2,1,0:T(8,128)(2,1)S(1)}, bf16[1,512,256]{2,1,0:T(8,128)(2,1)S(1)}, u32[]{:S(2)}, u32[]{:S(2)}) collective-permute-start(bf16[1,512,256]{2,1,0:T(8,128)(2,1)S(1)} %get-tuple-element.35), channel_id=1, source_target_pairs={{0,3},{1,0},{2,1},{3,2},{4,7},{5,4},{6,5},{7,6},{8,11},{9,8},{10,9... | collective-permute-start | bytes 786440 | tf_op jit(solution)/shard_map/ppermute | solution.py:29
  131.1 11.2 %collective-permute-start.20 = (bf16[1,512,256]{2,1,0:T(8,128)(2,1)S(1)}, bf16[1,512,256]{2,1,0:T(8,128)(2,1)S(1)}, u32[]{:S(2)}, u32[]{:S(2)}) collective-permute-start(bf16[1,512,256]{2,1,0:T(8,128)(2,1)S(1)} %collective-permute-done.18.refs_5_), channel_id=1, source_target_pairs={{0,1},{1,2},{2,3},{3,0},{4,5},{5,6},{6,7},{7,4},{8,9},{9,10},{10,1... | collective-permute-start | bytes 786440 | tf_op jit(solution)/shard_map/ppermute | solution.py:29
  131.1 12.5 %collective-permute-start.22 = (bf16[1,512,256]{2,1,0:T(8,128)(2,1)S(1)}, bf16[1,512,256]{2,1,0:T(8,128)(2,1)S(1)}, u32[]{:S(2)}, u32[]{:S(2)}) collective-permute-start(bf16[1,512,256]{2,1,0:T(8,128)(2,1)S(1)} %collective-permute-done.21.refs_10_), channel_id=1, source_target_pairs={{0,3},{1,0},{2,1},{3,2},{4,7},{5,4},{6,5},{7,6},{8,11},{9,8},{10,9... | collective-permute-start | bytes 786440 | tf_op jit(solution)/shard_map/ppermute | solution.py:29
  133.8 11.3 %collective-permute-start.15 = (bf16[1,256,256]{2,1,0:T(8,128)(2,1)S(1)}, bf16[1,256,256]{2,1,0:T(8,128)(2,1)S(1)}, u32[]{:S(2)}, u32[]{:S(2)}) collective-permute-start(bf16[1,256,256]{2,1,0:T(8,128)(2,1)S(1)} %get-tuple-element.63), channel_id=1, source_target_pairs={{0,1},{1,2},{2,3},{3,0},{4,5},{5,6},{6,7},{7,4},{8,9},{9,10},{10,1... | collective-permute-start | bytes 393224 | tf_op jit(solution)/shard_map/ppermute | solution.py:29
  136.7 12.1 %collective-permute-start.16 = (bf16[1,256,256]{2,1,0:T(8,128)(2,1)S(1)}, bf16[1,256,256]{2,1,0:T(8,128)(2,1)S(1)}, u32[]{:S(2)}, u32[]{:S(2)}) collective-permute-start(bf16[1,256,256]{2,1,0:T(8,128)(2,1)S(1)} %get-tuple-element.62), channel_id=1, source_target_pairs={{0,2},{1,3},{2,0},{3,1},{4,6},{5,7},{6,4},{7,5},{8,10},{9,11},{10,... | collective-permute-start | bytes 393224 | tf_op jit(solution)/shard_map/ppermute | solution.py:29
  136.8 12.0 %collective-permute-start.17 = (bf16[1,256,256]{2,1,0:T(8,128)(2,1)S(1)}, bf16[1,256,256]{2,1,0:T(8,128)(2,1)S(1)}, u32[]{:S(2)}, u32[]{:S(2)}) collective-permute-start(bf16[1,256,256]{2,1,0:T(8,128)(2,1)S(1)} %get-tuple-element.61), channel_id=1, source_target_pairs={{0,3},{1,0},{2,1},{3,2},{4,7},{5,4},{6,5},{7,6},{8,11},{9,8},{10,9... | collective-permute-start | bytes 393224 | tf_op jit(solution)/shard_map/ppermute | solution.py:29
  150.7 28.6 %all-to-all-start.3 = ((bf16[64,1,16,256]{3,2,1,0:T(8,128)(2,1)}), bf16[64,1,16,256]{3,2,1,0:T(8,128)(2,1)S(1)}, u32[]{:S(2)}, u32[]{:S(2)}) async-start(bf16[64,1,16,256]{3,2,1,0:T(8,128)(2,1)} %get-tuple-element.39), calls=%async_computation.3 | async-start | bytes 1048576 | tf_op jit(solution)/shard_map/all_to_all | solution.py:275
  179.9 15.5 %all-to-all-start.4 = ((f32[64,1,128]{2,1,0:T(1,128)}), f32[64,1,128]{2,1,0:T(1,128)S(1)}, u32[]{:S(2)}, u32[]{:S(2)}) async-start(f32[64,1,128]{2,1,0:T(1,128)} %broadcast_in_dim.55), calls=%async_computation.4 | async-start | bytes 65536 | tf_op jit(solution)/shard_map/all_to_all | solution.py:275
  187.3 8.6 %collective-permute-start.24 = (bf16[20,16,256]{2,1,0:T(8,128)(2,1)S(1)}, bf16[20,16,256]{2,1,0:T(8,128)(2,1)S(1)}, u32[]{:S(2)}, u32[]{:S(2)}) collective-permute-start(bf16[20,16,256]{2,1,0:T(8,128)(2,1)S(1)} %get-tuple-element.57), channel_id=1, source_target_pairs={{0,1},{1,2},{2,3},{3,0},{4,5},{5,6},{6,7},{7,4},{8,9},{9,10},{10,1... | collective-permute-start | bytes 491528 | tf_op jit(solution)/shard_map/ppermute | solution.py:29
  187.4 10.1 %collective-permute-start.25 = (bf16[20,16,256]{2,1,0:T(8,128)(2,1)S(1)}, bf16[20,16,256]{2,1,0:T(8,128)(2,1)S(1)}, u32[]{:S(2)}, u32[]{:S(2)}) collective-permute-start(bf16[20,16,256]{2,1,0:T(8,128)(2,1)S(1)} %get-tuple-element.56), channel_id=1, source_target_pairs={{0,2},{1,3},{2,0},{3,1},{4,6},{5,7},{6,4},{7,5},{8,10},{9,11},{10,... | collective-permute-start | bytes 491528 | tf_op jit(solution)/shard_map/ppermute | solution.py:29
  190.1 7.6 %collective-permute-start.26 = (bf16[20,16,256]{2,1,0:T(8,128)(2,1)S(1)}, bf16[20,16,256]{2,1,0:T(8,128)(2,1)S(1)}, u32[]{:S(2)}, u32[]{:S(2)}) collective-permute-start(bf16[20,16,256]{2,1,0:T(8,128)(2,1)S(1)} %get-tuple-element.55), channel_id=1, source_target_pairs={{0,3},{1,0},{2,1},{3,2},{4,7},{5,4},{6,5},{7,6},{8,11},{9,8},{10,9... | collective-permute-start | bytes 491528 | tf_op jit(solution)/shard_map/ppermute | solution.py:29
  (7 other events, 67.7 us)

commit v3 on v1

--- a/solution.py
+++ b/solution.py
@@ -47,9 +47,9 @@
     return (pieces[0], near_left, last_right, near_right, last_left), (on_right, on_left)
 
 
-def gather_over_rep(value):
+def gather_over_rep(value, *others):
     middle = value.shape[1] // 2
-    top, bottom = value[:, :middle], value[:, middle:]
+    top, bottom = after((value[:, :middle], value[:, middle:]), *others)
     left_top = shift(top, 1)
     right_bottom = shift(bottom, 3)
     left_bottom = shift(bottom, 1)
@@ -132,7 +132,7 @@
 
 def right_kernel(place, *refs):
     pieces, rights = refs[:REP], refs[REP : REP + 7]
-    out, total, full, wide_rows = refs[REP + 7 :]
+    out, total, full, wide_rows = refs[-4:]
     height, size = full.shape
     width = size // REP
     halves, _, half = wide_rows.shape
@@ -164,28 +164,31 @@
     total[0] = jnp.sum(squares, axis=0, keepdims=True)
 
 
-def right_multiply(place, pieces, rights):
-    count, height, width = pieces[0].shape
-    size = rights[0].shape[1]
+def right_multiply(place, pieces, rights, first, before):
+    slots, height, width = pieces[0].shape
+    count, size = rights[0].shape[:2]
     rows = size // OWNERS
+    kept = [] if before is None else [before]
     return pl.pallas_call(
         right_kernel,
         grid=(count,),
         out_shape=[
-            jax.ShapeDtypeStruct((OWNERS, count, rows, width), jnp.bfloat16),
+            jax.ShapeDtypeStruct((OWNERS, slots, rows, width), jnp.bfloat16),
             jax.ShapeDtypeStruct((count, 1, width), jnp.float32),
         ],
         in_specs=[SMEM]
-        + [pl.BlockSpec((1, height, width), lambda i: (i, 0, 0))] * 4
-        + [pl.BlockSpec((1,) + r.shape[1:], lambda i: (i, 0, 0)) for r in rights],
+        + [pl.BlockSpec((1, height, width), lambda i: (first + i, 0, 0))] * 4
+        + [pl.BlockSpec((1,) + r.shape[1:], lambda i: (i, 0, 0)) for r in rights]
+        + [pl.BlockSpec(memory_space=pl.ANY) for _ in kept],
         out_specs=[
-            pl.BlockSpec((OWNERS, 1, rows, width), lambda i: (0, i, 0, 0)),
+            pl.BlockSpec((OWNERS, 1, rows, width), lambda i: (0, first + i, 0, 0)),
             pl.BlockSpec((1, 1, width), lambda i: (i, 0, 0)),
         ],
         scratch_shapes=[
             pltpu.VMEM((height, size), jnp.bfloat16),
             pltpu.VMEM((width // 128, size, 128), jnp.float32),
         ],
+        input_output_aliases={1 + len(pieces) + len(rights): 0} if kept else {},
         compiler_params=pltpu.CompilerParams(vmem_limit_bytes=ROOM),
         cost_estimate=pl.CostEstimate(
             flops=count * 2 * size * size * width,
@@ -193,39 +196,35 @@
             transcendentals=0,
         ),
         name="right_multiply",
-    )(place, *pieces, *rights)
-
-
-def split_kernel(owner, slot, back01, back2, out, held):
+    )(place, *pieces, *rights, *kept)
+
+
+def split_kernel(owner, slot, back, out):
     _, groups, rows, _ = out.shape
     part = rows // REP
-
-    held[:, :2] = back01[...]
-    held[:, 2] = back2[:, 0]
 
     @pl.loop(0, groups)
     def _(g):
         parts = []
         for i in range(REP):
             b = g * REP + i
-            parts.append(wide(held[owner[b], slot[b]]))
+            parts.append(wide(back[owner[b], slot[b]]))
         for k in range(REP):
             joined = [p[k * part : (k + 1) * part] for p in parts]
             out[(REP - k) % REP, g] = jnp.concatenate(joined, axis=0).astype(jnp.bfloat16)
 
 
-def split_blocks(owner, slot, back01, back2):
+def split_blocks(owner, slot, back):
     blocks = owner.shape[0]
-    _, _, rows, width = back01.shape
+    _, _, rows, width = back.shape
     return pl.pallas_call(
         split_kernel,
         out_shape=jax.ShapeDtypeStruct((REP, blocks // REP, rows, width), jnp.bfloat16),
-        in_specs=[SMEM] * 2 + [VMEM] * 2,
+        in_specs=[SMEM] * 2 + [VMEM],
         out_specs=VMEM,
-        scratch_shapes=[pltpu.VMEM((OWNERS, CAP, rows, width), jnp.bfloat16)],
         compiler_params=pltpu.CompilerParams(vmem_limit_bytes=ROOM),
         name="split_blocks",
-    )(owner, slot, back01, back2)
+    )(owner, slot, back)
 
 
 def join_kernel(place, ratio, own, first, second, third, out, held):
@@ -288,7 +287,8 @@
         for k in range(REP)
     ]
     terms, passing = sum_over_rep(pieces)
-    rights01 = gather_over_rep(after(right_root[0, :2], *passing))
+    rights01 = gather_over_rep(right_root[0, :2], *passing)
+    rights2 = gather_over_rep(right_root[0, 2:], *rights01)
     low, packed = sum_pack(source, terms)
     owned = exchange(packed)
     adam = lax.psum(adam_squares(low, moment), "rep")
@@ -296,20 +296,16 @@
     def spread(sent):
         return [sent[0]] + [shift(sent[k], k) for k in (1, 2, 3)]
 
-    sent01 = left_multiply(after(place_ref, *rights01), owned, left_root[0], 0, 2)
-    held01 = spread(sent01)
-    result01, square01 = right_multiply(place_ref, held01, rights01)
-    back01 = exchange(result01)
-    rights2 = gather_over_rep(after(right_root[0, 2:], *held01))
-    sent2 = left_multiply(after(place_ref, *held01), owned, left_root[0], 2, 1)
-    held2 = spread(sent2)
-    result2, square2 = right_multiply(place_ref, held2, rights2)
-    back2 = exchange(after(result2, back01))
+    sent = left_multiply(after(place_ref, *rights01), owned, left_root[0], 0, CAP)
+    held = spread(sent)
+    result, square01 = right_multiply(place_ref, held, rights01, 0, None)
+    result, square2 = right_multiply(place_ref, held, rights2, 2, result)
+    back = exchange(result)
     squares = lax.psum(jnp.sum(jnp.concatenate([square01, square2]), axis=(1, 2)), "rep")
     known = jnp.concatenate([adam, squares, jnp.zeros((128 - blocks - CAP,), jnp.float32)])
     known = jnp.broadcast_to(known[None, None, :], (OWNERS, 1, 128))
-    sent = split_blocks(owner, slot, back01, back2)
-    known = exchange(after(known, sent))[:, 0]
+    sent = split_blocks(owner, slot, back)
+    known = exchange(after(known, back))[:, 0]
     adam_norm = jnp.sqrt(jnp.sum(known[:, :blocks], axis=0))
     by_place = jnp.transpose(known[:, blocks : blocks + CAP]).reshape(OWNERS * CAP, 1)
     shampoo_norm = jnp.sqrt(jnp.sum(jnp.where(matched, by_place, 0.0), axis=0))

time: 199 us -> 205 us (1.030)
  waiting for transfers between devices: 90 us -> 98.6 us
  starting transfers between devices: 69.3 us -> 65 us
  local copies, waits for them, and re-layouts: 10.2 us -> 12.9 us
  Pallas kernels: 17.3 us -> 15.1 us
  blocking collectives: 7.17 us -> 9.36 us
    all_to_all x4 -> x3, waiting for transfers between devices: 14.9 us -> 33 us  [exchange(): return lax.all_to_all(value, 'fsdp', split_axis=0, concat_axis=0)]
    ppermute x27 -> x24, waiting for transfers between devices: 75.1 us -> 65.6 us  [shift(): lax.ppermute(value, 'rep', [(i, (i + step) % REP) for i in range(REP)])]
    all_to_all x4 -> x3, starting transfers between devices: 41.3 us -> 33.8 us  [exchange(): return lax.all_to_all(value, 'fsdp', split_axis=0, concat_axis=0)]
    ppermute x27 -> x24, starting transfers between devices: 27.9 us -> 31.2 us  [shift(): lax.ppermute(value, 'rep', [(i, (i + step) % REP) for i in range(REP)])]
    unnamed x22 -> x40, local copies, waits for them, and re-layouts: 4.16 us -> 6.66 us
    psum x1, blocking collectives: 7.17 us -> 9.36 us  [shards(): lax.psum(jnp.sum(jnp.concatenate([square01, square2]), axis=(1, 2)), 'rep')]
    pallas_call x2 -> x1, Pallas kernels: 6.44 us -> 5.38 us  [left_multiply(): pl.pallas_call(lambda *refs: left_kernel(first, *refs), grid=(count,), ou...]
  transfers between devices with their start and end apart: 31 -> 27, of which waited for: 17 -> 15; matrix products, arithmetic and copies ran while one was open for 4% -> 4% of each run, Pallas kernels for 2% -> 2%
where the time goes in v3:
time: 205 us
  waiting for transfers between devices  98.6 us (48%)
  starting transfers between devices  65 us (32%)
  Pallas kernels  15.1 us (7%)
  local copies, waits for them, and re-layouts  12.9 us (6%)
  blocking collectives  9.36 us (5%)
  other arithmetic  3.45 us (2%)
    ppermute x24, waiting for transfers between devices, shift(): lax.ppermute(value, 'rep', [(i, (i + step) % REP) for i in range(REP)])  65.6 us
    all_to_all x3, starting transfers between devices, exchange(): return lax.all_to_all(value, 'fsdp', split_axis=0, concat_axis=0)  33.8 us
    all_to_all x3, waiting for transfers between devices, exchange(): return lax.all_to_all(value, 'fsdp', split_axis=0, concat_axis=0)  33 us
    ppermute x24, starting transfers between devices, shift(): lax.ppermute(value, 'rep', [(i, (i + step) % REP) for i in range(REP)])  31.2 us
    psum x1, blocking collectives, shards(): lax.psum(jnp.sum(jnp.concatenate([square01, square2]), axis=(1, 2)), 'rep')  9.36 us
    unnamed x40, local copies, waits for them, and re-layouts  6.66 us
    pallas_call x1, Pallas kernels, left_multiply(): pl.pallas_call(lambda *refs: left_kernel(first, *refs), grid=(count,), ou...  5.38 us
    pallas_call x2, Pallas kernels, right_multiply(): pl.pallas_call(right_kernel, grid=(count,), out_shape=[jax.ShapeDtypeStru...  4.23 us
  transfers between devices with their start and end apart: 27, of which 15 were waited for; matrix products, arithmetic and copies ran while one was open for 4% of the time, Pallas kernels for 2%

profile of v3, /device:TPU:1, one launch (start us, length us, event | category | flops | bytes accessed | tf_op | source)
XLA Modules:
  0.0 204.6 jit_solution(8129278822825381342)
XLA Ops:
  1.4 2.1 %collective-permute-start.1 = (bf16[40,16,256]{2,1,0:T(8,128)(2,1)S(1)}, bf16[40,16,256]{2,1,0:T(8,128)(2,1)S(1)}, u32[]{:S(2)}, u32[]{:S(2)}) collective-permute-start(bf16[40,16,256]{2,1,0:T(8,128)(2,1)S(1)} %get-tuple-element.32), channel_id=1, source_target_pairs={{0,1},{1,2},{2,3},{3,0},{4,5},{5,6},{6,7},{7,4},{8,9},{9,10},{10,1... | collective-permute-start | bytes 983048 | tf_op jit(solution)/shard_map/ppermute | solution.py:29
  6.5 3.4 %collective-permute-done.1 = bf16[40,16,256]{2,1,0:T(8,128)(2,1)S(1)} collective-permute-done((bf16[40,16,256]{2,1,0:T(8,128)(2,1)S(1)}, bf16[40,16,256]{2,1,0:T(8,128)(2,1)S(1)}, u32[]{:S(2)}, u32[]{:S(2)}) %collective-permute-start.1) | collective-permute-done | bytes 327712 | tf_op jit(solution)/shard_map/ppermute | solution.py:29
  12.7 1.6 collective-permute-start.2
  16.7 1.8 collective-permute-done.near_left
  18.4 5.8 %collective-permute-done.2.last_right = bf16[40,16,256]{2,1,0:T(8,128)(2,1)S(1)} collective-permute-done((bf16[40,16,256]{2,1,0:T(8,128)(2,1)S(1)}, bf16[40,16,256]{2,1,0:T(8,128)(2,1)S(1)}, u32[]{:S(2)}, u32[]{:S(2)}) %collective-permute-start.2) | collective-permute-done | bytes 327712 | tf_op jit(solution)/shard_map/ppermute | solution.py:29
  25.5 2.7 %sum_pack.1 = (bf16[80,16,256]{2,1,0:T(8,128)(2,1)S(1)}, bf16[64,3,16,256]{3,2,1,0:T(8,128)(2,1)}) custom-call(s32[192]{0:T(256)S(1)} %select_reduce_fusion.1.source, bf16[80,16,256]{2,1,0:T(8,128)(2,1)S(1)} %dynamic-slice_bitcast_fusion.own, bf16[40,16,256]{2,1,0:T(8,128)(2,1)S(1)} %collective-permute-done.near_left, ...), custom_call_target="tpu_custom_call" | custom-call | tf_op jit(solution)/shard_map/sum_pack/pallas_call | solution.py:79
  29.0 13.9 %all-to-all-start = ((bf16[64,3,16,256]{3,2,1,0:T(8,128)(2,1)}), bf16[64,3,16,256]{3,2,1,0:T(8,128)(2,1)S(1)}, u32[]{:S(2)}, u32[]{:S(2)}) async-start(bf16[64,3,16,256]{3,2,1,0:T(8,128)(2,1)} %get-tuple-element.21), calls=%async_computation | async-start | bytes 3145728 | tf_op jit(solution)/shard_map/all_to_all | solution.py:265
  44.2 2.8 %collective-permute-start.9 = (bf16[2,512,256]{2,1,0:T(8,128)(2,1)S(1)}, bf16[2,512,256]{2,1,0:T(8,128)(2,1)S(1)}, u32[]{:S(2)}, u32[]{:S(2)}) collective-permute-start(bf16[2,512,256]{2,1,0:T(8,128)(2,1)S(1)} %get-tuple-element.19), channel_id=1, source_target_pairs={{0,3},{1,0},{2,1},{3,2},{4,7},{5,4},{6,5},{7,6},{8,11},{9,8},{10,9... | collective-permute-start | bytes 1572872 | tf_op jit(solution)/shard_map/ppermute | solution.py:29
  47.0 2.7 %collective-permute-start.11 = (bf16[2,512,256]{2,1,0:T(8,128)(2,1)S(1)}, bf16[2,512,256]{2,1,0:T(8,128)(2,1)S(1)}, u32[]{:S(2)}, u32[]{:S(2)}) collective-permute-start(bf16[2,512,256]{2,1,0:T(8,128)(2,1)S(1)} %get-tuple-element.18), channel_id=1, source_target_pairs={{0,3},{1,0},{2,1},{3,2},{4,7},{5,4},{6,5},{7,6},{8,11},{9,8},{10,9... | collective-permute-start | bytes 1572872 | tf_op jit(solution)/shard_map/ppermute | solution.py:29
  49.6 8.2 %collective-permute-done.9.refs_10_ = bf16[2,512,256]{2,1,0:T(8,128)(2,1)S(1)} collective-permute-done((bf16[2,512,256]{2,1,0:T(8,128)(2,1)S(1)}, bf16[2,512,256]{2,1,0:T(8,128)(2,1)S(1)}, u32[]{:S(2)}, u32[]{:S(2)}) %collective-permute-start.9) | collective-permute-done | bytes 524320 | tf_op jit(solution)/shard_map/ppermute | solution.py:29
  57.8 3.4 %collective-permute-start.10 = (bf16[2,512,256]{2,1,0:T(8,128)(2,1)S(1)}, bf16[2,512,256]{2,1,0:T(8,128)(2,1)S(1)}, u32[]{:S(2)}, u32[]{:S(2)}) collective-permute-start(bf16[2,512,256]{2,1,0:T(8,128)(2,1)S(1)} %collective-permute-done.9.refs_10_), channel_id=1, source_target_pairs={{0,3},{1,0},{2,1},{3,2},{4,7},{5,4},{6,5},{7,6},{8,11},{9,8},{10,9... | collective-permute-start | bytes 1572872 | tf_op jit(solution)/shard_map/ppermute | solution.py:29
  62.5 6.5 %collective-permute-done.11.refs_9_ = bf16[2,512,256]{2,1,0:T(8,128)(2,1)S(1)} collective-permute-done((bf16[2,512,256]{2,1,0:T(8,128)(2,1)S(1)}, bf16[2,512,256]{2,1,0:T(8,128)(2,1)S(1)}, u32[]{:S(2)}, u32[]{:S(2)}) %collective-permute-start.11) | collective-permute-done | bytes 524320 | tf_op jit(solution)/shard_map/ppermute | solution.py:29
  69.8 2.3 %collective-permute-done.7.refs_6_ = bf16[2,512,256]{2,1,0:T(8,128)(2,1)S(1)} collective-permute-done((bf16[2,512,256]{2,1,0:T(8,128)(2,1)S(1)}, bf16[2,512,256]{2,1,0:T(8,128)(2,1)S(1)}, u32[]{:S(2)}, u32[]{:S(2)}) %collective-permute-start.7) | collective-permute-done | bytes 524320 | tf_op jit(solution)/shard_map/ppermute | solution.py:29
  72.9 7.3 %collective-permute-done.10.refs_8_ = bf16[2,512,256]{2,1,0:T(8,128)(2,1)S(1)} collective-permute-done((bf16[2,512,256]{2,1,0:T(8,128)(2,1)S(1)}, bf16[2,512,256]{2,1,0:T(8,128)(2,1)S(1)}, u32[]{:S(2)}, u32[]{:S(2)}) %collective-permute-start.10) | collective-permute-done | bytes 524320 | tf_op jit(solution)/shard_map/ppermute | solution.py:29
  81.1 2.3 %collective-permute-done.8.refs_7_ = bf16[2,512,256]{2,1,0:T(8,128)(2,1)S(1)} collective-permute-done((bf16[2,512,256]{2,1,0:T(8,128)(2,1)S(1)}, bf16[2,512,256]{2,1,0:T(8,128)(2,1)S(1)}, u32[]{:S(2)}, u32[]{:S(2)}) %collective-permute-start.8) | collective-permute-done | bytes 524320 | tf_op jit(solution)/shard_map/ppermute | solution.py:29
  84.2 5.4 %left_multiply.1 = bf16[4,3,256,256]{3,2,1,0:T(8,128)(2,1)S(1)} custom-call(s32[1]{0:T(128)} %bitcast.refs_0_.place, bf16[64,3,16,256]{3,2,1,0:T(8,128)(2,1)S(1)} %all-to-all-done.refs_1_, bf16[3,1024,1024]{2,1,0:T(8,128)(2,1)} %bitcast.45), custom_call_target="tpu_custom_call" | custom-call | flops 1610612736 | bytes 12582912 | tf_op jit(solution)/shard_map/left_multiply/pallas_call | solution.py:116
  90.0 2.3 %collective-permute-start.13 = (bf16[3,256,256]{2,1,0:T(8,128)(2,1)S(1)}, bf16[3,256,256]{2,1,0:T(8,128)(2,1)S(1)}, u32[]{:S(2)}, u32[]{:S(2)}) collective-permute-start(bf16[3,256,256]{2,1,0:T(8,128)(2,1)S(1)} %get-tuple-element.38), channel_id=1, source_target_pairs={{0,2},{1,3},{2,0},{3,1},{4,6},{5,7},{6,4},{7,5},{8,10},{9,11},{10,... | collective-permute-start | bytes 1179656 | tf_op jit(solution)/shard_map/ppermute | solution.py:29
  93.4 1.7 collective-permute-start.18
  95.1 19.1 %collective-permute-done.15.refs_5_ = bf16[1,512,256]{2,1,0:T(8,128)(2,1)S(1)} collective-permute-done((bf16[1,512,256]{2,1,0:T(8,128)(2,1)S(1)}, bf16[1,512,256]{2,1,0:T(8,128)(2,1)S(1)}, u32[]{:S(2)}, u32[]{:S(2)}) %collective-permute-start.15) | collective-permute-done | bytes 262176 | tf_op jit(solution)/shard_map/ppermute | solution.py:29
  114.2 2.7 %collective-permute-start.20 = (bf16[1,512,256]{2,1,0:T(8,128)(2,1)S(1)}, bf16[1,512,256]{2,1,0:T(8,128)(2,1)S(1)}, u32[]{:S(2)}, u32[]{:S(2)}) collective-permute-start(bf16[1,512,256]{2,1,0:T(8,128)(2,1)S(1)} %get-tuple-element.23), channel_id=1, source_target_pairs={{0,3},{1,0},{2,1},{3,2},{4,7},{5,4},{6,5},{7,6},{8,11},{9,8},{10,9... | collective-permute-start | bytes 786440 | tf_op jit(solution)/shard_map/ppermute | solution.py:29
  116.9 2.7 %collective-permute-start.19 = (bf16[1,512,256]{2,1,0:T(8,128)(2,1)S(1)}, bf16[1,512,256]{2,1,0:T(8,128)(2,1)S(1)}, u32[]{:S(2)}, u32[]{:S(2)}) collective-permute-start(bf16[1,512,256]{2,1,0:T(8,128)(2,1)S(1)} %collective-permute-done.18.refs_10_), channel_id=1, source_target_pairs={{0,3},{1,0},{2,1},{3,2},{4,7},{5,4},{6,5},{7,6},{8,11},{9,8},{10,9... | collective-permute-start | bytes 786440 | tf_op jit(solution)/shard_map/ppermute | solution.py:29
  119.6 3.1 %right_multiply.2 = (bf16[64,3,16,256]{3,2,1,0:T(8,128)(2,1)}, f32[2,1,256]{2,1,0:T(1,128)S(1)}) custom-call(s32[1]{0:T(128)} %bitcast.refs_0_.place, bf16[3,256,256]{2,1,0:T(8,128)(2,1)S(1)} %get-tuple-element.40.refs_0_, bf16[3,256,256]{2,1,0:T(8,128)(2,1)S(1)} %collective-permute-done.12.refs_1_, ...), custom_call_target="tpu_custom_call" | custom-call | flops 1073741824 | bytes 8388608 | tf_op jit(solution)/shard_map/right_multiply/pallas_call | solution.py:172
  122.8 3.6 %collective-permute-done.17.refs_7_ = bf16[1,512,256]{2,1,0:T(8,128)(2,1)S(1)} collective-permute-done((bf16[1,512,256]{2,1,0:T(8,128)(2,1)S(1)}, bf16[1,512,256]{2,1,0:T(8,128)(2,1)S(1)}, u32[]{:S(2)}, u32[]{:S(2)}) %collective-permute-start.17) | collective-permute-done | bytes 262176 | tf_op jit(solution)/shard_map/ppermute | solution.py:29
  130.1 13.8 %all-to-all-start.1 = ((bf16[64,3,16,256]{3,2,1,0:T(8,128)(2,1)}), bf16[64,3,16,256]{3,2,1,0:T(8,128)(2,1)S(1)}, u32[]{:S(2)}, u32[]{:S(2)}) async-start(bf16[64,3,16,256]{3,2,1,0:T(8,128)(2,1)} %copy-done.1), calls=%async_computation.1 | async-start | bytes 3145728 | tf_op jit(solution)/shard_map/all_to_all | solution.py:265
  143.9 1.5 fusion.4
  145.5 9.4 %all-reduce = (f32[3]{0:T(128)S(1)}, f32[80]{0:T(128)S(1)}) all-reduce(f32[3]{0:T(128)S(1)} %maximum_reduce_fusion, f32[80]{0:T(128)} %fusion.4), channel_id=1, replica_groups=mesh['fsdp'=64,'rep'=4] {'rep'}, use_global_device_ids=true, to_apply=%region_5.6 | all-reduce | flops 83 | bytes 664 | tf_op jit(solution)/shard_map/psum | solution.py:304
  154.9 28.7 %all-to-all-done.1.back = bf16[64,3,16,256]{3,2,1,0:T(8,128)(2,1)S(1)} async-done(((bf16[64,3,16,256]{3,2,1,0:T(8,128)(2,1)}), bf16[64,3,16,256]{3,2,1,0:T(8,128)(2,1)S(1)}, u32[]{:S(2)}, u32[]{:S(2)}) %all-to-all-start.1) | async-done | bytes 1572896 | tf_op jit(solution)/shard_map/all_to_all | solution.py:265
  184.3 6.1 %all-to-all-start.2 = ((f32[64,1,128]{2,1,0:T(1,128)}), f32[64,1,128]{2,1,0:T(1,128)S(1)}, u32[]{:S(2)}, u32[]{:S(2)}) async-start(f32[64,1,128]{2,1,0:T(1,128)} %broadcast_in_dim.55), calls=%async_computation.2 | async-start | bytes 65536 | tf_op jit(solution)/shard_map/all_to_all | solution.py:265
  191.5 3.8 %collective-permute-start.22 = (bf16[20,16,256]{2,1,0:T(8,128)(2,1)S(1)}, bf16[20,16,256]{2,1,0:T(8,128)(2,1)S(1)}, u32[]{:S(2)}, u32[]{:S(2)}) collective-permute-start(bf16[20,16,256]{2,1,0:T(8,128)(2,1)S(1)} %get-tuple-element.44), channel_id=1, source_target_pairs={{0,2},{1,3},{2,0},{3,1},{4,6},{5,7},{6,4},{7,5},{8,10},{9,11},{10,... | collective-permute-start | bytes 491528 | tf_op jit(solution)/shard_map/ppermute | solution.py:29
  195.3 4.3 %all-to-all-done.2 = f32[64,1,128]{2,1,0:T(1,128)S(1)} async-done(((f32[64,1,128]{2,1,0:T(1,128)}), f32[64,1,128]{2,1,0:T(1,128)S(1)}, u32[]{:S(2)}, u32[]{:S(2)}) %all-to-all-start.2) | async-done | bytes 32800 | tf_op jit(solution)/shard_map/all_to_all | solution.py:265
  200.1 2.6 %collective-permute-done.22.second = bf16[20,16,256]{2,1,0:T(8,128)(2,1)S(1)} collective-permute-done((bf16[20,16,256]{2,1,0:T(8,128)(2,1)S(1)}, bf16[20,16,256]{2,1,0:T(8,128)(2,1)S(1)}, u32[]{:S(2)}, u32[]{:S(2)}) %collective-permute-start.22) | collective-permute-done | bytes 163872 | tf_op jit(solution)/shard_map/ppermute | solution.py:29
  202.7 2.0 join_blocks.1
  (92 shorter events, 24.9 us)
Async XLA Ops:
  1.4 8.5 %collective-permute-start.1 = (bf16[40,16,256]{2,1,0:T(8,128)(2,1)S(1)}, bf16[40,16,256]{2,1,0:T(8,128)(2,1)S(1)}, u32[]{:S(2)}, u32[]{:S(2)}) collective-permute-start(bf16[40,16,256]{2,1,0:T(8,128)(2,1)S(1)} %get-tuple-element.32), channel_id=1, source_target_pairs={{0,1},{1,2},{2,3},{3,0},{4,5},{5,6},{6,7},{7,4},{8,9},{9,10},{10,1... | collective-permute-start | bytes 983048 | tf_op jit(solution)/shard_map/ppermute | solution.py:29
  3.5 7.9 %collective-permute-start.4 = (bf16[40,16,256]{2,1,0:T(8,128)(2,1)S(1)}, bf16[40,16,256]{2,1,0:T(8,128)(2,1)S(1)}, u32[]{:S(2)}, u32[]{:S(2)}) collective-permute-start(bf16[40,16,256]{2,1,0:T(8,128)(2,1)S(1)} %get-tuple-element.34), channel_id=1, source_target_pairs={{0,3},{1,0},{2,1},{3,2},{4,7},{5,4},{6,5},{7,6},{8,11},{9,8},{10,9... | collective-permute-start | bytes 983048 | tf_op jit(solution)/shard_map/ppermute | solution.py:29
  4.9 13.6 %collective-permute-start = (bf16[40,16,256]{2,1,0:T(8,128)(2,1)S(1)}, bf16[40,16,256]{2,1,0:T(8,128)(2,1)S(1)}, u32[]{:S(2)}, u32[]{:S(2)}) collective-permute-start(bf16[40,16,256]{2,1,0:T(8,128)(2,1)S(1)} %get-tuple-element.33), channel_id=1, source_target_pairs={{0,3},{1,0},{2,1},{3,2},{4,7},{5,4},{6,5},{7,6},{8,11},{9,8},{10,9... | collective-permute-start | bytes 983048 | tf_op jit(solution)/shard_map/ppermute | solution.py:29
  6.2 12.2 %collective-permute-start.3 = (bf16[40,16,256]{2,1,0:T(8,128)(2,1)S(1)}, bf16[40,16,256]{2,1,0:T(8,128)(2,1)S(1)}, u32[]{:S(2)}, u32[]{:S(2)}) collective-permute-start(bf16[40,16,256]{2,1,0:T(8,128)(2,1)S(1)} %get-tuple-element.31), channel_id=1, source_target_pairs={{0,1},{1,2},{2,3},{3,0},{4,5},{5,6},{6,7},{7,4},{8,9},{9,10},{10,1... | collective-permute-start | bytes 983048 | tf_op jit(solution)/shard_map/ppermute | solution.py:29
  12.7 11.5 %collective-permute-start.2 = (bf16[40,16,256]{2,1,0:T(8,128)(2,1)S(1)}, bf16[40,16,256]{2,1,0:T(8,128)(2,1)S(1)}, u32[]{:S(2)}, u32[]{:S(2)}) collective-permute-start(bf16[40,16,256]{2,1,0:T(8,128)(2,1)S(1)} %get-tuple-element.36), channel_id=1, source_target_pairs={{0,1},{1,2},{2,3},{3,0},{4,5},{5,6},{6,7},{7,4},{8,9},{9,10},{10,1... | collective-permute-start | bytes 983048 | tf_op jit(solution)/shard_map/ppermute | solution.py:29
  14.3 11.1 %collective-permute-start.5 = (bf16[40,16,256]{2,1,0:T(8,128)(2,1)S(1)}, bf16[40,16,256]{2,1,0:T(8,128)(2,1)S(1)}, u32[]{:S(2)}, u32[]{:S(2)}) collective-permute-start(bf16[40,16,256]{2,1,0:T(8,128)(2,1)S(1)} %get-tuple-element.35), channel_id=1, source_target_pairs={{0,3},{1,0},{2,1},{3,2},{4,7},{5,4},{6,5},{7,6},{8,11},{9,8},{10,9... | collective-permute-start | bytes 983048 | tf_op jit(solution)/shard_map/ppermute | solution.py:29
  29.0 55.2 %all-to-all-start = ((bf16[64,3,16,256]{3,2,1,0:T(8,128)(2,1)}), bf16[64,3,16,256]{3,2,1,0:T(8,128)(2,1)S(1)}, u32[]{:S(2)}, u32[]{:S(2)}) async-start(bf16[64,3,16,256]{3,2,1,0:T(8,128)(2,1)} %get-tuple-element.21), calls=%async_computation | async-start | bytes 3145728 | tf_op jit(solution)/shard_map/all_to_all | solution.py:265
  44.2 13.6 %collective-permute-start.9 = (bf16[2,512,256]{2,1,0:T(8,128)(2,1)S(1)}, bf16[2,512,256]{2,1,0:T(8,128)(2,1)S(1)}, u32[]{:S(2)}, u32[]{:S(2)}) collective-permute-start(bf16[2,512,256]{2,1,0:T(8,128)(2,1)S(1)} %get-tuple-element.19), channel_id=1, source_target_pairs={{0,3},{1,0},{2,1},{3,2},{4,7},{5,4},{6,5},{7,6},{8,11},{9,8},{10,9... | collective-permute-start | bytes 1572872 | tf_op jit(solution)/shard_map/ppermute | solution.py:29
  47.0 14.3 %collective-permute-start.6 = (bf16[2,512,256]{2,1,0:T(8,128)(2,1)S(1)}, bf16[2,512,256]{2,1,0:T(8,128)(2,1)S(1)}, u32[]{:S(2)}, u32[]{:S(2)}) collective-permute-start(bf16[2,512,256]{2,1,0:T(8,128)(2,1)S(1)} %get-tuple-element.18), channel_id=1, source_target_pairs={{0,1},{1,2},{2,3},{3,0},{4,5},{5,6},{6,7},{7,4},{8,9},{9,10},{10,1... | collective-permute-start | bytes 1572872 | tf_op jit(solution)/shard_map/ppermute | solution.py:29
  47.0 22.1 %collective-permute-start.11 = (bf16[2,512,256]{2,1,0:T(8,128)(2,1)S(1)}, bf16[2,512,256]{2,1,0:T(8,128)(2,1)S(1)}, u32[]{:S(2)}, u32[]{:S(2)}) collective-permute-start(bf16[2,512,256]{2,1,0:T(8,128)(2,1)S(1)} %get-tuple-element.18), channel_id=1, source_target_pairs={{0,3},{1,0},{2,1},{3,2},{4,7},{5,4},{6,5},{7,6},{8,11},{9,8},{10,9... | collective-permute-start | bytes 1572872 | tf_op jit(solution)/shard_map/ppermute | solution.py:29
  49.6 22.5 %collective-permute-start.7 = (bf16[2,512,256]{2,1,0:T(8,128)(2,1)S(1)}, bf16[2,512,256]{2,1,0:T(8,128)(2,1)S(1)}, u32[]{:S(2)}, u32[]{:S(2)}) collective-permute-start(bf16[2,512,256]{2,1,0:T(8,128)(2,1)S(1)} %get-tuple-element.19), channel_id=1, source_target_pairs={{0,1},{1,2},{2,3},{3,0},{4,5},{5,6},{6,7},{7,4},{8,9},{9,10},{10,1... | collective-permute-start | bytes 1572872 | tf_op jit(solution)/shard_map/ppermute | solution.py:29
  57.8 22.5 %collective-permute-start.10 = (bf16[2,512,256]{2,1,0:T(8,128)(2,1)S(1)}, bf16[2,512,256]{2,1,0:T(8,128)(2,1)S(1)}, u32[]{:S(2)}, u32[]{:S(2)}) collective-permute-start(bf16[2,512,256]{2,1,0:T(8,128)(2,1)S(1)} %collective-permute-done.9.refs_10_), channel_id=1, source_target_pairs={{0,3},{1,0},{2,1},{3,2},{4,7},{5,4},{6,5},{7,6},{8,11},{9,8},{10,9... | collective-permute-start | bytes 1572872 | tf_op jit(solution)/shard_map/ppermute | solution.py:29
  61.2 22.1 %collective-permute-start.8 = (bf16[2,512,256]{2,1,0:T(8,128)(2,1)S(1)}, bf16[2,512,256]{2,1,0:T(8,128)(2,1)S(1)}, u32[]{:S(2)}, u32[]{:S(2)}) collective-permute-start(bf16[2,512,256]{2,1,0:T(8,128)(2,1)S(1)} %collective-permute-done.6.refs_5_), channel_id=1, source_target_pairs={{0,1},{1,2},{2,3},{3,0},{4,5},{5,6},{6,7},{7,4},{8,9},{9,10},{10,1... | collective-permute-start | bytes 1572872 | tf_op jit(solution)/shard_map/ppermute | solution.py:29
  89.5 30.0 %copy-start.5 = (bf16[2,512,256]{2,1,0:T(8,128)(2,1)S(1)}, bf16[2,512,256]{2,1,0:T(8,128)(2,1)}, u32[]{:S(2)}) copy-start(bf16[2,512,256]{2,1,0:T(8,128)(2,1)} %copy-done.4) | copy-start | bytes 1572868
  89.6 30.0 %copy-start.7 = (bf16[2,512,256]{2,1,0:T(8,128)(2,1)S(1)}, bf16[2,512,256]{2,1,0:T(8,128)(2,1)}, u32[]{:S(2)}) copy-start(bf16[2,512,256]{2,1,0:T(8,128)(2,1)} %copy-done.6) | copy-start | bytes 1572868
  89.6 30.0 %copy-start.9 = (bf16[2,512,256]{2,1,0:T(8,128)(2,1)S(1)}, bf16[2,512,256]{2,1,0:T(8,128)(2,1)}, u32[]{:S(2)}) copy-start(bf16[2,512,256]{2,1,0:T(8,128)(2,1)} %copy-done.8) | copy-start | bytes 1572868
  89.6 30.0 %copy-start.11 = (bf16[2,512,256]{2,1,0:T(8,128)(2,1)S(1)}, bf16[2,512,256]{2,1,0:T(8,128)(2,1)}, u32[]{:S(2)}) copy-start(bf16[2,512,256]{2,1,0:T(8,128)(2,1)} %copy-done.10) | copy-start | bytes 1572868
  89.6 30.0 %copy-start.13 = (bf16[2,512,256]{2,1,0:T(8,128)(2,1)S(1)}, bf16[2,512,256]{2,1,0:T(8,128)(2,1)}, u32[]{:S(2)}) copy-start(bf16[2,512,256]{2,1,0:T(8,128)(2,1)} %copy-done.12) | copy-start | bytes 1572868
  89.7 27.2 %collective-permute-start.12 = (bf16[3,256,256]{2,1,0:T(8,128)(2,1)S(1)}, bf16[3,256,256]{2,1,0:T(8,128)(2,1)S(1)}, u32[]{:S(2)}, u32[]{:S(2)}) collective-permute-start(bf16[3,256,256]{2,1,0:T(8,128)(2,1)S(1)} %get-tuple-element.39), channel_id=1, source_target_pairs={{0,1},{1,2},{2,3},{3,0},{4,5},{5,6},{6,7},{7,4},{8,9},{9,10},{10,1... | collective-permute-start | bytes 1179656 | tf_op jit(solution)/shard_map/ppermute | solution.py:29
  90.0 26.9 %collective-permute-start.13 = (bf16[3,256,256]{2,1,0:T(8,128)(2,1)S(1)}, bf16[3,256,256]{2,1,0:T(8,128)(2,1)S(1)}, u32[]{:S(2)}, u32[]{:S(2)}) collective-permute-start(bf16[3,256,256]{2,1,0:T(8,128)(2,1)S(1)} %get-tuple-element.38), channel_id=1, source_target_pairs={{0,2},{1,3},{2,0},{3,1},{4,6},{5,7},{6,4},{7,5},{8,10},{9,11},{10,... | collective-permute-start | bytes 1179656 | tf_op jit(solution)/shard_map/ppermute | solution.py:29
  92.3 21.9 %collective-permute-start.15 = (bf16[1,512,256]{2,1,0:T(8,128)(2,1)S(1)}, bf16[1,512,256]{2,1,0:T(8,128)(2,1)S(1)}, u32[]{:S(2)}, u32[]{:S(2)}) collective-permute-start(bf16[1,512,256]{2,1,0:T(8,128)(2,1)S(1)} %get-tuple-element.23), channel_id=1, source_target_pairs={{0,1},{1,2},{2,3},{3,0},{4,5},{5,6},{6,7},{7,4},{8,9},{9,10},{10,1... | collective-permute-start | bytes 786440 | tf_op jit(solution)/shard_map/ppermute | solution.py:29
  93.4 20.9 %collective-permute-start.18 = (bf16[1,512,256]{2,1,0:T(8,128)(2,1)S(1)}, bf16[1,512,256]{2,1,0:T(8,128)(2,1)S(1)}, u32[]{:S(2)}, u32[]{:S(2)}) collective-permute-start(bf16[1,512,256]{2,1,0:T(8,128)(2,1)S(1)} %get-tuple-element.24), channel_id=1, source_target_pairs={{0,3},{1,0},{2,1},{3,2},{4,7},{5,4},{6,5},{7,6},{8,11},{9,8},{10,9... | collective-permute-start | bytes 786440 | tf_op jit(solution)/shard_map/ppermute | solution.py:29
  95.1 24.5 %collective-permute-start.14 = (bf16[3,256,256]{2,1,0:T(8,128)(2,1)S(1)}, bf16[3,256,256]{2,1,0:T(8,128)(2,1)S(1)}, u32[]{:S(2)}, u32[]{:S(2)}) collective-permute-start(bf16[3,256,256]{2,1,0:T(8,128)(2,1)S(1)} %get-tuple-element.37), channel_id=1, source_target_pairs={{0,3},{1,0},{2,1},{3,2},{4,7},{5,4},{6,5},{7,6},{8,11},{9,8},{10,9... | collective-permute-start | bytes 1179656 | tf_op jit(solution)/shard_map/ppermute | solution.py:29
  114.2 8.5 %collective-permute-start.16 = (bf16[1,512,256]{2,1,0:T(8,128)(2,1)S(1)}, bf16[1,512,256]{2,1,0:T(8,128)(2,1)S(1)}, u32[]{:S(2)}, u32[]{:S(2)}) collective-permute-start(bf16[1,512,256]{2,1,0:T(8,128)(2,1)S(1)} %get-tuple-element.24), channel_id=1, source_target_pairs={{0,1},{1,2},{2,3},{3,0},{4,5},{5,6},{6,7},{7,4},{8,9},{9,10},{10,1... | collective-permute-start | bytes 786440 | tf_op jit(solution)/shard_map/ppermute | solution.py:29
  114.2 8.5 %collective-permute-start.20 = (bf16[1,512,256]{2,1,0:T(8,128)(2,1)S(1)}, bf16[1,512,256]{2,1,0:T(8,128)(2,1)S(1)}, u32[]{:S(2)}, u32[]{:S(2)}) collective-permute-start(bf16[1,512,256]{2,1,0:T(8,128)(2,1)S(1)} %get-tuple-element.23), channel_id=1, source_target_pairs={{0,3},{1,0},{2,1},{3,2},{4,7},{5,4},{6,5},{7,6},{8,11},{9,8},{10,9... | collective-permute-start | bytes 786440 | tf_op jit(solution)/shard_map/ppermute | solution.py:29
  116.9 9.4 %collective-permute-start.17 = (bf16[1,512,256]{2,1,0:T(8,128)(2,1)S(1)}, bf16[1,512,256]{2,1,0:T(8,128)(2,1)S(1)}, u32[]{:S(2)}, u32[]{:S(2)}) collective-permute-start(bf16[1,512,256]{2,1,0:T(8,128)(2,1)S(1)} %collective-permute-done.15.refs_5_), channel_id=1, source_target_pairs={{0,1},{1,2},{2,3},{3,0},{4,5},{5,6},{6,7},{7,4},{8,9},{9,10},{10,1... | collective-permute-start | bytes 786440 | tf_op jit(solution)/shard_map/ppermute | solution.py:29
  116.9 9.4 %collective-permute-start.19 = (bf16[1,512,256]{2,1,0:T(8,128)(2,1)S(1)}, bf16[1,512,256]{2,1,0:T(8,128)(2,1)S(1)}, u32[]{:S(2)}, u32[]{:S(2)}) collective-permute-start(bf16[1,512,256]{2,1,0:T(8,128)(2,1)S(1)} %collective-permute-done.18.refs_10_), channel_id=1, source_target_pairs={{0,3},{1,0},{2,1},{3,2},{4,7},{5,4},{6,5},{7,6},{8,11},{9,8},{10,9... | collective-permute-start | bytes 786440 | tf_op jit(solution)/shard_map/ppermute | solution.py:29
  130.1 53.6 %all-to-all-start.1 = ((bf16[64,3,16,256]{3,2,1,0:T(8,128)(2,1)}), bf16[64,3,16,256]{3,2,1,0:T(8,128)(2,1)S(1)}, u32[]{:S(2)}, u32[]{:S(2)}) async-start(bf16[64,3,16,256]{3,2,1,0:T(8,128)(2,1)} %copy-done.1), calls=%async_computation.1 | async-start | bytes 3145728 | tf_op jit(solution)/shard_map/all_to_all | solution.py:265
  184.3 15.3 %all-to-all-start.2 = ((f32[64,1,128]{2,1,0:T(1,128)}), f32[64,1,128]{2,1,0:T(1,128)S(1)}, u32[]{:S(2)}, u32[]{:S(2)}) async-start(f32[64,1,128]{2,1,0:T(1,128)} %broadcast_in_dim.55), calls=%async_computation.2 | async-start | bytes 65536 | tf_op jit(solution)/shard_map/all_to_all | solution.py:265
  191.4 8.7 %collective-permute-start.21 = (bf16[20,16,256]{2,1,0:T(8,128)(2,1)S(1)}, bf16[20,16,256]{2,1,0:T(8,128)(2,1)S(1)}, u32[]{:S(2)}, u32[]{:S(2)}) collective-permute-start(bf16[20,16,256]{2,1,0:T(8,128)(2,1)S(1)} %get-tuple-element.45), channel_id=1, source_target_pairs={{0,1},{1,2},{2,3},{3,0},{4,5},{5,6},{6,7},{7,4},{8,9},{9,10},{10,1... | collective-permute-start | bytes 491528 | tf_op jit(solution)/shard_map/ppermute | solution.py:29
  191.5 11.2 %collective-permute-start.22 = (bf16[20,16,256]{2,1,0:T(8,128)(2,1)S(1)}, bf16[20,16,256]{2,1,0:T(8,128)(2,1)S(1)}, u32[]{:S(2)}, u32[]{:S(2)}) collective-permute-start(bf16[20,16,256]{2,1,0:T(8,128)(2,1)S(1)} %get-tuple-element.44), channel_id=1, source_target_pairs={{0,2},{1,3},{2,0},{3,1},{4,6},{5,7},{6,4},{7,5},{8,10},{9,11},{10,... | collective-permute-start | bytes 491528 | tf_op jit(solution)/shard_map/ppermute | solution.py:29
  195.3 7.4 %collective-permute-start.23 = (bf16[20,16,256]{2,1,0:T(8,128)(2,1)S(1)}, bf16[20,16,256]{2,1,0:T(8,128)(2,1)S(1)}, u32[]{:S(2)}, u32[]{:S(2)}) collective-permute-start(bf16[20,16,256]{2,1,0:T(8,128)(2,1)S(1)} %get-tuple-element.43), channel_id=1, source_target_pairs={{0,3},{1,0},{2,1},{3,2},{4,7},{5,4},{6,5},{7,6},{8,11},{9,8},{10,9... | collective-permute-start | bytes 491528 | tf_op jit(solution)/shard_map/ppermute | solution.py:29
  (15 other events, 140.5 us)

commit v4 on v1

--- a/solution.py
+++ b/solution.py
@@ -47,9 +47,9 @@
     return (pieces[0], near_left, last_right, near_right, last_left), (on_right, on_left)
 
 
-def gather_over_rep(value):
+def gather_over_rep(value, *others):
     middle = value.shape[1] // 2
-    top, bottom = value[:, :middle], value[:, middle:]
+    top, bottom = after((value[:, :middle], value[:, middle:]), *others)
     left_top = shift(top, 1)
     right_bottom = shift(bottom, 3)
     left_bottom = shift(bottom, 1)
@@ -62,13 +62,13 @@
 def sum_pack_kernel(source, own, near_left, last_right, near_right, last_left, low, out):
     middle = near_left.shape[0]
 
-    @pl.loop(0, middle)
+    @pl.loop(0, middle, unroll=4)
     def _(b):
         low[b] = (wide(own[b]) + (wide(near_left[b]) + wide(last_right[b]))).astype(jnp.bfloat16)
         c = middle + b
         low[c] = (wide(own[c]) + (wide(near_right[b]) + wide(last_left[b]))).astype(jnp.bfloat16)
 
-    @pl.loop(0, OWNERS)
+    @pl.loop(0, OWNERS, unroll=4)
     def _(o):
         for s in range(CAP):
             out[o, s] = low[source[s * OWNERS + o]]
@@ -203,7 +203,7 @@
     held[:, :2] = back01[...]
     held[:, 2] = back2[:, 0]
 
-    @pl.loop(0, groups)
+    @pl.loop(0, groups, unroll=2)
     def _(g):
         parts = []
         for i in range(REP):
@@ -234,7 +234,7 @@
     for k, piece in enumerate((own, first, second, third)):
         held[lax.rem(place[0] + (REP - k), REP)] = piece[...]
 
-    @pl.loop(0, groups)
+    @pl.loop(0, groups, unroll=2)
     def _(g):
         parts = [wide(held[q, g]) for q in range(REP)]
         for i in range(REP):
@@ -288,7 +288,7 @@
         for k in range(REP)
     ]
     terms, passing = sum_over_rep(pieces)
-    rights01 = gather_over_rep(after(right_root[0, :2], *passing))
+    rights01 = gather_over_rep(right_root[0, :2], *passing)
     low, packed = sum_pack(source, terms)
     owned = exchange(packed)
     adam = lax.psum(adam_squares(low, moment), "rep")
@@ -297,10 +297,13 @@
         return [sent[0]] + [shift(sent[k], k) for k in (1, 2, 3)]
 
     sent01 = left_multiply(after(place_ref, *rights01), owned, left_root[0], 0, 2)
-    held01 = spread(sent01)
+    across = shift(sent01[2][:1], 2)
+    back_once = shift(sent01[2][1:], 3)
+    held01 = [sent01[0], shift(sent01[1], 1), None, shift(sent01[3], 3)]
+    held01[2] = jnp.concatenate([across, shift(back_once, 3)])
     result01, square01 = right_multiply(place_ref, held01, rights01)
     back01 = exchange(result01)
-    rights2 = gather_over_rep(after(right_root[0, 2:], *held01))
+    rights2 = gather_over_rep(right_root[0, 2:], *held01)
     sent2 = left_multiply(after(place_ref, *held01), owned, left_root[0], 2, 1)
     held2 = spread(sent2)
     result2, square2 = right_multiply(place_ref, held2, rights2)

time: 199 us -> 200 us (level)
  waiting for transfers between devices: 90 us -> 72.7 us
  starting transfers between devices: 69.3 us -> 84.3 us
  blocking collectives: 7.17 us -> 9.43 us
    ppermute x27 -> x29, waiting for transfers between devices: 75.1 us -> 62.2 us  [shift(): lax.ppermute(value, 'rep', [(i, (i + step) % REP) for i in range(REP)])]
    ppermute x27 -> x29, starting transfers between devices: 27.9 us -> 39.3 us  [shift(): lax.ppermute(value, 'rep', [(i, (i + step) % REP) for i in range(REP)])]
    all_to_all x4, waiting for transfers between devices: 14.9 us -> 10.5 us  [exchange(): return lax.all_to_all(value, 'fsdp', split_axis=0, concat_axis=0)]
    all_to_all x4, starting transfers between devices: 41.3 us -> 45 us  [exchange(): return lax.all_to_all(value, 'fsdp', split_axis=0, concat_axis=0)]
    psum x1, blocking collectives: 7.17 us -> 9.43 us  [shards(): lax.psum(jnp.sum(jnp.concatenate([square01, square2]), axis=(1, 2)), 'rep')]
    unnamed x22 -> x27, local copies, waits for them, and re-layouts: 4.16 us -> 5.88 us
  transfers between devices with their start and end apart: 31 -> 33, of which waited for: 17 -> 18; matrix products, arithmetic and copies ran while one was open for 4% -> 4% of each run, Pallas kernels for 2% -> 2%
where the time goes in v4:
time: 200 us
  starting transfers between devices  84.3 us (42%)
  waiting for transfers between devices  72.7 us (36%)
  Pallas kernels  16.8 us (8%)
  local copies, waits for them, and re-layouts  11.9 us (6%)
  blocking collectives  9.43 us (5%)
  other arithmetic  4.26 us (2%)
    ppermute x29, waiting for transfers between devices, shift(): lax.ppermute(value, 'rep', [(i, (i + step) % REP) for i in range(REP)])  62.2 us
    all_to_all x4, starting transfers between devices, exchange(): return lax.all_to_all(value, 'fsdp', split_axis=0, concat_axis=0)  45 us
    ppermute x29, starting transfers between devices, shift(): lax.ppermute(value, 'rep', [(i, (i + step) % REP) for i in range(REP)])  39.3 us
    all_to_all x4, waiting for transfers between devices, exchange(): return lax.all_to_all(value, 'fsdp', split_axis=0, concat_axis=0)  10.5 us
    psum x1, blocking collectives, shards(): lax.psum(jnp.sum(jnp.concatenate([square01, square2]), axis=(1, 2)), 'rep')  9.43 us
    pallas_call x2, Pallas kernels, left_multiply(): pl.pallas_call(lambda *refs: left_kernel(first, *refs), grid=(count,), ou...  6.44 us
    unnamed x27, local copies, waits for them, and re-layouts  5.88 us
    pallas_call x2, Pallas kernels, right_multiply(): pl.pallas_call(right_kernel, grid=(count,), out_shape=[jax.ShapeDtypeStru...  5.27 us
  transfers between devices with their start and end apart: 33, of which 18 were waited for; matrix products, arithmetic and copies ran while one was open for 4% of the time, Pallas kernels for 2%

profile of v4, /device:TPU:1, one launch (start us, length us, event | category | flops | bytes accessed | tf_op | source)
XLA Modules:
  0.0 199.7 jit_solution(4134827029099406081)
XLA Ops:
  6.5 3.4 %collective-permute-done.1 = bf16[40,16,256]{2,1,0:T(8,128)(2,1)S(1)} collective-permute-done((bf16[40,16,256]{2,1,0:T(8,128)(2,1)S(1)}, bf16[40,16,256]{2,1,0:T(8,128)(2,1)S(1)}, u32[]{:S(2)}, u32[]{:S(2)}) %collective-permute-start.1) | collective-permute-done | bytes 327712 | tf_op jit(solution)/shard_map/ppermute | solution.py:29
  18.4 5.8 %collective-permute-done.2.last_right = bf16[40,16,256]{2,1,0:T(8,128)(2,1)S(1)} collective-permute-done((bf16[40,16,256]{2,1,0:T(8,128)(2,1)S(1)}, bf16[40,16,256]{2,1,0:T(8,128)(2,1)S(1)}, u32[]{:S(2)}, u32[]{:S(2)}) %collective-permute-start.2) | collective-permute-done | bytes 327712 | tf_op jit(solution)/shard_map/ppermute | solution.py:29
  25.5 2.3 %sum_pack.1 = (bf16[80,16,256]{2,1,0:T(8,128)(2,1)S(1)}, bf16[64,3,16,256]{3,2,1,0:T(8,128)(2,1)}) custom-call(s32[192]{0:T(256)S(1)} %select_reduce_fusion.1.source, bf16[80,16,256]{2,1,0:T(8,128)(2,1)S(1)} %dynamic-slice_bitcast_fusion.own, bf16[40,16,256]{2,1,0:T(8,128)(2,1)S(1)} %collective-permute-done.near_left, ...), custom_call_target="tpu_custom_call" | custom-call | tf_op jit(solution)/shard_map/sum_pack/pallas_call | solution.py:79
  27.7 13.9 %all-to-all-start = ((bf16[64,3,16,256]{3,2,1,0:T(8,128)(2,1)}), bf16[64,3,16,256]{3,2,1,0:T(8,128)(2,1)S(1)}, u32[]{:S(2)}, u32[]{:S(2)}) async-start(bf16[64,3,16,256]{3,2,1,0:T(8,128)(2,1)} %get-tuple-element.23), calls=%async_computation | async-start | bytes 3145728 | tf_op jit(solution)/shard_map/all_to_all | solution.py:266
  43.9 2.7 %collective-permute-start.9 = (bf16[2,512,256]{2,1,0:T(8,128)(2,1)S(1)}, bf16[2,512,256]{2,1,0:T(8,128)(2,1)S(1)}, u32[]{:S(2)}, u32[]{:S(2)}) collective-permute-start(bf16[2,512,256]{2,1,0:T(8,128)(2,1)S(1)} %get-tuple-element.21), channel_id=1, source_target_pairs={{0,3},{1,0},{2,1},{3,2},{4,7},{5,4},{6,5},{7,6},{8,11},{9,8},{10,9... | collective-permute-start | bytes 1572872 | tf_op jit(solution)/shard_map/ppermute | solution.py:29
  46.6 2.7 %collective-permute-start.11 = (bf16[2,512,256]{2,1,0:T(8,128)(2,1)S(1)}, bf16[2,512,256]{2,1,0:T(8,128)(2,1)S(1)}, u32[]{:S(2)}, u32[]{:S(2)}) collective-permute-start(bf16[2,512,256]{2,1,0:T(8,128)(2,1)S(1)} %get-tuple-element.20), channel_id=1, source_target_pairs={{0,3},{1,0},{2,1},{3,2},{4,7},{5,4},{6,5},{7,6},{8,11},{9,8},{10,9... | collective-permute-start | bytes 1572872 | tf_op jit(solution)/shard_map/ppermute | solution.py:29
  49.2 8.2 %collective-permute-done.9.refs_10_ = bf16[2,512,256]{2,1,0:T(8,128)(2,1)S(1)} collective-permute-done((bf16[2,512,256]{2,1,0:T(8,128)(2,1)S(1)}, bf16[2,512,256]{2,1,0:T(8,128)(2,1)S(1)}, u32[]{:S(2)}, u32[]{:S(2)}) %collective-permute-start.9) | collective-permute-done | bytes 524320 | tf_op jit(solution)/shard_map/ppermute | solution.py:29
  57.4 3.4 %collective-permute-start.10 = (bf16[2,512,256]{2,1,0:T(8,128)(2,1)S(1)}, bf16[2,512,256]{2,1,0:T(8,128)(2,1)S(1)}, u32[]{:S(2)}, u32[]{:S(2)}) collective-permute-start(bf16[2,512,256]{2,1,0:T(8,128)(2,1)S(1)} %collective-permute-done.9.refs_10_), channel_id=1, source_target_pairs={{0,3},{1,0},{2,1},{3,2},{4,7},{5,4},{6,5},{7,6},{8,11},{9,8},{10,9... | collective-permute-start | bytes 1572872 | tf_op jit(solution)/shard_map/ppermute | solution.py:29
  61.6 7.0 %collective-permute-done.11.refs_9_ = bf16[2,512,256]{2,1,0:T(8,128)(2,1)S(1)} collective-permute-done((bf16[2,512,256]{2,1,0:T(8,128)(2,1)S(1)}, bf16[2,512,256]{2,1,0:T(8,128)(2,1)S(1)}, u32[]{:S(2)}, u32[]{:S(2)}) %collective-permute-start.11) | collective-permute-done | bytes 524320 | tf_op jit(solution)/shard_map/ppermute | solution.py:29
  69.4 2.3 %collective-permute-done.7.refs_6_ = bf16[2,512,256]{2,1,0:T(8,128)(2,1)S(1)} collective-permute-done((bf16[2,512,256]{2,1,0:T(8,128)(2,1)S(1)}, bf16[2,512,256]{2,1,0:T(8,128)(2,1)S(1)}, u32[]{:S(2)}, u32[]{:S(2)}) %collective-permute-start.7) | collective-permute-done | bytes 524320 | tf_op jit(solution)/shard_map/ppermute | solution.py:29
  72.5 7.3 %collective-permute-done.10.refs_8_ = bf16[2,512,256]{2,1,0:T(8,128)(2,1)S(1)} collective-permute-done((bf16[2,512,256]{2,1,0:T(8,128)(2,1)S(1)}, bf16[2,512,256]{2,1,0:T(8,128)(2,1)S(1)}, u32[]{:S(2)}, u32[]{:S(2)}) %collective-permute-start.10) | collective-permute-done | bytes 524320 | tf_op jit(solution)/shard_map/ppermute | solution.py:29
  80.7 2.3 %collective-permute-done.8.refs_7_ = bf16[2,512,256]{2,1,0:T(8,128)(2,1)S(1)} collective-permute-done((bf16[2,512,256]{2,1,0:T(8,128)(2,1)S(1)}, bf16[2,512,256]{2,1,0:T(8,128)(2,1)S(1)}, u32[]{:S(2)}, u32[]{:S(2)}) %collective-permute-start.8) | collective-permute-done | bytes 524320 | tf_op jit(solution)/shard_map/ppermute | solution.py:29
  83.8 3.8 %left_multiply.2 = bf16[4,2,256,256]{3,2,1,0:T(8,128)(2,1)S(1)} custom-call(s32[1]{0:T(128)} %bitcast.refs_0_.place, bf16[64,3,16,256]{3,2,1,0:T(8,128)(2,1)S(1)} %all-to-all-done.refs_1_, bf16[3,1024,1024]{2,1,0:T(8,128)(2,1)} %bitcast.55), custom_call_target="tpu_custom_call" | custom-call | flops 1073741824 | bytes 8388608 | tf_op jit(solution)/shard_map/left_multiply/pallas_call | solution.py:116
  89.7 2.5 %collective-permute-start.16 = (bf16[2,256,256]{2,1,0:T(8,128)(2,1)S(1)}, bf16[2,256,256]{2,1,0:T(8,128)(2,1)S(1)}, u32[]{:S(2)}, u32[]{:S(2)}) collective-permute-start(bf16[2,256,256]{2,1,0:T(8,128)(2,1)S(1)} %get-tuple-element.41), channel_id=1, source_target_pairs={{0,3},{1,0},{2,1},{3,2},{4,7},{5,4},{6,5},{7,6},{8,11},{9,8},{10,9... | collective-permute-start | bytes 786440 | tf_op jit(solution)/shard_map/ppermute | solution.py:29
  92.2 2.4 %collective-permute-done.14 = bf16[1,256,256]{2,1,0:T(8,128)(2,1)S(1)} collective-permute-done((bf16[1,256,256]{2,1,0:T(8,128)(2,1)S(1)}, bf16[1,256,256]{2,1,0:T(8,128)(2,1)S(1)}, u32[]{:S(2)}, u32[]{:S(2)}) %collective-permute-start.14) | collective-permute-done | bytes 131104 | tf_op jit(solution)/shard_map/ppermute | solution.py:29
  94.6 3.6 %collective-permute-start.15 = (bf16[1,256,256]{2,1,0:T(8,128)(2,1)S(1)}, bf16[1,256,256]{2,1,0:T(8,128)(2,1)S(1)}, u32[]{:S(2)}, u32[]{:S(2)}) collective-permute-start(bf16[1,256,256]{2,1,0:T(8,128)(2,1)S(1)} %collective-permute-done.14), channel_id=1, source_target_pairs={{0,3},{1,0},{2,1},{3,2},{4,7},{5,4},{6,5},{7,6},{8,11},{9,8},{10,9... | collective-permute-start | bytes 393224 | tf_op jit(solution)/shard_map/ppermute | solution.py:29
  98.2 5.0 %collective-permute-done.15 = bf16[1,256,256]{2,1,0:T(8,128)(2,1)S(1)} collective-permute-done((bf16[1,256,256]{2,1,0:T(8,128)(2,1)S(1)}, bf16[1,256,256]{2,1,0:T(8,128)(2,1)S(1)}, u32[]{:S(2)}, u32[]{:S(2)}) %collective-permute-start.15) | collective-permute-done | bytes 131104 | tf_op jit(solution)/shard_map/ppermute | solution.py:29
  103.3 3.4 %right_multiply.2 = (bf16[64,2,16,256]{3,2,1,0:T(8,128)(2,1)S(1)}, f32[2,1,256]{2,1,0:T(1,128)S(1)}) custom-call(s32[1]{0:T(128)} %bitcast.refs_0_.place, bf16[2,256,256]{2,1,0:T(8,128)(2,1)S(1)} %get-tuple-element.43.refs_0_, bf16[2,256,256]{2,1,0:T(8,128)(2,1)S(1)} %collective-permute-done.12.refs_1_, ...), custom_call_target="tpu_custom_call" | custom-call | flops 1073741824 | bytes 8388608 | tf_op jit(solution)/shard_map/right_multiply/pallas_call | solution.py:171
  107.7 12.1 %all-to-all-start.1 = ((bf16[64,2,16,256]{3,2,1,0:T(8,128)(2,1)}), bf16[64,2,16,256]{3,2,1,0:T(8,128)(2,1)S(1)}, u32[]{:S(2)}, u32[]{:S(2)}) async-start(bf16[64,2,16,256]{3,2,1,0:T(8,128)(2,1)} %copy-done), calls=%async_computation.1 | async-start | bytes 2097152 | tf_op jit(solution)/shard_map/all_to_all | solution.py:266
  121.4 2.3 %collective-permute-start.23 = (bf16[1,512,256]{2,1,0:T(8,128)(2,1)S(1)}, bf16[1,512,256]{2,1,0:T(8,128)(2,1)S(1)}, u32[]{:S(2)}, u32[]{:S(2)}) collective-permute-start(bf16[1,512,256]{2,1,0:T(8,128)(2,1)S(1)} %get-tuple-element.27), channel_id=1, source_target_pairs={{0,3},{1,0},{2,1},{3,2},{4,7},{5,4},{6,5},{7,6},{8,11},{9,8},{10,9... | collective-permute-start | bytes 786440 | tf_op jit(solution)/shard_map/ppermute | solution.py:29
  123.7 2.7 %left_multiply.3 = bf16[4,1,256,256]{3,2,1,0:T(8,128)(2,1)S(1)} custom-call(s32[1]{0:T(128)} %bitcast.refs_0_.place, bf16[64,3,16,256]{3,2,1,0:T(8,128)(2,1)S(1)} %all-to-all-done.refs_1_, bf16[3,1024,1024]{2,1,0:T(8,128)(2,1)} %bitcast.56), custom_call_target="tpu_custom_call" | custom-call | flops 536870912 | bytes 4194304 | tf_op jit(solution)/shard_map/left_multiply/pallas_call | solution.py:116
  126.5 2.4 %collective-permute-start.18 = (bf16[1,256,256]{2,1,0:T(8,128)(2,1)S(1)}, bf16[1,256,256]{2,1,0:T(8,128)(2,1)S(1)}, u32[]{:S(2)}, u32[]{:S(2)}) collective-permute-start(bf16[1,256,256]{2,1,0:T(8,128)(2,1)S(1)} %get-tuple-element.55), channel_id=1, source_target_pairs={{0,2},{1,3},{2,0},{3,1},{4,6},{5,7},{6,4},{7,5},{8,10},{9,11},{10,... | collective-permute-start | bytes 393224 | tf_op jit(solution)/shard_map/ppermute | solution.py:29
  129.7 2.2 %collective-permute-done.17.refs_1_ = bf16[1,256,256]{2,1,0:T(8,128)(2,1)S(1)} collective-permute-done((bf16[1,256,256]{2,1,0:T(8,128)(2,1)S(1)}, bf16[1,256,256]{2,1,0:T(8,128)(2,1)S(1)}, u32[]{:S(2)}, u32[]{:S(2)}) %collective-permute-start.17) | collective-permute-done | bytes 131104 | tf_op jit(solution)/shard_map/ppermute | solution.py:29
  133.6 2.7 %collective-permute-start.24 = (bf16[1,512,256]{2,1,0:T(8,128)(2,1)S(1)}, bf16[1,512,256]{2,1,0:T(8,128)(2,1)S(1)}, u32[]{:S(2)}, u32[]{:S(2)}) collective-permute-start(bf16[1,512,256]{2,1,0:T(8,128)(2,1)S(1)} %collective-permute-done.23.refs_10_), channel_id=1, source_target_pairs={{0,3},{1,0},{2,1},{3,2},{4,7},{5,4},{6,5},{7,6},{8,11},{9,8},{10,9... | collective-permute-start | bytes 786440 | tf_op jit(solution)/shard_map/ppermute | solution.py:29
  136.6 8.8 %collective-permute-done.19.refs_3_ = bf16[1,256,256]{2,1,0:T(8,128)(2,1)S(1)} collective-permute-done((bf16[1,256,256]{2,1,0:T(8,128)(2,1)S(1)}, bf16[1,256,256]{2,1,0:T(8,128)(2,1)S(1)}, u32[]{:S(2)}, u32[]{:S(2)}) %collective-permute-start.19) | collective-permute-done | bytes 131104 | tf_op jit(solution)/shard_map/ppermute | solution.py:29
  148.5 12.6 %all-to-all-start.2 = ((bf16[64,1,16,256]{3,2,1,0:T(8,128)(2,1)}), bf16[64,1,16,256]{3,2,1,0:T(8,128)(2,1)S(1)}, u32[]{:S(2)}, u32[]{:S(2)}) async-start(bf16[64,1,16,256]{3,2,1,0:T(8,128)(2,1)} %get-tuple-element.31), calls=%async_computation.2 | async-start | bytes 1048576 | tf_op jit(solution)/shard_map/all_to_all | solution.py:266
  161.1 2.3 %fusion.4 = f32[80]{0:T(128)S(1)} fusion(f32[80,16,256]{2,1,0:T(8,128)} %param.6, bf16[80,16,256]{2,1,0:T(8,128)(2,1)S(1)} %get-tuple-element.19), kind=kLoop, calls=%fused_computation.6 | loop fusion | flops 2949040 | bytes 1966400 | tf_op jit(solution)/shard_map/reduce_sum | solution.py:262
  163.5 9.4 %all-reduce = (f32[3]{0:T(128)S(1)}, f32[80]{0:T(128)S(1)}) all-reduce(f32[3]{0:T(128)S(1)} %maximum_reduce_fusion, f32[80]{0:T(128)S(1)} %fusion.4), channel_id=1, replica_groups=mesh['fsdp'=64,'rep'=4] {'rep'}, use_global_device_ids=true, to_apply=%region_5.6 | all-reduce | flops 83 | bytes 664 | tf_op jit(solution)/shard_map/psum | solution.py:311
  173.0 5.4 %all-to-all-done.2.back2 = bf16[64,1,16,256]{3,2,1,0:T(8,128)(2,1)S(1)} async-done(((bf16[64,1,16,256]{3,2,1,0:T(8,128)(2,1)}), bf16[64,1,16,256]{3,2,1,0:T(8,128)(2,1)S(1)}, u32[]{:S(2)}, u32[]{:S(2)}) %all-to-all-start.2) | async-done | bytes 524320 | tf_op jit(solution)/shard_map/all_to_all | solution.py:266
  180.0 6.4 %all-to-all-start.3 = ((f32[64,1,128]{2,1,0:T(1,128)}), f32[64,1,128]{2,1,0:T(1,128)S(1)}, u32[]{:S(2)}, u32[]{:S(2)}) async-start(f32[64,1,128]{2,1,0:T(1,128)} %broadcast_in_dim.55), calls=%async_computation.3 | async-start | bytes 65536 | tf_op jit(solution)/shard_map/all_to_all | solution.py:266
  186.7 3.7 %collective-permute-start.27 = (bf16[20,16,256]{2,1,0:T(8,128)(2,1)S(1)}, bf16[20,16,256]{2,1,0:T(8,128)(2,1)S(1)}, u32[]{:S(2)}, u32[]{:S(2)}) collective-permute-start(bf16[20,16,256]{2,1,0:T(8,128)(2,1)S(1)} %get-tuple-element.49), channel_id=1, source_target_pairs={{0,2},{1,3},{2,0},{3,1},{4,6},{5,7},{6,4},{7,5},{8,10},{9,11},{10,... | collective-permute-start | bytes 491528 | tf_op jit(solution)/shard_map/ppermute | solution.py:29
  190.4 5.1 %all-to-all-done.3 = f32[64,1,128]{2,1,0:T(1,128)S(1)} async-done(((f32[64,1,128]{2,1,0:T(1,128)}), f32[64,1,128]{2,1,0:T(1,128)S(1)}, u32[]{:S(2)}, u32[]{:S(2)}) %all-to-all-start.3) | async-done | bytes 32800 | tf_op jit(solution)/shard_map/all_to_all | solution.py:266
  (95 shorter events, 39.4 us)
Async XLA Ops:
  1.4 8.5 %collective-permute-start.1 = (bf16[40,16,256]{2,1,0:T(8,128)(2,1)S(1)}, bf16[40,16,256]{2,1,0:T(8,128)(2,1)S(1)}, u32[]{:S(2)}, u32[]{:S(2)}) collective-permute-start(bf16[40,16,256]{2,1,0:T(8,128)(2,1)S(1)} %get-tuple-element.36), channel_id=1, source_target_pairs={{0,1},{1,2},{2,3},{3,0},{4,5},{5,6},{6,7},{7,4},{8,9},{9,10},{10,1... | collective-permute-start | bytes 983048 | tf_op jit(solution)/shard_map/ppermute | solution.py:29
  3.5 7.9 %collective-permute-start.4 = (bf16[40,16,256]{2,1,0:T(8,128)(2,1)S(1)}, bf16[40,16,256]{2,1,0:T(8,128)(2,1)S(1)}, u32[]{:S(2)}, u32[]{:S(2)}) collective-permute-start(bf16[40,16,256]{2,1,0:T(8,128)(2,1)S(1)} %get-tuple-element.38), channel_id=1, source_target_pairs={{0,3},{1,0},{2,1},{3,2},{4,7},{5,4},{6,5},{7,6},{8,11},{9,8},{10,9... | collective-permute-start | bytes 983048 | tf_op jit(solution)/shard_map/ppermute | solution.py:29
  4.9 13.6 %collective-permute-start = (bf16[40,16,256]{2,1,0:T(8,128)(2,1)S(1)}, bf16[40,16,256]{2,1,0:T(8,128)(2,1)S(1)}, u32[]{:S(2)}, u32[]{:S(2)}) collective-permute-start(bf16[40,16,256]{2,1,0:T(8,128)(2,1)S(1)} %get-tuple-element.37), channel_id=1, source_target_pairs={{0,3},{1,0},{2,1},{3,2},{4,7},{5,4},{6,5},{7,6},{8,11},{9,8},{10,9... | collective-permute-start | bytes 983048 | tf_op jit(solution)/shard_map/ppermute | solution.py:29
  6.2 12.2 %collective-permute-start.3 = (bf16[40,16,256]{2,1,0:T(8,128)(2,1)S(1)}, bf16[40,16,256]{2,1,0:T(8,128)(2,1)S(1)}, u32[]{:S(2)}, u32[]{:S(2)}) collective-permute-start(bf16[40,16,256]{2,1,0:T(8,128)(2,1)S(1)} %get-tuple-element.35), channel_id=1, source_target_pairs={{0,1},{1,2},{2,3},{3,0},{4,5},{5,6},{6,7},{7,4},{8,9},{9,10},{10,1... | collective-permute-start | bytes 983048 | tf_op jit(solution)/shard_map/ppermute | solution.py:29
  12.7 11.5 %collective-permute-start.2 = (bf16[40,16,256]{2,1,0:T(8,128)(2,1)S(1)}, bf16[40,16,256]{2,1,0:T(8,128)(2,1)S(1)}, u32[]{:S(2)}, u32[]{:S(2)}) collective-permute-start(bf16[40,16,256]{2,1,0:T(8,128)(2,1)S(1)} %get-tuple-element.40), channel_id=1, source_target_pairs={{0,1},{1,2},{2,3},{3,0},{4,5},{5,6},{6,7},{7,4},{8,9},{9,10},{10,1... | collective-permute-start | bytes 983048 | tf_op jit(solution)/shard_map/ppermute | solution.py:29
  14.3 11.1 %collective-permute-start.5 = (bf16[40,16,256]{2,1,0:T(8,128)(2,1)S(1)}, bf16[40,16,256]{2,1,0:T(8,128)(2,1)S(1)}, u32[]{:S(2)}, u32[]{:S(2)}) collective-permute-start(bf16[40,16,256]{2,1,0:T(8,128)(2,1)S(1)} %get-tuple-element.39), channel_id=1, source_target_pairs={{0,3},{1,0},{2,1},{3,2},{4,7},{5,4},{6,5},{7,6},{8,11},{9,8},{10,9... | collective-permute-start | bytes 983048 | tf_op jit(solution)/shard_map/ppermute | solution.py:29
  27.7 56.0 %all-to-all-start = ((bf16[64,3,16,256]{3,2,1,0:T(8,128)(2,1)}), bf16[64,3,16,256]{3,2,1,0:T(8,128)(2,1)S(1)}, u32[]{:S(2)}, u32[]{:S(2)}) async-start(bf16[64,3,16,256]{3,2,1,0:T(8,128)(2,1)} %get-tuple-element.23), calls=%async_computation | async-start | bytes 3145728 | tf_op jit(solution)/shard_map/all_to_all | solution.py:266
  43.9 13.5 %collective-permute-start.9 = (bf16[2,512,256]{2,1,0:T(8,128)(2,1)S(1)}, bf16[2,512,256]{2,1,0:T(8,128)(2,1)S(1)}, u32[]{:S(2)}, u32[]{:S(2)}) collective-permute-start(bf16[2,512,256]{2,1,0:T(8,128)(2,1)S(1)} %get-tuple-element.21), channel_id=1, source_target_pairs={{0,3},{1,0},{2,1},{3,2},{4,7},{5,4},{6,5},{7,6},{8,11},{9,8},{10,9... | collective-permute-start | bytes 1572872 | tf_op jit(solution)/shard_map/ppermute | solution.py:29
  46.6 14.3 %collective-permute-start.6 = (bf16[2,512,256]{2,1,0:T(8,128)(2,1)S(1)}, bf16[2,512,256]{2,1,0:T(8,128)(2,1)S(1)}, u32[]{:S(2)}, u32[]{:S(2)}) collective-permute-start(bf16[2,512,256]{2,1,0:T(8,128)(2,1)S(1)} %get-tuple-element.20), channel_id=1, source_target_pairs={{0,1},{1,2},{2,3},{3,0},{4,5},{5,6},{6,7},{7,4},{8,9},{9,10},{10,1... | collective-permute-start | bytes 1572872 | tf_op jit(solution)/shard_map/ppermute | solution.py:29
  46.6 22.1 %collective-permute-start.11 = (bf16[2,512,256]{2,1,0:T(8,128)(2,1)S(1)}, bf16[2,512,256]{2,1,0:T(8,128)(2,1)S(1)}, u32[]{:S(2)}, u32[]{:S(2)}) collective-permute-start(bf16[2,512,256]{2,1,0:T(8,128)(2,1)S(1)} %get-tuple-element.20), channel_id=1, source_target_pairs={{0,3},{1,0},{2,1},{3,2},{4,7},{5,4},{6,5},{7,6},{8,11},{9,8},{10,9... | collective-permute-start | bytes 1572872 | tf_op jit(solution)/shard_map/ppermute | solution.py:29
  49.2 22.5 %collective-permute-start.7 = (bf16[2,512,256]{2,1,0:T(8,128)(2,1)S(1)}, bf16[2,512,256]{2,1,0:T(8,128)(2,1)S(1)}, u32[]{:S(2)}, u32[]{:S(2)}) collective-permute-start(bf16[2,512,256]{2,1,0:T(8,128)(2,1)S(1)} %get-tuple-element.21), channel_id=1, source_target_pairs={{0,1},{1,2},{2,3},{3,0},{4,5},{5,6},{6,7},{7,4},{8,9},{9,10},{10,1... | collective-permute-start | bytes 1572872 | tf_op jit(solution)/shard_map/ppermute | solution.py:29
  57.4 22.5 %collective-permute-start.10 = (bf16[2,512,256]{2,1,0:T(8,128)(2,1)S(1)}, bf16[2,512,256]{2,1,0:T(8,128)(2,1)S(1)}, u32[]{:S(2)}, u32[]{:S(2)}) collective-permute-start(bf16[2,512,256]{2,1,0:T(8,128)(2,1)S(1)} %collective-permute-done.9.refs_10_), channel_id=1, source_target_pairs={{0,3},{1,0},{2,1},{3,2},{4,7},{5,4},{6,5},{7,6},{8,11},{9,8},{10,9... | collective-permute-start | bytes 1572872 | tf_op jit(solution)/shard_map/ppermute | solution.py:29
  60.8 22.1 %collective-permute-start.8 = (bf16[2,512,256]{2,1,0:T(8,128)(2,1)S(1)}, bf16[2,512,256]{2,1,0:T(8,128)(2,1)S(1)}, u32[]{:S(2)}, u32[]{:S(2)}) collective-permute-start(bf16[2,512,256]{2,1,0:T(8,128)(2,1)S(1)} %collective-permute-done.6.refs_5_), channel_id=1, source_target_pairs={{0,1},{1,2},{2,3},{3,0},{4,5},{5,6},{6,7},{7,4},{8,9},{9,10},{10,1... | collective-permute-start | bytes 1572872 | tf_op jit(solution)/shard_map/ppermute | solution.py:29
  87.6 10.6 %collective-permute-start.13 = (bf16[1,256,256]{2,1,0:T(8,128)(2,1)S(1)}, bf16[1,256,256]{2,1,0:T(8,128)(2,1)S(1)}, u32[]{:S(2)}, u32[]{:S(2)}) collective-permute-start(bf16[1,256,256]{2,1,0:T(8,128)(2,1)S(1)} %get-tuple-element.45), channel_id=1, source_target_pairs={{0,2},{1,3},{2,0},{3,1},{4,6},{5,7},{6,4},{7,5},{8,10},{9,11},{10,... | collective-permute-start | bytes 393224 | tf_op jit(solution)/shard_map/ppermute | solution.py:29
  88.0 6.7 %collective-permute-start.14 = (bf16[1,256,256]{2,1,0:T(8,128)(2,1)S(1)}, bf16[1,256,256]{2,1,0:T(8,128)(2,1)S(1)}, u32[]{:S(2)}, u32[]{:S(2)}) collective-permute-start(bf16[1,256,256]{2,1,0:T(8,128)(2,1)S(1)} %get-tuple-element.44), channel_id=1, source_target_pairs={{0,3},{1,0},{2,1},{3,2},{4,7},{5,4},{6,5},{7,6},{8,11},{9,8},{10,9... | collective-permute-start | bytes 393224 | tf_op jit(solution)/shard_map/ppermute | solution.py:29
  89.5 13.8 %collective-permute-start.12 = (bf16[2,256,256]{2,1,0:T(8,128)(2,1)S(1)}, bf16[2,256,256]{2,1,0:T(8,128)(2,1)S(1)}, u32[]{:S(2)}, u32[]{:S(2)}) collective-permute-start(bf16[2,256,256]{2,1,0:T(8,128)(2,1)S(1)} %get-tuple-element.42), channel_id=1, source_target_pairs={{0,1},{1,2},{2,3},{3,0},{4,5},{5,6},{6,7},{7,4},{8,9},{9,10},{10,1... | collective-permute-start | bytes 786440 | tf_op jit(solution)/shard_map/ppermute | solution.py:29
  89.7 13.5 %collective-permute-start.16 = (bf16[2,256,256]{2,1,0:T(8,128)(2,1)S(1)}, bf16[2,256,256]{2,1,0:T(8,128)(2,1)S(1)}, u32[]{:S(2)}, u32[]{:S(2)}) collective-permute-start(bf16[2,256,256]{2,1,0:T(8,128)(2,1)S(1)} %get-tuple-element.41), channel_id=1, source_target_pairs={{0,3},{1,0},{2,1},{3,2},{4,7},{5,4},{6,5},{7,6},{8,11},{9,8},{10,9... | collective-permute-start | bytes 786440 | tf_op jit(solution)/shard_map/ppermute | solution.py:29
  94.6 8.6 %collective-permute-start.15 = (bf16[1,256,256]{2,1,0:T(8,128)(2,1)S(1)}, bf16[1,256,256]{2,1,0:T(8,128)(2,1)S(1)}, u32[]{:S(2)}, u32[]{:S(2)}) collective-permute-start(bf16[1,256,256]{2,1,0:T(8,128)(2,1)S(1)} %collective-permute-done.14), channel_id=1, source_target_pairs={{0,3},{1,0},{2,1},{3,2},{4,7},{5,4},{6,5},{7,6},{8,11},{9,8},{10,9... | collective-permute-start | bytes 393224 | tf_op jit(solution)/shard_map/ppermute | solution.py:29
  107.7 40.8 %all-to-all-start.1 = ((bf16[64,2,16,256]{3,2,1,0:T(8,128)(2,1)}), bf16[64,2,16,256]{3,2,1,0:T(8,128)(2,1)S(1)}, u32[]{:S(2)}, u32[]{:S(2)}) async-start(bf16[64,2,16,256]{3,2,1,0:T(8,128)(2,1)} %copy-done), calls=%async_computation.1 | async-start | bytes 2097152 | tf_op jit(solution)/shard_map/all_to_all | solution.py:266
  120.9 12.7 %collective-permute-start.20 = (bf16[1,512,256]{2,1,0:T(8,128)(2,1)S(1)}, bf16[1,512,256]{2,1,0:T(8,128)(2,1)S(1)}, u32[]{:S(2)}, u32[]{:S(2)}) collective-permute-start(bf16[1,512,256]{2,1,0:T(8,128)(2,1)S(1)} %get-tuple-element.26), channel_id=1, source_target_pairs={{0,1},{1,2},{2,3},{3,0},{4,5},{5,6},{6,7},{7,4},{8,9},{9,10},{10,1... | collective-permute-start | bytes 786440 | tf_op jit(solution)/shard_map/ppermute | solution.py:29
  121.4 12.2 %collective-permute-start.23 = (bf16[1,512,256]{2,1,0:T(8,128)(2,1)S(1)}, bf16[1,512,256]{2,1,0:T(8,128)(2,1)S(1)}, u32[]{:S(2)}, u32[]{:S(2)}) collective-permute-start(bf16[1,512,256]{2,1,0:T(8,128)(2,1)S(1)} %get-tuple-element.27), channel_id=1, source_target_pairs={{0,3},{1,0},{2,1},{3,2},{4,7},{5,4},{6,5},{7,6},{8,11},{9,8},{10,9... | collective-permute-start | bytes 786440 | tf_op jit(solution)/shard_map/ppermute | solution.py:29
  126.5 9.8 %collective-permute-start.18 = (bf16[1,256,256]{2,1,0:T(8,128)(2,1)S(1)}, bf16[1,256,256]{2,1,0:T(8,128)(2,1)S(1)}, u32[]{:S(2)}, u32[]{:S(2)}) collective-permute-start(bf16[1,256,256]{2,1,0:T(8,128)(2,1)S(1)} %get-tuple-element.55), channel_id=1, source_target_pairs={{0,2},{1,3},{2,0},{3,1},{4,6},{5,7},{6,4},{7,5},{8,10},{9,11},{10,... | collective-permute-start | bytes 393224 | tf_op jit(solution)/shard_map/ppermute | solution.py:29
  128.8 16.6 %collective-permute-start.21 = (bf16[1,512,256]{2,1,0:T(8,128)(2,1)S(1)}, bf16[1,512,256]{2,1,0:T(8,128)(2,1)S(1)}, u32[]{:S(2)}, u32[]{:S(2)}) collective-permute-start(bf16[1,512,256]{2,1,0:T(8,128)(2,1)S(1)} %get-tuple-element.27), channel_id=1, source_target_pairs={{0,1},{1,2},{2,3},{3,0},{4,5},{5,6},{6,7},{7,4},{8,9},{9,10},{10,1... | collective-permute-start | bytes 786440 | tf_op jit(solution)/shard_map/ppermute | solution.py:29
  132.0 13.5 %collective-permute-start.25 = (bf16[1,512,256]{2,1,0:T(8,128)(2,1)S(1)}, bf16[1,512,256]{2,1,0:T(8,128)(2,1)S(1)}, u32[]{:S(2)}, u32[]{:S(2)}) collective-permute-start(bf16[1,512,256]{2,1,0:T(8,128)(2,1)S(1)} %get-tuple-element.26), channel_id=1, source_target_pairs={{0,3},{1,0},{2,1},{3,2},{4,7},{5,4},{6,5},{7,6},{8,11},{9,8},{10,9... | collective-permute-start | bytes 786440 | tf_op jit(solution)/shard_map/ppermute | solution.py:29
  133.6 13.0 %collective-permute-start.22 = (bf16[1,512,256]{2,1,0:T(8,128)(2,1)S(1)}, bf16[1,512,256]{2,1,0:T(8,128)(2,1)S(1)}, u32[]{:S(2)}, u32[]{:S(2)}) collective-permute-start(bf16[1,512,256]{2,1,0:T(8,128)(2,1)S(1)} %collective-permute-done.20.refs_5_), channel_id=1, source_target_pairs={{0,1},{1,2},{2,3},{3,0},{4,5},{5,6},{6,7},{7,4},{8,9},{9,10},{10,1... | collective-permute-start | bytes 786440 | tf_op jit(solution)/shard_map/ppermute | solution.py:29
  133.6 13.0 %collective-permute-start.24 = (bf16[1,512,256]{2,1,0:T(8,128)(2,1)S(1)}, bf16[1,512,256]{2,1,0:T(8,128)(2,1)S(1)}, u32[]{:S(2)}, u32[]{:S(2)}) collective-permute-start(bf16[1,512,256]{2,1,0:T(8,128)(2,1)S(1)} %collective-permute-done.23.refs_10_), channel_id=1, source_target_pairs={{0,3},{1,0},{2,1},{3,2},{4,7},{5,4},{6,5},{7,6},{8,11},{9,8},{10,9... | collective-permute-start | bytes 786440 | tf_op jit(solution)/shard_map/ppermute | solution.py:29
  136.3 9.1 %collective-permute-start.19 = (bf16[1,256,256]{2,1,0:T(8,128)(2,1)S(1)}, bf16[1,256,256]{2,1,0:T(8,128)(2,1)S(1)}, u32[]{:S(2)}, u32[]{:S(2)}) collective-permute-start(bf16[1,256,256]{2,1,0:T(8,128)(2,1)S(1)} %get-tuple-element.54), channel_id=1, source_target_pairs={{0,3},{1,0},{2,1},{3,2},{4,7},{5,4},{6,5},{7,6},{8,11},{9,8},{10,9... | collective-permute-start | bytes 393224 | tf_op jit(solution)/shard_map/ppermute | solution.py:29
  148.5 29.9 %all-to-all-start.2 = ((bf16[64,1,16,256]{3,2,1,0:T(8,128)(2,1)}), bf16[64,1,16,256]{3,2,1,0:T(8,128)(2,1)S(1)}, u32[]{:S(2)}, u32[]{:S(2)}) async-start(bf16[64,1,16,256]{3,2,1,0:T(8,128)(2,1)} %get-tuple-element.31), calls=%async_computation.2 | async-start | bytes 1048576 | tf_op jit(solution)/shard_map/all_to_all | solution.py:266
  180.0 15.6 %all-to-all-start.3 = ((f32[64,1,128]{2,1,0:T(1,128)}), f32[64,1,128]{2,1,0:T(1,128)S(1)}, u32[]{:S(2)}, u32[]{:S(2)}) async-start(f32[64,1,128]{2,1,0:T(1,128)} %broadcast_in_dim.55), calls=%async_computation.3 | async-start | bytes 65536 | tf_op jit(solution)/shard_map/all_to_all | solution.py:266
  186.4 9.6 %collective-permute-start.26 = (bf16[20,16,256]{2,1,0:T(8,128)(2,1)S(1)}, bf16[20,16,256]{2,1,0:T(8,128)(2,1)S(1)}, u32[]{:S(2)}, u32[]{:S(2)}) collective-permute-start(bf16[20,16,256]{2,1,0:T(8,128)(2,1)S(1)} %get-tuple-element.50), channel_id=1, source_target_pairs={{0,1},{1,2},{2,3},{3,0},{4,5},{5,6},{6,7},{7,4},{8,9},{9,10},{10,1... | collective-permute-start | bytes 491528 | tf_op jit(solution)/shard_map/ppermute | solution.py:29
  186.7 11.1 %collective-permute-start.27 = (bf16[20,16,256]{2,1,0:T(8,128)(2,1)S(1)}, bf16[20,16,256]{2,1,0:T(8,128)(2,1)S(1)}, u32[]{:S(2)}, u32[]{:S(2)}) collective-permute-start(bf16[20,16,256]{2,1,0:T(8,128)(2,1)S(1)} %get-tuple-element.49), channel_id=1, source_target_pairs={{0,2},{1,3},{2,0},{3,1},{4,6},{5,7},{6,4},{7,5},{8,10},{9,11},{10,... | collective-permute-start | bytes 491528 | tf_op jit(solution)/shard_map/ppermute | solution.py:29
  190.4 7.4 %collective-permute-start.28 = (bf16[20,16,256]{2,1,0:T(8,128)(2,1)S(1)}, bf16[20,16,256]{2,1,0:T(8,128)(2,1)S(1)}, u32[]{:S(2)}, u32[]{:S(2)}) collective-permute-start(bf16[20,16,256]{2,1,0:T(8,128)(2,1)S(1)} %get-tuple-element.48), channel_id=1, source_target_pairs={{0,3},{1,0},{2,1},{3,2},{4,7},{5,4},{6,5},{7,6},{8,11},{9,8},{10,9... | collective-permute-start | bytes 491528 | tf_op jit(solution)/shard_map/ppermute | solution.py:29
  (14 other events, 96.4 us)

commit v5 on v4

--- a/solution.py
+++ b/solution.py
@@ -196,36 +196,32 @@
     )(place, *pieces, *rights)
 
 
-def split_kernel(owner, slot, back01, back2, out, held):
+def split_kernel(owner, slot, back, out):
     _, groups, rows, _ = out.shape
     part = rows // REP
-
-    held[:, :2] = back01[...]
-    held[:, 2] = back2[:, 0]
 
     @pl.loop(0, groups, unroll=2)
     def _(g):
         parts = []
         for i in range(REP):
             b = g * REP + i
-            parts.append(wide(held[owner[b], slot[b]]))
+            parts.append(wide(back[owner[b], slot[b]]))
         for k in range(REP):
             joined = [p[k * part : (k + 1) * part] for p in parts]
             out[(REP - k) % REP, g] = jnp.concatenate(joined, axis=0).astype(jnp.bfloat16)
 
 
-def split_blocks(owner, slot, back01, back2):
+def split_blocks(owner, slot, back):
     blocks = owner.shape[0]
-    _, _, rows, width = back01.shape
+    _, _, rows, width = back.shape
     return pl.pallas_call(
         split_kernel,
         out_shape=jax.ShapeDtypeStruct((REP, blocks // REP, rows, width), jnp.bfloat16),
-        in_specs=[SMEM] * 2 + [VMEM] * 2,
+        in_specs=[SMEM] * 2 + [VMEM],
         out_specs=VMEM,
-        scratch_shapes=[pltpu.VMEM((OWNERS, CAP, rows, width), jnp.bfloat16)],
         compiler_params=pltpu.CompilerParams(vmem_limit_bytes=ROOM),
         name="split_blocks",
-    )(owner, slot, back01, back2)
+    )(owner, slot, back)
 
 
 def join_kernel(place, ratio, own, first, second, third, out, held):
@@ -288,7 +284,7 @@
         for k in range(REP)
     ]
     terms, passing = sum_over_rep(pieces)
-    rights01 = gather_over_rep(right_root[0, :2], *passing)
+    rights = gather_over_rep(right_root[0], *passing)
     low, packed = sum_pack(source, terms)
     owned = exchange(packed)
     adam = lax.psum(adam_squares(low, moment), "rep")
@@ -296,22 +292,13 @@
     def spread(sent):
         return [sent[0]] + [shift(sent[k], k) for k in (1, 2, 3)]
 
-    sent01 = left_multiply(after(place_ref, *rights01), owned, left_root[0], 0, 2)
-    across = shift(sent01[2][:1], 2)
-    back_once = shift(sent01[2][1:], 3)
-    held01 = [sent01[0], shift(sent01[1], 1), None, shift(sent01[3], 3)]
-    held01[2] = jnp.concatenate([across, shift(back_once, 3)])
-    result01, square01 = right_multiply(place_ref, held01, rights01)
-    back01 = exchange(result01)
-    rights2 = gather_over_rep(right_root[0, 2:], *held01)
-    sent2 = left_multiply(after(place_ref, *held01), owned, left_root[0], 2, 1)
-    held2 = spread(sent2)
-    result2, square2 = right_multiply(place_ref, held2, rights2)
-    back2 = exchange(after(result2, back01))
-    squares = lax.psum(jnp.sum(jnp.concatenate([square01, square2]), axis=(1, 2)), "rep")
+    held = spread(left_multiply(place_ref, owned, left_root[0], 0, CAP))
+    result, square = right_multiply(place_ref, held, rights)
+    back = exchange(result)
+    squares = lax.psum(jnp.sum(square, axis=(1, 2)), "rep")
     known = jnp.concatenate([adam, squares, jnp.zeros((128 - blocks - CAP,), jnp.float32)])
     known = jnp.broadcast_to(known[None, None, :], (OWNERS, 1, 128))
-    sent = split_blocks(owner, slot, back01, back2)
+    sent = split_blocks(owner, slot, back)
     known = exchange(after(known, sent))[:, 0]
     adam_norm = jnp.sqrt(jnp.sum(known[:, :blocks], axis=0))
     by_place = jnp.transpose(known[:, blocks : blocks + CAP]).reshape(OWNERS * CAP, 1)

time: 200 us -> 197 us (0.985)
  waiting for transfers between devices: 72.7 us -> 112 us
  starting transfers between devices: 84.3 us -> 50.8 us
  local copies, waits for them, and re-layouts: 11.9 us -> 5.68 us
    all_to_all x4 -> x3, waiting for transfers between devices: 10.5 us -> 50.8 us  [exchange(): return lax.all_to_all(value, 'fsdp', split_axis=0, concat_axis=0)]
    ppermute x29 -> x18, starting transfers between devices: 39.3 us -> 19.7 us  [shift(): lax.ppermute(value, 'rep', [(i, (i + step) % REP) for i in range(REP)])]
    all_to_all x4 -> x3, starting transfers between devices: 45 us -> 31.2 us  [exchange(): return lax.all_to_all(value, 'fsdp', split_axis=0, concat_axis=0)]
    unnamed x27 -> x14, local copies, waits for them, and re-layouts: 5.88 us -> 0.86 us
    squeeze x3 -> x0, local copies, waits for them, and re-layouts: 2.43 us -> none  [the longest x1 1.3 us: shards(): rights01 = gather_over_rep(right_root[0, :2], *passing)]
    ppermute x29 -> x18, waiting for transfers between devices: 62.2 us -> 61 us  [shift(): lax.ppermute(value, 'rep', [(i, (i + step) % REP) for i in range(REP)])]
    pallas_call x2 -> x1, Pallas kernels: 6.44 us -> 5.38 us  [left_multiply(): pl.pallas_call(lambda *refs: left_kernel(first, *refs), grid=(count,), ou...]
    pallas_call x2 -> x1, Pallas kernels: 5.27 us -> 5.96 us  [right_multiply(): pl.pallas_call(right_kernel, grid=(count,), out_shape=[jax.ShapeDtypeStru...]
  transfers between devices with their start and end apart: 33 -> 21, of which waited for: 18 -> 12; matrix products, arithmetic and copies ran while one was open for 4% -> 3% of each run, Pallas kernels for 2% -> 3%
where the time goes in v5:
time: 197 us
  waiting for transfers between devices  112 us (57%)
  starting transfers between devices  50.8 us (26%)
  Pallas kernels  16.3 us (8%)
  blocking collectives  9.23 us (5%)
  local copies, waits for them, and re-layouts  5.68 us (3%)
  other arithmetic  2.97 us (2%)
    ppermute x18, waiting for transfers between devices, shift(): lax.ppermute(value, 'rep', [(i, (i + step) % REP) for i in range(REP)])  61 us
    all_to_all x3, waiting for transfers between devices, exchange(): return lax.all_to_all(value, 'fsdp', split_axis=0, concat_axis=0)  50.8 us
    all_to_all x3, starting transfers between devices, exchange(): return lax.all_to_all(value, 'fsdp', split_axis=0, concat_axis=0)  31.2 us
    ppermute x18, starting transfers between devices, shift(): lax.ppermute(value, 'rep', [(i, (i + step) % REP) for i in range(REP)])  19.7 us
    psum x1, blocking collectives, shards(): squares = lax.psum(jnp.sum(square, axis=(1, 2)), 'rep')  9.23 us
    pallas_call x1, Pallas kernels, right_multiply(): pl.pallas_call(right_kernel, grid=(count,), out_shape=[jax.ShapeDtypeStru...  5.96 us
    pallas_call x1, Pallas kernels, left_multiply(): pl.pallas_call(lambda *refs: left_kernel(first, *refs), grid=(count,), ou...  5.38 us
  transfers between devices with their start and end apart: 21, of which 12 were waited for; matrix products, arithmetic and copies ran while one was open for 3% of the time, Pallas kernels for 3%

profile of v5, /device:TPU:1, one launch (start us, length us, event | category | flops | bytes accessed | tf_op | source)
XLA Modules:
  0.0 196.9 jit_solution(6892992485767732303)
XLA Ops:
  0.0 1.4 dynamic-slice_bitcast_fusion.1
  1.4 3.4 %collective-permute-start.4 = (bf16[40,16,256]{2,1,0:T(8,128)(2,1)S(1)}, bf16[40,16,256]{2,1,0:T(8,128)(2,1)S(1)}, u32[]{:S(2)}, u32[]{:S(2)}) collective-permute-start(bf16[40,16,256]{2,1,0:T(8,128)(2,1)S(1)} %get-tuple-element.23), channel_id=1, source_target_pairs={{0,3},{1,0},{2,1},{3,2},{4,7},{5,4},{6,5},{7,6},{8,11},{9,8},{10,9... | collective-permute-start | bytes 983048 | tf_op jit(solution)/shard_map/ppermute | solution.py:29
  4.8 2.7 %collective-permute-start = (bf16[40,16,256]{2,1,0:T(8,128)(2,1)S(1)}, bf16[40,16,256]{2,1,0:T(8,128)(2,1)S(1)}, u32[]{:S(2)}, u32[]{:S(2)}) collective-permute-start(bf16[40,16,256]{2,1,0:T(8,128)(2,1)S(1)} %get-tuple-element.25), channel_id=1, source_target_pairs={{0,3},{1,0},{2,1},{3,2},{4,7},{5,4},{6,5},{7,6},{8,11},{9,8},{10,9... | collective-permute-start | bytes 983048 | tf_op jit(solution)/shard_map/ppermute | solution.py:29
  7.6 3.5 %collective-permute-done.4 = bf16[40,16,256]{2,1,0:T(8,128)(2,1)S(1)} collective-permute-done((bf16[40,16,256]{2,1,0:T(8,128)(2,1)S(1)}, bf16[40,16,256]{2,1,0:T(8,128)(2,1)S(1)}, u32[]{:S(2)}, u32[]{:S(2)}) %collective-permute-start.4) | collective-permute-done | bytes 327712 | tf_op jit(solution)/shard_map/ppermute | solution.py:29
  11.2 3.1 %collective-permute-done.1 = bf16[40,16,256]{2,1,0:T(8,128)(2,1)S(1)} collective-permute-done((bf16[40,16,256]{2,1,0:T(8,128)(2,1)S(1)}, bf16[40,16,256]{2,1,0:T(8,128)(2,1)S(1)}, u32[]{:S(2)}, u32[]{:S(2)}) %collective-permute-start.1) | collective-permute-done | bytes 327712 | tf_op jit(solution)/shard_map/ppermute | solution.py:29
  14.2 1.3 fusion.5
  15.9 1.1 collective-permute-start.2
  17.2 1.1 dynamic-slice_bitcast_fusion.own
  18.3 2.9 %collective-permute-done.3.near_right = bf16[40,16,256]{2,1,0:T(8,128)(2,1)S(1)} collective-permute-done((bf16[40,16,256]{2,1,0:T(8,128)(2,1)S(1)}, bf16[40,16,256]{2,1,0:T(8,128)(2,1)S(1)}, u32[]{:S(2)}, u32[]{:S(2)}) %collective-permute-start.3) | collective-permute-done | bytes 327712 | tf_op jit(solution)/shard_map/ppermute | solution.py:29
  21.3 3.9 %collective-permute-done.5.last_left = bf16[40,16,256]{2,1,0:T(8,128)(2,1)S(1)} collective-permute-done((bf16[40,16,256]{2,1,0:T(8,128)(2,1)S(1)}, bf16[40,16,256]{2,1,0:T(8,128)(2,1)S(1)}, u32[]{:S(2)}, u32[]{:S(2)}) %collective-permute-start.5) | collective-permute-done | bytes 327712 | tf_op jit(solution)/shard_map/ppermute | solution.py:29
  25.2 3.1 %collective-permute-done.2.last_right = bf16[40,16,256]{2,1,0:T(8,128)(2,1)S(1)} collective-permute-done((bf16[40,16,256]{2,1,0:T(8,128)(2,1)S(1)}, bf16[40,16,256]{2,1,0:T(8,128)(2,1)S(1)}, u32[]{:S(2)}, u32[]{:S(2)}) %collective-permute-start.2) | collective-permute-done | bytes 327712 | tf_op jit(solution)/shard_map/ppermute | solution.py:29
  28.3 2.3 %sum_pack.1 = (bf16[80,16,256]{2,1,0:T(8,128)(2,1)S(1)}, bf16[64,3,16,256]{3,2,1,0:T(8,128)(2,1)}) custom-call(s32[192]{0:T(256)S(1)} %select_reduce_fusion.1.source, bf16[80,16,256]{2,1,0:T(8,128)(2,1)S(1)} %dynamic-slice_bitcast_fusion.own, bf16[40,16,256]{2,1,0:T(8,128)(2,1)S(1)} %collective-permute-done.near_left, ...), custom_call_target="tpu_custom_call" | custom-call | tf_op jit(solution)/shard_map/sum_pack/pallas_call | solution.py:79
  31.4 13.6 %all-to-all-start = ((bf16[64,3,16,256]{3,2,1,0:T(8,128)(2,1)}), bf16[64,3,16,256]{3,2,1,0:T(8,128)(2,1)S(1)}, u32[]{:S(2)}, u32[]{:S(2)}) async-start(bf16[64,3,16,256]{3,2,1,0:T(8,128)(2,1)} %get-tuple-element.13), calls=%async_computation | async-start | bytes 3145728 | tf_op jit(solution)/shard_map/all_to_all | solution.py:262
  45.1 1.3 fusion.8
  46.3 2.7 %collective-permute-start.12 = (bf16[3,512,256]{2,1,0:T(8,128)(2,1)}, bf16[3,512,256]{2,1,0:T(8,128)(2,1)}, u32[]{:S(2)}, u32[]{:S(2)}) collective-permute-start(bf16[3,512,256]{2,1,0:T(8,128)(2,1)} %get-tuple-element.15), channel_id=1, source_target_pairs={{0,3},{1,0},{2,1},{3,2},{4,7},{5,4},{6,5},{7,6},{8,11},{9,8},{10,9... | collective-permute-start | bytes 2359304 | tf_op jit(solution)/shard_map/ppermute | solution.py:29
  49.1 1.4 collective-permute-start.10
  50.5 15.9 %collective-permute-done.9.refs_5_ = bf16[3,512,256]{2,1,0:T(8,128)(2,1)S(1)} collective-permute-done((bf16[3,512,256]{2,1,0:T(8,128)(2,1)}, bf16[3,512,256]{2,1,0:T(8,128)(2,1)S(1)}, u32[]{:S(2)}, u32[]{:S(2)}) %collective-permute-start.9) | collective-permute-done | bytes 786464 | tf_op jit(solution)/shard_map/ppermute | solution.py:29
  66.4 2.7 %collective-permute-start.13 = (bf16[3,512,256]{2,1,0:T(8,128)(2,1)}, bf16[3,512,256]{2,1,0:T(8,128)(2,1)}, u32[]{:S(2)}, u32[]{:S(2)}) collective-permute-start(bf16[3,512,256]{2,1,0:T(8,128)(2,1)} %collective-permute-done.12.refs_10_), channel_id=1, source_target_pairs={{0,3},{1,0},{2,1},{3,2},{4,7},{5,4},{6,5},{7,6},{8,11},{9,8},{10,9... | collective-permute-start | bytes 2359304 | tf_op jit(solution)/shard_map/ppermute | solution.py:29
  69.1 15.7 %all-to-all-done.refs_1_ = bf16[64,3,16,256]{3,2,1,0:T(8,128)(2,1)S(1)} async-done(((bf16[64,3,16,256]{3,2,1,0:T(8,128)(2,1)}), bf16[64,3,16,256]{3,2,1,0:T(8,128)(2,1)S(1)}, u32[]{:S(2)}, u32[]{:S(2)}) %all-to-all-start) | async-done | bytes 1572896 | tf_op jit(solution)/shard_map/all_to_all | solution.py:262
  84.8 5.4 %left_multiply.1 = bf16[4,3,256,256]{3,2,1,0:T(8,128)(2,1)S(1)} custom-call(s32[1]{0:T(128)} %bitcast.refs_0_.place, bf16[64,3,16,256]{3,2,1,0:T(8,128)(2,1)S(1)} %all-to-all-done.refs_1_, bf16[3,1024,1024]{2,1,0:T(8,128)(2,1)} %bitcast.42), custom_call_target="tpu_custom_call" | custom-call | flops 1610612736 | bytes 12582912 | tf_op jit(solution)/shard_map/left_multiply/pallas_call | solution.py:116
  92.2 16.1 %collective-permute-done.11.refs_7_ = bf16[3,512,256]{2,1,0:T(8,128)(2,1)} collective-permute-done((bf16[3,512,256]{2,1,0:T(8,128)(2,1)S(1)}, bf16[3,512,256]{2,1,0:T(8,128)(2,1)}, u32[]{:S(2)}, u32[]{:S(2)}) %collective-permute-start.11) | collective-permute-done | bytes 786464 | tf_op jit(solution)/shard_map/ppermute | solution.py:29
  108.3 8.7 %collective-permute-done.6.refs_1_ = bf16[3,256,256]{2,1,0:T(8,128)(2,1)S(1)} collective-permute-done((bf16[3,256,256]{2,1,0:T(8,128)(2,1)S(1)}, bf16[3,256,256]{2,1,0:T(8,128)(2,1)S(1)}, u32[]{:S(2)}, u32[]{:S(2)}) %collective-permute-start.6) | collective-permute-done | bytes 393248 | tf_op jit(solution)/shard_map/ppermute | solution.py:29
  117.0 6.0 %right_multiply.1 = (bf16[64,3,16,256]{3,2,1,0:T(8,128)(2,1)}, f32[3,1,256]{2,1,0:T(1,128)S(1)}) custom-call(s32[1]{0:T(128)} %bitcast.refs_0_.place, bf16[3,256,256]{2,1,0:T(8,128)(2,1)S(1)} %get-tuple-element.32.refs_0_, bf16[3,256,256]{2,1,0:T(8,128)(2,1)S(1)} %collective-permute-done.6.refs_1_, bf16[3,256,256]{2,1,0:T(8,128)(2,1)S(1)} %collective-permute-done.7.refs_2_, ...), custom_call_target="tpu_custom_call" | custom-call | flops 1610612736 | bytes 12582912 | tf_op jit(solution)/shard_map/right_multiply/pallas_call | solution.py:171
  123.0 11.4 %all-to-all-start.1 = ((bf16[64,3,16,256]{3,2,1,0:T(8,128)(2,1)}), bf16[64,3,16,256]{3,2,1,0:T(8,128)(2,1)S(1)}, u32[]{:S(2)}, u32[]{:S(2)}) async-start(bf16[64,3,16,256]{3,2,1,0:T(8,128)(2,1)} %get-tuple-element.17), calls=%async_computation.1 | async-start | bytes 3145728 | tf_op jit(solution)/shard_map/all_to_all | solution.py:262
  134.4 1.0 fusion.4
  135.5 9.2 %all-reduce = (f32[3]{0:T(128)S(1)}, f32[80]{0:T(128)S(1)}) all-reduce(f32[3]{0:T(128)S(1)} %reduce_sum.57, f32[80]{0:T(128)S(1)} %fusion.4), channel_id=1, replica_groups=mesh['fsdp'=64,'rep'=4] {'rep'}, use_global_device_ids=true, to_apply=%region_5.6 | all-reduce | flops 83 | bytes 664 | tf_op jit(solution)/shard_map/psum | solution.py:298
  144.8 29.3 %all-to-all-done.1.back = bf16[64,3,16,256]{3,2,1,0:T(8,128)(2,1)S(1)} async-done(((bf16[64,3,16,256]{3,2,1,0:T(8,128)(2,1)}), bf16[64,3,16,256]{3,2,1,0:T(8,128)(2,1)S(1)}, u32[]{:S(2)}, u32[]{:S(2)}) %all-to-all-start.1) | async-done | bytes 1572896 | tf_op jit(solution)/shard_map/all_to_all | solution.py:262
  175.6 6.1 %all-to-all-start.2 = ((f32[64,1,128]{2,1,0:T(1,128)}), f32[64,1,128]{2,1,0:T(1,128)S(1)}, u32[]{:S(2)}, u32[]{:S(2)}) async-start(f32[64,1,128]{2,1,0:T(1,128)} %broadcast_in_dim.55), calls=%async_computation.2 | async-start | bytes 65536 | tf_op jit(solution)/shard_map/all_to_all | solution.py:262
  181.8 2.8 %collective-permute-start.17 = (bf16[20,16,256]{2,1,0:T(8,128)(2,1)S(1)}, bf16[20,16,256]{2,1,0:T(8,128)(2,1)S(1)}, u32[]{:S(2)}, u32[]{:S(2)}) collective-permute-start(bf16[20,16,256]{2,1,0:T(8,128)(2,1)S(1)} %get-tuple-element.33), channel_id=1, source_target_pairs={{0,3},{1,0},{2,1},{3,2},{4,7},{5,4},{6,5},{7,6},{8,11},{9,8},{10,9... | collective-permute-start | bytes 491528 | tf_op jit(solution)/shard_map/ppermute | solution.py:29
  185.2 5.7 %all-to-all-done.2 = f32[64,1,128]{2,1,0:T(1,128)S(1)} async-done(((f32[64,1,128]{2,1,0:T(1,128)}), f32[64,1,128]{2,1,0:T(1,128)S(1)}, u32[]{:S(2)}, u32[]{:S(2)}) %all-to-all-start.2) | async-done | bytes 32800 | tf_op jit(solution)/shard_map/all_to_all | solution.py:262
  191.4 3.6 %collective-permute-done.15.first = bf16[20,16,256]{2,1,0:T(8,128)(2,1)S(1)} collective-permute-done((bf16[20,16,256]{2,1,0:T(8,128)(2,1)S(1)}, bf16[20,16,256]{2,1,0:T(8,128)(2,1)S(1)}, u32[]{:S(2)}, u32[]{:S(2)}) %collective-permute-start.15) | collective-permute-done | bytes 163872 | tf_op jit(solution)/shard_map/ppermute | solution.py:29
  195.1 1.9 join_blocks.1
  (50 shorter events, 6.3 us)
Async XLA Ops:
  0.0 7.5 %copy-start.2 = (s32[80]{0:T(128)S(1)}, s32[80]{0:T(128)}, u32[]{:S(2)}) copy-start(s32[80]{0:T(128)} %owner.1) | copy-start | bytes 964
  1.4 9.8 %collective-permute-start.4 = (bf16[40,16,256]{2,1,0:T(8,128)(2,1)S(1)}, bf16[40,16,256]{2,1,0:T(8,128)(2,1)S(1)}, u32[]{:S(2)}, u32[]{:S(2)}) collective-permute-start(bf16[40,16,256]{2,1,0:T(8,128)(2,1)S(1)} %get-tuple-element.23), channel_id=1, source_target_pairs={{0,3},{1,0},{2,1},{3,2},{4,7},{5,4},{6,5},{7,6},{8,11},{9,8},{10,9... | collective-permute-start | bytes 983048 | tf_op jit(solution)/shard_map/ppermute | solution.py:29
  4.8 9.5 %collective-permute-start.1 = (bf16[40,16,256]{2,1,0:T(8,128)(2,1)S(1)}, bf16[40,16,256]{2,1,0:T(8,128)(2,1)S(1)}, u32[]{:S(2)}, u32[]{:S(2)}) collective-permute-start(bf16[40,16,256]{2,1,0:T(8,128)(2,1)S(1)} %get-tuple-element.24), channel_id=1, source_target_pairs={{0,1},{1,2},{2,3},{3,0},{4,5},{5,6},{6,7},{7,4},{8,9},{9,10},{10,1... | collective-permute-start | bytes 983048 | tf_op jit(solution)/shard_map/ppermute | solution.py:29
  4.8 13.5 %collective-permute-start = (bf16[40,16,256]{2,1,0:T(8,128)(2,1)S(1)}, bf16[40,16,256]{2,1,0:T(8,128)(2,1)S(1)}, u32[]{:S(2)}, u32[]{:S(2)}) collective-permute-start(bf16[40,16,256]{2,1,0:T(8,128)(2,1)S(1)} %get-tuple-element.25), channel_id=1, source_target_pairs={{0,3},{1,0},{2,1},{3,2},{4,7},{5,4},{6,5},{7,6},{8,11},{9,8},{10,9... | collective-permute-start | bytes 983048 | tf_op jit(solution)/shard_map/ppermute | solution.py:29
  7.5 13.8 %collective-permute-start.3 = (bf16[40,16,256]{2,1,0:T(8,128)(2,1)S(1)}, bf16[40,16,256]{2,1,0:T(8,128)(2,1)S(1)}, u32[]{:S(2)}, u32[]{:S(2)}) collective-permute-start(bf16[40,16,256]{2,1,0:T(8,128)(2,1)S(1)} %get-tuple-element.26), channel_id=1, source_target_pairs={{0,1},{1,2},{2,3},{3,0},{4,5},{5,6},{6,7},{7,4},{8,9},{9,10},{10,1... | collective-permute-start | bytes 983048 | tf_op jit(solution)/shard_map/ppermute | solution.py:29
  15.5 9.7 %collective-permute-start.5 = (bf16[40,16,256]{2,1,0:T(8,128)(2,1)S(1)}, bf16[40,16,256]{2,1,0:T(8,128)(2,1)S(1)}, u32[]{:S(2)}, u32[]{:S(2)}) collective-permute-start(bf16[40,16,256]{2,1,0:T(8,128)(2,1)S(1)} %get-tuple-element.21), channel_id=1, source_target_pairs={{0,3},{1,0},{2,1},{3,2},{4,7},{5,4},{6,5},{7,6},{8,11},{9,8},{10,9... | collective-permute-start | bytes 983048 | tf_op jit(solution)/shard_map/ppermute | solution.py:29
  15.9 12.4 %collective-permute-start.2 = (bf16[40,16,256]{2,1,0:T(8,128)(2,1)S(1)}, bf16[40,16,256]{2,1,0:T(8,128)(2,1)S(1)}, u32[]{:S(2)}, u32[]{:S(2)}) collective-permute-start(bf16[40,16,256]{2,1,0:T(8,128)(2,1)S(1)} %get-tuple-element.22), channel_id=1, source_target_pairs={{0,1},{1,2},{2,3},{3,0},{4,5},{5,6},{6,7},{7,4},{8,9},{9,10},{10,1... | collective-permute-start | bytes 983048 | tf_op jit(solution)/shard_map/ppermute | solution.py:29
  17.1 13.5 %copy-start.5 = (s32[80]{0:T(128)}, s32[80]{0:T(128)S(1)}, u32[]{:S(2)}) copy-start(s32[80]{0:T(128)S(1)} %multiply_add_fusion) | copy-start | bytes 964
  30.5 0.8 copy-start
  31.4 13.7 %copy-start.3 = (bf16[1,3,1024,256]{3,2,1,0:T(8,128)(2,1)S(1)}, bf16[1,3,1024,256]{3,2,1,0:T(8,128)(2,1)}, u32[]{:S(2)}) copy-start(bf16[1,3,1024,256]{3,2,1,0:T(8,128)(2,1)} %param.9) | copy-start | bytes 4718596
  31.4 53.4 %all-to-all-start = ((bf16[64,3,16,256]{3,2,1,0:T(8,128)(2,1)}), bf16[64,3,16,256]{3,2,1,0:T(8,128)(2,1)S(1)}, u32[]{:S(2)}, u32[]{:S(2)}) async-start(bf16[64,3,16,256]{3,2,1,0:T(8,128)(2,1)} %get-tuple-element.13), calls=%async_computation | async-start | bytes 3145728 | tf_op jit(solution)/shard_map/all_to_all | solution.py:262
  46.3 20.1 %collective-permute-start.9 = (bf16[3,512,256]{2,1,0:T(8,128)(2,1)}, bf16[3,512,256]{2,1,0:T(8,128)(2,1)S(1)}, u32[]{:S(2)}, u32[]{:S(2)}) collective-permute-start(bf16[3,512,256]{2,1,0:T(8,128)(2,1)} %get-tuple-element.14), channel_id=1, source_target_pairs={{0,1},{1,2},{2,3},{3,0},{4,5},{5,6},{6,7},{7,4},{8,9},{9,10},{10,1... | collective-permute-start | bytes 2359304 | tf_op jit(solution)/shard_map/ppermute | solution.py:29
  46.3 20.1 %collective-permute-start.12 = (bf16[3,512,256]{2,1,0:T(8,128)(2,1)}, bf16[3,512,256]{2,1,0:T(8,128)(2,1)}, u32[]{:S(2)}, u32[]{:S(2)}) collective-permute-start(bf16[3,512,256]{2,1,0:T(8,128)(2,1)} %get-tuple-element.15), channel_id=1, source_target_pairs={{0,3},{1,0},{2,1},{3,2},{4,7},{5,4},{6,5},{7,6},{8,11},{9,8},{10,9... | collective-permute-start | bytes 2359304 | tf_op jit(solution)/shard_map/ppermute | solution.py:29
  49.0 41.6 %collective-permute-start.14 = (bf16[3,512,256]{2,1,0:T(8,128)(2,1)}, bf16[3,512,256]{2,1,0:T(8,128)(2,1)S(1)}, u32[]{:S(2)}, u32[]{:S(2)}) collective-permute-start(bf16[3,512,256]{2,1,0:T(8,128)(2,1)} %get-tuple-element.14), channel_id=1, source_target_pairs={{0,3},{1,0},{2,1},{3,2},{4,7},{5,4},{6,5},{7,6},{8,11},{9,8},{10,9... | collective-permute-start | bytes 2359304 | tf_op jit(solution)/shard_map/ppermute | solution.py:29
  49.1 42.1 %collective-permute-start.10 = (bf16[3,512,256]{2,1,0:T(8,128)(2,1)}, bf16[3,512,256]{2,1,0:T(8,128)(2,1)}, u32[]{:S(2)}, u32[]{:S(2)}) collective-permute-start(bf16[3,512,256]{2,1,0:T(8,128)(2,1)} %get-tuple-element.15), channel_id=1, source_target_pairs={{0,1},{1,2},{2,3},{3,0},{4,5},{5,6},{6,7},{7,4},{8,9},{9,10},{10,1... | collective-permute-start | bytes 2359304 | tf_op jit(solution)/shard_map/ppermute | solution.py:29
  66.4 41.9 %collective-permute-start.11 = (bf16[3,512,256]{2,1,0:T(8,128)(2,1)S(1)}, bf16[3,512,256]{2,1,0:T(8,128)(2,1)}, u32[]{:S(2)}, u32[]{:S(2)}) collective-permute-start(bf16[3,512,256]{2,1,0:T(8,128)(2,1)S(1)} %collective-permute-done.9.refs_5_), channel_id=1, source_target_pairs={{0,1},{1,2},{2,3},{3,0},{4,5},{5,6},{6,7},{7,4},{8,9},{9,10},{10,1... | collective-permute-start | bytes 2359304 | tf_op jit(solution)/shard_map/ppermute | solution.py:29
  66.4 41.9 %collective-permute-start.13 = (bf16[3,512,256]{2,1,0:T(8,128)(2,1)}, bf16[3,512,256]{2,1,0:T(8,128)(2,1)}, u32[]{:S(2)}, u32[]{:S(2)}) collective-permute-start(bf16[3,512,256]{2,1,0:T(8,128)(2,1)} %collective-permute-done.12.refs_10_), channel_id=1, source_target_pairs={{0,3},{1,0},{2,1},{3,2},{4,7},{5,4},{6,5},{7,6},{8,11},{9,8},{10,9... | collective-permute-start | bytes 2359304 | tf_op jit(solution)/shard_map/ppermute | solution.py:29
  90.3 18.0 %collective-permute-start.8 = (bf16[3,256,256]{2,1,0:T(8,128)(2,1)S(1)}, bf16[3,256,256]{2,1,0:T(8,128)(2,1)S(1)}, u32[]{:S(2)}, u32[]{:S(2)}) collective-permute-start(bf16[3,256,256]{2,1,0:T(8,128)(2,1)S(1)} %get-tuple-element.29), channel_id=1, source_target_pairs={{0,3},{1,0},{2,1},{3,2},{4,7},{5,4},{6,5},{7,6},{8,11},{9,8},{10,9... | collective-permute-start | bytes 1179656 | tf_op jit(solution)/shard_map/ppermute | solution.py:29
  90.6 17.7 %collective-permute-start.7 = (bf16[3,256,256]{2,1,0:T(8,128)(2,1)S(1)}, bf16[3,256,256]{2,1,0:T(8,128)(2,1)S(1)}, u32[]{:S(2)}, u32[]{:S(2)}) collective-permute-start(bf16[3,256,256]{2,1,0:T(8,128)(2,1)S(1)} %get-tuple-element.30), channel_id=1, source_target_pairs={{0,2},{1,3},{2,0},{3,1},{4,6},{5,7},{6,4},{7,5},{8,10},{9,11},{10,... | collective-permute-start | bytes 1179656 | tf_op jit(solution)/shard_map/ppermute | solution.py:29
  91.2 25.8 %collective-permute-start.6 = (bf16[3,256,256]{2,1,0:T(8,128)(2,1)S(1)}, bf16[3,256,256]{2,1,0:T(8,128)(2,1)S(1)}, u32[]{:S(2)}, u32[]{:S(2)}) collective-permute-start(bf16[3,256,256]{2,1,0:T(8,128)(2,1)S(1)} %get-tuple-element.31), channel_id=1, source_target_pairs={{0,1},{1,2},{2,3},{3,0},{4,5},{5,6},{6,7},{7,4},{8,9},{9,10},{10,1... | collective-permute-start | bytes 1179656 | tf_op jit(solution)/shard_map/ppermute | solution.py:29
  122.9 11.4 %copy-start.1 = (bf16[80,16,256]{2,1,0:T(8,128)(2,1)S(1)}, bf16[80,16,256]{2,1,0:T(8,128)(2,1)}, u32[]{:S(2)}) copy-start(bf16[80,16,256]{2,1,0:T(8,128)(2,1)} %copy-done) | copy-start | bytes 1966084
  123.0 11.4 %copy-start.4 = (f32[80,16,256]{2,1,0:T(8,128)S(1)}, f32[80,16,256]{2,1,0:T(8,128)}, u32[]{:S(2)}) copy-start(f32[80,16,256]{2,1,0:T(8,128)} %param.6) | copy-start | bytes 3932164
  123.0 51.2 %all-to-all-start.1 = ((bf16[64,3,16,256]{3,2,1,0:T(8,128)(2,1)}), bf16[64,3,16,256]{3,2,1,0:T(8,128)(2,1)S(1)}, u32[]{:S(2)}, u32[]{:S(2)}) async-start(bf16[64,3,16,256]{3,2,1,0:T(8,128)(2,1)} %get-tuple-element.17), calls=%async_computation.1 | async-start | bytes 3145728 | tf_op jit(solution)/shard_map/all_to_all | solution.py:262
  174.9 16.2 %copy-start.6 = (s32[80]{0:T(128)S(1)}, s32[80]{0:T(128)}, u32[]{:S(2)}) copy-start(s32[80]{0:T(128)} %copy-done.5) | copy-start | bytes 964
  175.6 15.3 %all-to-all-start.2 = ((f32[64,1,128]{2,1,0:T(1,128)}), f32[64,1,128]{2,1,0:T(1,128)S(1)}, u32[]{:S(2)}, u32[]{:S(2)}) async-start(f32[64,1,128]{2,1,0:T(1,128)} %broadcast_in_dim.55), calls=%async_computation.2 | async-start | bytes 65536 | tf_op jit(solution)/shard_map/all_to_all | solution.py:262
  181.8 9.6 %collective-permute-start.17 = (bf16[20,16,256]{2,1,0:T(8,128)(2,1)S(1)}, bf16[20,16,256]{2,1,0:T(8,128)(2,1)S(1)}, u32[]{:S(2)}, u32[]{:S(2)}) collective-permute-start(bf16[20,16,256]{2,1,0:T(8,128)(2,1)S(1)} %get-tuple-element.33), channel_id=1, source_target_pairs={{0,3},{1,0},{2,1},{3,2},{4,7},{5,4},{6,5},{7,6},{8,11},{9,8},{10,9... | collective-permute-start | bytes 491528 | tf_op jit(solution)/shard_map/ppermute | solution.py:29
  184.5 6.9 %collective-permute-start.16 = (bf16[20,16,256]{2,1,0:T(8,128)(2,1)S(1)}, bf16[20,16,256]{2,1,0:T(8,128)(2,1)S(1)}, u32[]{:S(2)}, u32[]{:S(2)}) collective-permute-start(bf16[20,16,256]{2,1,0:T(8,128)(2,1)S(1)} %get-tuple-element.34), channel_id=1, source_target_pairs={{0,2},{1,3},{2,0},{3,1},{4,6},{5,7},{6,4},{7,5},{8,10},{9,11},{10,... | collective-permute-start | bytes 491528 | tf_op jit(solution)/shard_map/ppermute | solution.py:29
  184.5 10.5 %collective-permute-start.15 = (bf16[20,16,256]{2,1,0:T(8,128)(2,1)S(1)}, bf16[20,16,256]{2,1,0:T(8,128)(2,1)S(1)}, u32[]{:S(2)}, u32[]{:S(2)}) collective-permute-start(bf16[20,16,256]{2,1,0:T(8,128)(2,1)S(1)} %get-tuple-element.35), channel_id=1, source_target_pairs={{0,1},{1,2},{2,3},{3,0},{4,5},{5,6},{6,7},{7,4},{8,9},{9,10},{10,1... | collective-permute-start | bytes 491528 | tf_op jit(solution)/shard_map/ppermute | solution.py:29

commit v6 on v5

--- a/solution.py
+++ b/solution.py
@@ -131,16 +131,19 @@
 
 
 def right_kernel(place, *refs):
-    pieces, rights = refs[:REP], refs[REP : REP + 7]
-    out, total, full, wide_rows = refs[REP + 7 :]
+    pieces, rights = refs[: REP + 1], refs[REP + 1 : REP + 8]
+    out, total, full, wide_rows = refs[REP + 8 :]
     height, size = full.shape
     width = size // REP
     halves, _, half = wide_rows.shape
     rows = out.shape[2]
     part = rows // REP
-    for k, piece in enumerate(pieces):
+    first_row = 0
+    for k, piece in zip((0, 1, 2, 2, 3), pieces):
         at = pl.multiple_of(lax.rem(place[0] + (REP - k), REP) * width, width)
-        full[:, pl.ds(at, width)] = piece[0]
+        last_row = first_row + piece.shape[1]
+        full[first_row:last_row, pl.ds(at, width)] = piece[0]
+        first_row = last_row % height
     squares = jnp.zeros((8, width), jnp.float32)
     middle = size // 2
     for k in range(REP):
@@ -176,7 +179,7 @@
             jax.ShapeDtypeStruct((count, 1, width), jnp.float32),
         ],
         in_specs=[SMEM]
-        + [pl.BlockSpec((1, height, width), lambda i: (i, 0, 0))] * 4
+        + [pl.BlockSpec((1,) + p.shape[1:], lambda i: (i, 0, 0)) for p in pieces]
         + [pl.BlockSpec((1,) + r.shape[1:], lambda i: (i, 0, 0)) for r in rights],
         out_specs=[
             pl.BlockSpec((OWNERS, 1, rows, width), lambda i: (0, i, 0, 0)),
@@ -292,7 +295,12 @@
     def spread(sent):
         return [sent[0]] + [shift(sent[k], k) for k in (1, 2, 3)]
 
-    held = spread(left_multiply(place_ref, owned, left_root[0], 0, CAP))
+    sent = left_multiply(place_ref, owned, left_root[0], 0, CAP)
+    middle = sent.shape[2] // 2
+    passed_right = shift(sent[2, :, :middle], 1)
+    passed_left = shift(sent[2, :, middle:], 3)
+    held = [sent[0], shift(sent[1], 1), None, None, shift(sent[3], 3)]
+    held[2], held[3] = shift(passed_right, 1), shift(passed_left, 3)
     result, square = right_multiply(place_ref, held, rights)
     back = exchange(result)
     squares = lax.psum(jnp.sum(square, axis=(1, 2)), "rep")

time: 197 us -> 197 us (level)
  waiting for transfers between devices: 112 us -> 106 us
  starting transfers between devices: 50.8 us -> 56.2 us
    ppermute x18 -> x21, waiting for transfers between devices: 61 us -> 55.6 us  [shift(): lax.ppermute(value, 'rep', [(i, (i + step) % REP) for i in range(REP)])]
    ppermute x18 -> x21, starting transfers between devices: 19.7 us -> 24.3 us  [shift(): lax.ppermute(value, 'rep', [(i, (i + step) % REP) for i in range(REP)])]
  transfers between devices with their start and end apart: 21 -> 24, of which waited for: 12 -> 14; matrix products, arithmetic and copies ran while one was open for 3% -> 3% of each run, Pallas kernels for 3% -> 3%
where the time goes in v6:
time: 197 us
  waiting for transfers between devices  106 us (54%)
  starting transfers between devices  56.2 us (29%)
  Pallas kernels  16.3 us (8%)
  blocking collectives  9.23 us (5%)
  local copies, waits for them, and re-layouts  5.67 us (3%)
  other arithmetic  2.97 us (2%)
    ppermute x21, waiting for transfers between devices, shift(): lax.ppermute(value, 'rep', [(i, (i + step) % REP) for i in range(REP)])  55.6 us
    all_to_all x3, waiting for transfers between devices, exchange(): return lax.all_to_all(value, 'fsdp', split_axis=0, concat_axis=0)  50.8 us
    all_to_all x3, starting transfers between devices, exchange(): return lax.all_to_all(value, 'fsdp', split_axis=0, concat_axis=0)  31.9 us
    ppermute x21, starting transfers between devices, shift(): lax.ppermute(value, 'rep', [(i, (i + step) % REP) for i in range(REP)])  24.3 us
    psum x1, blocking collectives, shards(): squares = lax.psum(jnp.sum(square, axis=(1, 2)), 'rep')  9.23 us
    pallas_call x1, Pallas kernels, right_multiply(): pl.pallas_call(right_kernel, grid=(count,), out_shape=[jax.ShapeDtypeStru...  5.93 us
    pallas_call x1, Pallas kernels, left_multiply(): pl.pallas_call(lambda *refs: left_kernel(first, *refs), grid=(count,), ou...  5.4 us
  transfers between devices with their start and end apart: 24, of which 14 were waited for; matrix products, arithmetic and copies ran while one was open for 3% of the time, Pallas kernels for 3%

profile of v6, /device:TPU:1, one launch (start us, length us, event | category | flops | bytes accessed | tf_op | source)
XLA Modules:
  0.0 196.9 jit_solution(13783867217499783881)
XLA Ops:
  0.0 1.4 dynamic-slice_bitcast_fusion.1
  1.4 3.4 %collective-permute-start.4 = (bf16[40,16,256]{2,1,0:T(8,128)(2,1)S(1)}, bf16[40,16,256]{2,1,0:T(8,128)(2,1)S(1)}, u32[]{:S(2)}, u32[]{:S(2)}) collective-permute-start(bf16[40,16,256]{2,1,0:T(8,128)(2,1)S(1)} %get-tuple-element.23), channel_id=1, source_target_pairs={{0,3},{1,0},{2,1},{3,2},{4,7},{5,4},{6,5},{7,6},{8,11},{9,8},{10,9... | collective-permute-start | bytes 983048 | tf_op jit(solution)/shard_map/ppermute | solution.py:29
  4.8 2.7 %collective-permute-start = (bf16[40,16,256]{2,1,0:T(8,128)(2,1)S(1)}, bf16[40,16,256]{2,1,0:T(8,128)(2,1)S(1)}, u32[]{:S(2)}, u32[]{:S(2)}) collective-permute-start(bf16[40,16,256]{2,1,0:T(8,128)(2,1)S(1)} %get-tuple-element.25), channel_id=1, source_target_pairs={{0,3},{1,0},{2,1},{3,2},{4,7},{5,4},{6,5},{7,6},{8,11},{9,8},{10,9... | collective-permute-start | bytes 983048 | tf_op jit(solution)/shard_map/ppermute | solution.py:29
  7.6 3.5 %collective-permute-done.4 = bf16[40,16,256]{2,1,0:T(8,128)(2,1)S(1)} collective-permute-done((bf16[40,16,256]{2,1,0:T(8,128)(2,1)S(1)}, bf16[40,16,256]{2,1,0:T(8,128)(2,1)S(1)}, u32[]{:S(2)}, u32[]{:S(2)}) %collective-permute-start.4) | collective-permute-done | bytes 327712 | tf_op jit(solution)/shard_map/ppermute | solution.py:29
  11.2 3.1 %collective-permute-done.1 = bf16[40,16,256]{2,1,0:T(8,128)(2,1)S(1)} collective-permute-done((bf16[40,16,256]{2,1,0:T(8,128)(2,1)S(1)}, bf16[40,16,256]{2,1,0:T(8,128)(2,1)S(1)}, u32[]{:S(2)}, u32[]{:S(2)}) %collective-permute-start.1) | collective-permute-done | bytes 327712 | tf_op jit(solution)/shard_map/ppermute | solution.py:29
  14.2 1.3 fusion.5
  18.3 2.9 %collective-permute-done.3.near_right = bf16[40,16,256]{2,1,0:T(8,128)(2,1)S(1)} collective-permute-done((bf16[40,16,256]{2,1,0:T(8,128)(2,1)S(1)}, bf16[40,16,256]{2,1,0:T(8,128)(2,1)S(1)}, u32[]{:S(2)}, u32[]{:S(2)}) %collective-permute-start.3) | collective-permute-done | bytes 327712 | tf_op jit(solution)/shard_map/ppermute | solution.py:29
  21.3 3.9 %collective-permute-done.5.last_left = bf16[40,16,256]{2,1,0:T(8,128)(2,1)S(1)} collective-permute-done((bf16[40,16,256]{2,1,0:T(8,128)(2,1)S(1)}, bf16[40,16,256]{2,1,0:T(8,128)(2,1)S(1)}, u32[]{:S(2)}, u32[]{:S(2)}) %collective-permute-start.5) | collective-permute-done | bytes 327712 | tf_op jit(solution)/shard_map/ppermute | solution.py:29
  25.2 3.1 %collective-permute-done.2.last_right = bf16[40,16,256]{2,1,0:T(8,128)(2,1)S(1)} collective-permute-done((bf16[40,16,256]{2,1,0:T(8,128)(2,1)S(1)}, bf16[40,16,256]{2,1,0:T(8,128)(2,1)S(1)}, u32[]{:S(2)}, u32[]{:S(2)}) %collective-permute-start.2) | collective-permute-done | bytes 327712 | tf_op jit(solution)/shard_map/ppermute | solution.py:29
  28.3 2.2 %sum_pack.1 = (bf16[80,16,256]{2,1,0:T(8,128)(2,1)S(1)}, bf16[64,3,16,256]{3,2,1,0:T(8,128)(2,1)}) custom-call(s32[192]{0:T(256)S(1)} %select_reduce_fusion.1.source, bf16[80,16,256]{2,1,0:T(8,128)(2,1)S(1)} %dynamic-slice_bitcast_fusion.own, bf16[40,16,256]{2,1,0:T(8,128)(2,1)S(1)} %collective-permute-done.near_left, ...), custom_call_target="tpu_custom_call" | custom-call | tf_op jit(solution)/shard_map/sum_pack/pallas_call | solution.py:79
  31.4 13.6 %all-to-all-start = ((bf16[64,3,16,256]{3,2,1,0:T(8,128)(2,1)}), bf16[64,3,16,256]{3,2,1,0:T(8,128)(2,1)S(1)}, u32[]{:S(2)}, u32[]{:S(2)}) async-start(bf16[64,3,16,256]{3,2,1,0:T(8,128)(2,1)} %get-tuple-element.13), calls=%async_computation | async-start | bytes 3145728 | tf_op jit(solution)/shard_map/all_to_all | solution.py:265
  45.1 1.3 fusion.8
  46.3 2.7 %collective-permute-start.15 = (bf16[3,512,256]{2,1,0:T(8,128)(2,1)}, bf16[3,512,256]{2,1,0:T(8,128)(2,1)}, u32[]{:S(2)}, u32[]{:S(2)}) collective-permute-start(bf16[3,512,256]{2,1,0:T(8,128)(2,1)} %get-tuple-element.15), channel_id=1, source_target_pairs={{0,3},{1,0},{2,1},{3,2},{4,7},{5,4},{6,5},{7,6},{8,11},{9,8},{10,9... | collective-permute-start | bytes 2359304 | tf_op jit(solution)/shard_map/ppermute | solution.py:29
  49.0 1.4 collective-permute-start.13
  50.5 15.9 %collective-permute-done.12.refs_6_ = bf16[3,512,256]{2,1,0:T(8,128)(2,1)S(1)} collective-permute-done((bf16[3,512,256]{2,1,0:T(8,128)(2,1)}, bf16[3,512,256]{2,1,0:T(8,128)(2,1)S(1)}, u32[]{:S(2)}, u32[]{:S(2)}) %collective-permute-start.12) | collective-permute-done | bytes 786464 | tf_op jit(solution)/shard_map/ppermute | solution.py:29
  66.4 2.7 %collective-permute-start.16 = (bf16[3,512,256]{2,1,0:T(8,128)(2,1)}, bf16[3,512,256]{2,1,0:T(8,128)(2,1)}, u32[]{:S(2)}, u32[]{:S(2)}) collective-permute-start(bf16[3,512,256]{2,1,0:T(8,128)(2,1)} %collective-permute-done.15.refs_11_), channel_id=1, source_target_pairs={{0,3},{1,0},{2,1},{3,2},{4,7},{5,4},{6,5},{7,6},{8,11},{9,8},{10,9... | collective-permute-start | bytes 2359304 | tf_op jit(solution)/shard_map/ppermute | solution.py:29
  69.1 15.8 %all-to-all-done.refs_1_ = bf16[64,3,16,256]{3,2,1,0:T(8,128)(2,1)S(1)} async-done(((bf16[64,3,16,256]{3,2,1,0:T(8,128)(2,1)}), bf16[64,3,16,256]{3,2,1,0:T(8,128)(2,1)S(1)}, u32[]{:S(2)}, u32[]{:S(2)}) %all-to-all-start) | async-done | bytes 1572896 | tf_op jit(solution)/shard_map/all_to_all | solution.py:265
  84.8 5.4 %left_multiply.1 = bf16[4,3,256,256]{3,2,1,0:T(8,128)(2,1)S(1)} custom-call(s32[1]{0:T(128)} %bitcast.refs_0_.place, bf16[64,3,16,256]{3,2,1,0:T(8,128)(2,1)S(1)} %all-to-all-done.refs_1_, bf16[3,1024,1024]{2,1,0:T(8,128)(2,1)} %bitcast.44), custom_call_target="tpu_custom_call" | custom-call | flops 1610612736 | bytes 12582912 | tf_op jit(solution)/shard_map/left_multiply/pallas_call | solution.py:116
  90.7 1.5 collective-permute-start.7
  93.4 6.8 %collective-permute-done.14.refs_8_ = bf16[3,512,256]{2,1,0:T(8,128)(2,1)} collective-permute-done((bf16[3,512,256]{2,1,0:T(8,128)(2,1)S(1)}, bf16[3,512,256]{2,1,0:T(8,128)(2,1)}, u32[]{:S(2)}, u32[]{:S(2)}) %collective-permute-start.14) | collective-permute-done | bytes 786464 | tf_op jit(solution)/shard_map/ppermute | solution.py:29
  100.2 3.0 %collective-permute-done.9 = bf16[3,128,256]{2,1,0:T(8,128)(2,1)S(1)} collective-permute-done((bf16[3,128,256]{2,1,0:T(8,128)(2,1)S(1)}, bf16[3,128,256]{2,1,0:T(8,128)(2,1)S(1)}, u32[]{:S(2)}, u32[]{:S(2)}) %collective-permute-start.9) | collective-permute-done | bytes 196640 | tf_op jit(solution)/shard_map/ppermute | solution.py:29
  103.3 3.4 %collective-permute-start.10 = (bf16[3,128,256]{2,1,0:T(8,128)(2,1)S(1)}, bf16[3,128,256]{2,1,0:T(8,128)(2,1)S(1)}, u32[]{:S(2)}, u32[]{:S(2)}) collective-permute-start(bf16[3,128,256]{2,1,0:T(8,128)(2,1)S(1)} %collective-permute-done.9), channel_id=1, source_target_pairs={{0,3},{1,0},{2,1},{3,2},{4,7},{5,4},{6,5},{7,6},{8,11},{9,8},{10,9... | collective-permute-start | bytes 589832 | tf_op jit(solution)/shard_map/ppermute | solution.py:29
  106.7 9.2 %collective-permute-done.10.refs_3_ = bf16[3,128,256]{2,1,0:T(8,128)(2,1)S(1)} collective-permute-done((bf16[3,128,256]{2,1,0:T(8,128)(2,1)S(1)}, bf16[3,128,256]{2,1,0:T(8,128)(2,1)S(1)}, u32[]{:S(2)}, u32[]{:S(2)}) %collective-permute-start.10) | collective-permute-done | bytes 196640 | tf_op jit(solution)/shard_map/ppermute | solution.py:29
  116.2 5.9 %right_multiply.1 = (bf16[64,3,16,256]{3,2,1,0:T(8,128)(2,1)}, f32[3,1,256]{2,1,0:T(1,128)S(1)}) custom-call(s32[1]{0:T(128)} %bitcast.refs_0_.place, bf16[3,256,256]{2,1,0:T(8,128)(2,1)S(1)} %get-tuple-element.31.refs_0_, bf16[3,256,256]{2,1,0:T(8,128)(2,1)S(1)} %collective-permute-done.6.refs_1_, bf16[3,128,256]{2,1,0:T(8,128)(2,1)S(1)} %collective-permute-done.8.refs_2_, ...), custom_call_target="tpu_custom_call" | custom-call | flops 1610612736 | bytes 12582912 | tf_op jit(solution)/shard_map/right_multiply/pallas_call | solution.py:174
  122.2 12.1 %all-to-all-start.1 = ((bf16[64,3,16,256]{3,2,1,0:T(8,128)(2,1)}), bf16[64,3,16,256]{3,2,1,0:T(8,128)(2,1)S(1)}, u32[]{:S(2)}, u32[]{:S(2)}) async-start(bf16[64,3,16,256]{3,2,1,0:T(8,128)(2,1)} %get-tuple-element.17), calls=%async_computation.1 | async-start | bytes 3145728 | tf_op jit(solution)/shard_map/all_to_all | solution.py:265
  135.4 9.2 %all-reduce = (f32[3]{0:T(128)S(1)}, f32[80]{0:T(128)S(1)}) all-reduce(f32[3]{0:T(128)S(1)} %reduce_sum.57, f32[80]{0:T(128)S(1)} %fusion.4), channel_id=1, replica_groups=mesh['fsdp'=64,'rep'=4] {'rep'}, use_global_device_ids=true, to_apply=%region_5.6 | all-reduce | flops 83 | bytes 664 | tf_op jit(solution)/shard_map/psum | solution.py:306
  144.8 29.3 %all-to-all-done.1.back = bf16[64,3,16,256]{3,2,1,0:T(8,128)(2,1)S(1)} async-done(((bf16[64,3,16,256]{3,2,1,0:T(8,128)(2,1)}), bf16[64,3,16,256]{3,2,1,0:T(8,128)(2,1)S(1)}, u32[]{:S(2)}, u32[]{:S(2)}) %all-to-all-start.1) | async-done | bytes 1572896 | tf_op jit(solution)/shard_map/all_to_all | solution.py:265
  175.5 6.1 %all-to-all-start.2 = ((f32[64,1,128]{2,1,0:T(1,128)}), f32[64,1,128]{2,1,0:T(1,128)S(1)}, u32[]{:S(2)}, u32[]{:S(2)}) async-start(f32[64,1,128]{2,1,0:T(1,128)} %broadcast_in_dim.55), calls=%async_computation.2 | async-start | bytes 65536 | tf_op jit(solution)/shard_map/all_to_all | solution.py:265
  181.7 2.8 %collective-permute-start.20 = (bf16[20,16,256]{2,1,0:T(8,128)(2,1)S(1)}, bf16[20,16,256]{2,1,0:T(8,128)(2,1)S(1)}, u32[]{:S(2)}, u32[]{:S(2)}) collective-permute-start(bf16[20,16,256]{2,1,0:T(8,128)(2,1)S(1)} %get-tuple-element.34), channel_id=1, source_target_pairs={{0,3},{1,0},{2,1},{3,2},{4,7},{5,4},{6,5},{7,6},{8,11},{9,8},{10,9... | collective-permute-start | bytes 491528 | tf_op jit(solution)/shard_map/ppermute | solution.py:29
  185.2 5.7 %all-to-all-done.2 = f32[64,1,128]{2,1,0:T(1,128)S(1)} async-done(((f32[64,1,128]{2,1,0:T(1,128)}), f32[64,1,128]{2,1,0:T(1,128)S(1)}, u32[]{:S(2)}, u32[]{:S(2)}) %all-to-all-start.2) | async-done | bytes 32800 | tf_op jit(solution)/shard_map/all_to_all | solution.py:265
  191.4 3.6 %collective-permute-done.18.first = bf16[20,16,256]{2,1,0:T(8,128)(2,1)S(1)} collective-permute-done((bf16[20,16,256]{2,1,0:T(8,128)(2,1)S(1)}, bf16[20,16,256]{2,1,0:T(8,128)(2,1)S(1)}, u32[]{:S(2)}, u32[]{:S(2)}) %collective-permute-start.18) | collective-permute-done | bytes 163872 | tf_op jit(solution)/shard_map/ppermute | solution.py:29
  195.0 1.9 join_blocks.1
  (57 shorter events, 9.6 us)
Async XLA Ops:
  0.0 7.5 %copy-start.2 = (s32[80]{0:T(128)S(1)}, s32[80]{0:T(128)}, u32[]{:S(2)}) copy-start(s32[80]{0:T(128)} %owner.1) | copy-start | bytes 964
  1.4 9.8 %collective-permute-start.4 = (bf16[40,16,256]{2,1,0:T(8,128)(2,1)S(1)}, bf16[40,16,256]{2,1,0:T(8,128)(2,1)S(1)}, u32[]{:S(2)}, u32[]{:S(2)}) collective-permute-start(bf16[40,16,256]{2,1,0:T(8,128)(2,1)S(1)} %get-tuple-element.23), channel_id=1, source_target_pairs={{0,3},{1,0},{2,1},{3,2},{4,7},{5,4},{6,5},{7,6},{8,11},{9,8},{10,9... | collective-permute-start | bytes 983048 | tf_op jit(solution)/shard_map/ppermute | solution.py:29
  4.8 9.5 %collective-permute-start.1 = (bf16[40,16,256]{2,1,0:T(8,128)(2,1)S(1)}, bf16[40,16,256]{2,1,0:T(8,128)(2,1)S(1)}, u32[]{:S(2)}, u32[]{:S(2)}) collective-permute-start(bf16[40,16,256]{2,1,0:T(8,128)(2,1)S(1)} %get-tuple-element.24), channel_id=1, source_target_pairs={{0,1},{1,2},{2,3},{3,0},{4,5},{5,6},{6,7},{7,4},{8,9},{9,10},{10,1... | collective-permute-start | bytes 983048 | tf_op jit(solution)/shard_map/ppermute | solution.py:29
  4.8 13.5 %collective-permute-start = (bf16[40,16,256]{2,1,0:T(8,128)(2,1)S(1)}, bf16[40,16,256]{2,1,0:T(8,128)(2,1)S(1)}, u32[]{:S(2)}, u32[]{:S(2)}) collective-permute-start(bf16[40,16,256]{2,1,0:T(8,128)(2,1)S(1)} %get-tuple-element.25), channel_id=1, source_target_pairs={{0,3},{1,0},{2,1},{3,2},{4,7},{5,4},{6,5},{7,6},{8,11},{9,8},{10,9... | collective-permute-start | bytes 983048 | tf_op jit(solution)/shard_map/ppermute | solution.py:29
  7.5 13.8 %collective-permute-start.3 = (bf16[40,16,256]{2,1,0:T(8,128)(2,1)S(1)}, bf16[40,16,256]{2,1,0:T(8,128)(2,1)S(1)}, u32[]{:S(2)}, u32[]{:S(2)}) collective-permute-start(bf16[40,16,256]{2,1,0:T(8,128)(2,1)S(1)} %get-tuple-element.26), channel_id=1, source_target_pairs={{0,1},{1,2},{2,3},{3,0},{4,5},{5,6},{6,7},{7,4},{8,9},{9,10},{10,1... | collective-permute-start | bytes 983048 | tf_op jit(solution)/shard_map/ppermute | solution.py:29
  15.5 9.7 %collective-permute-start.5 = (bf16[40,16,256]{2,1,0:T(8,128)(2,1)S(1)}, bf16[40,16,256]{2,1,0:T(8,128)(2,1)S(1)}, u32[]{:S(2)}, u32[]{:S(2)}) collective-permute-start(bf16[40,16,256]{2,1,0:T(8,128)(2,1)S(1)} %get-tuple-element.21), channel_id=1, source_target_pairs={{0,3},{1,0},{2,1},{3,2},{4,7},{5,4},{6,5},{7,6},{8,11},{9,8},{10,9... | collective-permute-start | bytes 983048 | tf_op jit(solution)/shard_map/ppermute | solution.py:29
  15.9 12.4 %collective-permute-start.2 = (bf16[40,16,256]{2,1,0:T(8,128)(2,1)S(1)}, bf16[40,16,256]{2,1,0:T(8,128)(2,1)S(1)}, u32[]{:S(2)}, u32[]{:S(2)}) collective-permute-start(bf16[40,16,256]{2,1,0:T(8,128)(2,1)S(1)} %get-tuple-element.22), channel_id=1, source_target_pairs={{0,1},{1,2},{2,3},{3,0},{4,5},{5,6},{6,7},{7,4},{8,9},{9,10},{10,1... | collective-permute-start | bytes 983048 | tf_op jit(solution)/shard_map/ppermute | solution.py:29
  17.1 13.5 %copy-start.5 = (s32[80]{0:T(128)}, s32[80]{0:T(128)S(1)}, u32[]{:S(2)}) copy-start(s32[80]{0:T(128)S(1)} %multiply_add_fusion) | copy-start | bytes 964
  30.5 0.8 copy-start
  31.4 13.7 %copy-start.3 = (bf16[1,3,1024,256]{3,2,1,0:T(8,128)(2,1)S(1)}, bf16[1,3,1024,256]{3,2,1,0:T(8,128)(2,1)}, u32[]{:S(2)}) copy-start(bf16[1,3,1024,256]{3,2,1,0:T(8,128)(2,1)} %param.9) | copy-start | bytes 4718596
  31.4 53.4 %all-to-all-start = ((bf16[64,3,16,256]{3,2,1,0:T(8,128)(2,1)}), bf16[64,3,16,256]{3,2,1,0:T(8,128)(2,1)S(1)}, u32[]{:S(2)}, u32[]{:S(2)}) async-start(bf16[64,3,16,256]{3,2,1,0:T(8,128)(2,1)} %get-tuple-element.13), calls=%async_computation | async-start | bytes 3145728 | tf_op jit(solution)/shard_map/all_to_all | solution.py:265
  46.3 20.1 %collective-permute-start.12 = (bf16[3,512,256]{2,1,0:T(8,128)(2,1)}, bf16[3,512,256]{2,1,0:T(8,128)(2,1)S(1)}, u32[]{:S(2)}, u32[]{:S(2)}) collective-permute-start(bf16[3,512,256]{2,1,0:T(8,128)(2,1)} %get-tuple-element.14), channel_id=1, source_target_pairs={{0,1},{1,2},{2,3},{3,0},{4,5},{5,6},{6,7},{7,4},{8,9},{9,10},{10,1... | collective-permute-start | bytes 2359304 | tf_op jit(solution)/shard_map/ppermute | solution.py:29
  46.3 20.1 %collective-permute-start.15 = (bf16[3,512,256]{2,1,0:T(8,128)(2,1)}, bf16[3,512,256]{2,1,0:T(8,128)(2,1)}, u32[]{:S(2)}, u32[]{:S(2)}) collective-permute-start(bf16[3,512,256]{2,1,0:T(8,128)(2,1)} %get-tuple-element.15), channel_id=1, source_target_pairs={{0,3},{1,0},{2,1},{3,2},{4,7},{5,4},{6,5},{7,6},{8,11},{9,8},{10,9... | collective-permute-start | bytes 2359304 | tf_op jit(solution)/shard_map/ppermute | solution.py:29
  49.0 41.7 %collective-permute-start.17 = (bf16[3,512,256]{2,1,0:T(8,128)(2,1)}, bf16[3,512,256]{2,1,0:T(8,128)(2,1)S(1)}, u32[]{:S(2)}, u32[]{:S(2)}) collective-permute-start(bf16[3,512,256]{2,1,0:T(8,128)(2,1)} %get-tuple-element.14), channel_id=1, source_target_pairs={{0,3},{1,0},{2,1},{3,2},{4,7},{5,4},{6,5},{7,6},{8,11},{9,8},{10,9... | collective-permute-start | bytes 2359304 | tf_op jit(solution)/shard_map/ppermute | solution.py:29
  49.0 43.2 %collective-permute-start.13 = (bf16[3,512,256]{2,1,0:T(8,128)(2,1)}, bf16[3,512,256]{2,1,0:T(8,128)(2,1)}, u32[]{:S(2)}, u32[]{:S(2)}) collective-permute-start(bf16[3,512,256]{2,1,0:T(8,128)(2,1)} %get-tuple-element.15), channel_id=1, source_target_pairs={{0,1},{1,2},{2,3},{3,0},{4,5},{5,6},{6,7},{7,4},{8,9},{9,10},{10,1... | collective-permute-start | bytes 2359304 | tf_op jit(solution)/shard_map/ppermute | solution.py:29
  66.4 33.8 %collective-permute-start.14 = (bf16[3,512,256]{2,1,0:T(8,128)(2,1)S(1)}, bf16[3,512,256]{2,1,0:T(8,128)(2,1)}, u32[]{:S(2)}, u32[]{:S(2)}) collective-permute-start(bf16[3,512,256]{2,1,0:T(8,128)(2,1)S(1)} %collective-permute-done.12.refs_6_), channel_id=1, source_target_pairs={{0,1},{1,2},{2,3},{3,0},{4,5},{5,6},{6,7},{7,4},{8,9},{9,10},{10,1... | collective-permute-start | bytes 2359304 | tf_op jit(solution)/shard_map/ppermute | solution.py:29
  66.4 40.3 %collective-permute-start.16 = (bf16[3,512,256]{2,1,0:T(8,128)(2,1)}, bf16[3,512,256]{2,1,0:T(8,128)(2,1)}, u32[]{:S(2)}, u32[]{:S(2)}) collective-permute-start(bf16[3,512,256]{2,1,0:T(8,128)(2,1)} %collective-permute-done.15.refs_11_), channel_id=1, source_target_pairs={{0,3},{1,0},{2,1},{3,2},{4,7},{5,4},{6,5},{7,6},{8,11},{9,8},{10,9... | collective-permute-start | bytes 2359304 | tf_op jit(solution)/shard_map/ppermute | solution.py:29
  90.3 13.0 %collective-permute-start.9 = (bf16[3,128,256]{2,1,0:T(8,128)(2,1)S(1)}, bf16[3,128,256]{2,1,0:T(8,128)(2,1)S(1)}, u32[]{:S(2)}, u32[]{:S(2)}) collective-permute-start(bf16[3,128,256]{2,1,0:T(8,128)(2,1)S(1)} %get-tuple-element.32), channel_id=1, source_target_pairs={{0,3},{1,0},{2,1},{3,2},{4,7},{5,4},{6,5},{7,6},{8,11},{9,8},{10,9... | collective-permute-start | bytes 589832 | tf_op jit(solution)/shard_map/ppermute | solution.py:29
  90.7 16.0 %collective-permute-start.7 = (bf16[3,128,256]{2,1,0:T(8,128)(2,1)S(1)}, bf16[3,128,256]{2,1,0:T(8,128)(2,1)S(1)}, u32[]{:S(2)}, u32[]{:S(2)}) collective-permute-start(bf16[3,128,256]{2,1,0:T(8,128)(2,1)S(1)} %get-tuple-element.33), channel_id=1, source_target_pairs={{0,1},{1,2},{2,3},{3,0},{4,5},{5,6},{6,7},{7,4},{8,9},{9,10},{10,1... | collective-permute-start | bytes 589832 | tf_op jit(solution)/shard_map/ppermute | solution.py:29
  92.2 24.0 %collective-permute-start.11 = (bf16[3,256,256]{2,1,0:T(8,128)(2,1)S(1)}, bf16[3,256,256]{2,1,0:T(8,128)(2,1)S(1)}, u32[]{:S(2)}, u32[]{:S(2)}) collective-permute-start(bf16[3,256,256]{2,1,0:T(8,128)(2,1)S(1)} %get-tuple-element.29), channel_id=1, source_target_pairs={{0,3},{1,0},{2,1},{3,2},{4,7},{5,4},{6,5},{7,6},{8,11},{9,8},{10,9... | collective-permute-start | bytes 1179656 | tf_op jit(solution)/shard_map/ppermute | solution.py:29
  100.2 16.0 %collective-permute-start.6 = (bf16[3,256,256]{2,1,0:T(8,128)(2,1)S(1)}, bf16[3,256,256]{2,1,0:T(8,128)(2,1)S(1)}, u32[]{:S(2)}, u32[]{:S(2)}) collective-permute-start(bf16[3,256,256]{2,1,0:T(8,128)(2,1)S(1)} %get-tuple-element.30), channel_id=1, source_target_pairs={{0,1},{1,2},{2,3},{3,0},{4,5},{5,6},{6,7},{7,4},{8,9},{9,10},{10,1... | collective-permute-start | bytes 1179656 | tf_op jit(solution)/shard_map/ppermute | solution.py:29
  103.3 12.6 %collective-permute-start.10 = (bf16[3,128,256]{2,1,0:T(8,128)(2,1)S(1)}, bf16[3,128,256]{2,1,0:T(8,128)(2,1)S(1)}, u32[]{:S(2)}, u32[]{:S(2)}) collective-permute-start(bf16[3,128,256]{2,1,0:T(8,128)(2,1)S(1)} %collective-permute-done.9), channel_id=1, source_target_pairs={{0,3},{1,0},{2,1},{3,2},{4,7},{5,4},{6,5},{7,6},{8,11},{9,8},{10,9... | collective-permute-start | bytes 589832 | tf_op jit(solution)/shard_map/ppermute | solution.py:29
  106.7 9.6 %collective-permute-start.8 = (bf16[3,128,256]{2,1,0:T(8,128)(2,1)S(1)}, bf16[3,128,256]{2,1,0:T(8,128)(2,1)S(1)}, u32[]{:S(2)}, u32[]{:S(2)}) collective-permute-start(bf16[3,128,256]{2,1,0:T(8,128)(2,1)S(1)} %collective-permute-done.7), channel_id=1, source_target_pairs={{0,1},{1,2},{2,3},{3,0},{4,5},{5,6},{6,7},{7,4},{8,9},{9,10},{10,1... | collective-permute-start | bytes 589832 | tf_op jit(solution)/shard_map/ppermute | solution.py:29
  122.2 12.1 %copy-start.1 = (bf16[80,16,256]{2,1,0:T(8,128)(2,1)S(1)}, bf16[80,16,256]{2,1,0:T(8,128)(2,1)}, u32[]{:S(2)}) copy-start(bf16[80,16,256]{2,1,0:T(8,128)(2,1)} %copy-done) | copy-start | bytes 1966084
  122.2 12.1 %copy-start.4 = (f32[80,16,256]{2,1,0:T(8,128)S(1)}, f32[80,16,256]{2,1,0:T(8,128)}, u32[]{:S(2)}) copy-start(f32[80,16,256]{2,1,0:T(8,128)} %param.6) | copy-start | bytes 3932164
  122.2 51.9 %all-to-all-start.1 = ((bf16[64,3,16,256]{3,2,1,0:T(8,128)(2,1)}), bf16[64,3,16,256]{3,2,1,0:T(8,128)(2,1)S(1)}, u32[]{:S(2)}, u32[]{:S(2)}) async-start(bf16[64,3,16,256]{3,2,1,0:T(8,128)(2,1)} %get-tuple-element.17), calls=%async_computation.1 | async-start | bytes 3145728 | tf_op jit(solution)/shard_map/all_to_all | solution.py:265
  174.9 16.2 %copy-start.6 = (s32[80]{0:T(128)S(1)}, s32[80]{0:T(128)}, u32[]{:S(2)}) copy-start(s32[80]{0:T(128)} %copy-done.5) | copy-start | bytes 964
  175.5 15.3 %all-to-all-start.2 = ((f32[64,1,128]{2,1,0:T(1,128)}), f32[64,1,128]{2,1,0:T(1,128)S(1)}, u32[]{:S(2)}, u32[]{:S(2)}) async-start(f32[64,1,128]{2,1,0:T(1,128)} %broadcast_in_dim.55), calls=%async_computation.2 | async-start | bytes 65536 | tf_op jit(solution)/shard_map/all_to_all | solution.py:265
  181.7 9.6 %collective-permute-start.20 = (bf16[20,16,256]{2,1,0:T(8,128)(2,1)S(1)}, bf16[20,16,256]{2,1,0:T(8,128)(2,1)S(1)}, u32[]{:S(2)}, u32[]{:S(2)}) collective-permute-start(bf16[20,16,256]{2,1,0:T(8,128)(2,1)S(1)} %get-tuple-element.34), channel_id=1, source_target_pairs={{0,3},{1,0},{2,1},{3,2},{4,7},{5,4},{6,5},{7,6},{8,11},{9,8},{10,9... | collective-permute-start | bytes 491528 | tf_op jit(solution)/shard_map/ppermute | solution.py:29
  184.5 6.9 %collective-permute-start.19 = (bf16[20,16,256]{2,1,0:T(8,128)(2,1)S(1)}, bf16[20,16,256]{2,1,0:T(8,128)(2,1)S(1)}, u32[]{:S(2)}, u32[]{:S(2)}) collective-permute-start(bf16[20,16,256]{2,1,0:T(8,128)(2,1)S(1)} %get-tuple-element.35), channel_id=1, source_target_pairs={{0,2},{1,3},{2,0},{3,1},{4,6},{5,7},{6,4},{7,5},{8,10},{9,11},{10,... | collective-permute-start | bytes 491528 | tf_op jit(solution)/shard_map/ppermute | solution.py:29
  184.5 10.5 %collective-permute-start.18 = (bf16[20,16,256]{2,1,0:T(8,128)(2,1)S(1)}, bf16[20,16,256]{2,1,0:T(8,128)(2,1)S(1)}, u32[]{:S(2)}, u32[]{:S(2)}) collective-permute-start(bf16[20,16,256]{2,1,0:T(8,128)(2,1)S(1)} %get-tuple-element.36), channel_id=1, source_target_pairs={{0,1},{1,2},{2,3},{3,0},{4,5},{5,6},{6,7},{7,4},{8,9},{9,10},{10,1... | collective-permute-start | bytes 491528 | tf_op jit(solution)/shard_map/ppermute | solution.py:29

commit v7 on v5

--- a/solution.py
+++ b/solution.py
@@ -89,37 +89,52 @@
     )(source, *terms)
 
 
-def left_kernel(first, place, gradient, left, out, wide_rows):
-    halves, size, half = wide_rows.shape
-    width = halves * half
-    rows = gradient.shape[2]
+def order_kernel(order, left, out):
+    out[0] = jnp.dot(order[...], left[0], preferred_element_type=jnp.float32).astype(jnp.bfloat16)
+
+
+def order_rows(left, rows):
+    slots, size, _ = left.shape
     part = rows // REP
-    s = pl.program_id(0)
-    low = gradient[:, first + s].reshape(size, width)
-    tile = size // 4
-    for i in range(4):
-        at = slice(i * tile, (i + 1) * tile)
-        product = jnp.dot(left[0, at, :], low, preferred_element_type=jnp.float32)
-        for h in range(halves):
-            wide_rows[h, at, :] = product[:, h * half : (h + 1) * half]
+    number = jnp.arange(size, dtype=jnp.int32)
+    target, j, o = number // (part * OWNERS), number // OWNERS % part, number % OWNERS
+    taken = o * rows + target * part + j
+    order = jnp.where(taken[:, None] == number[None, :], 1.0, 0.0).astype(jnp.bfloat16)
+    return pl.pallas_call(
+        order_kernel,
+        grid=(slots,),
+        out_shape=jax.ShapeDtypeStruct(left.shape, jnp.bfloat16),
+        in_specs=[VMEM, pl.BlockSpec((1, size, size), lambda i: (i, 0, 0))],
+        out_specs=pl.BlockSpec((1, size, size), lambda i: (i, 0, 0)),
+        compiler_params=pltpu.CompilerParams(vmem_limit_bytes=ROOM),
+        cost_estimate=pl.CostEstimate(
+            flops=slots * 2 * size**3, bytes_accessed=slots * 4 * size * size, transcendentals=0
+        ),
+        name="order_rows",
+    )(order, left)
+
+
+def left_kernel(place, gradient, left, out):
+    size = left.shape[1]
+    width = gradient.shape[3]
+    tile = size // REP
+    low = gradient[:, pl.program_id(0)].reshape(size, width)
     for target in range(REP):
         k = lax.rem(target + REP - place[0], REP)
-        for j in range(part):
-            for h in range(halves):
-                strided = wide_rows[h, pl.ds(target * part + j, OWNERS, stride=rows), :]
-                at = slice(j * OWNERS, (j + 1) * OWNERS), slice(h * half, (h + 1) * half)
-                out[(k, 0) + at] = strided.astype(jnp.bfloat16)
-
-
-def left_multiply(place, gradient, left, first, count):
-    size, width = left.shape[1], gradient.shape[3]
-    return pl.pallas_call(
-        lambda *refs: left_kernel(first, *refs),
+        rows = left[0, target * tile : (target + 1) * tile, :]
+        product = jnp.dot(rows, low, preferred_element_type=jnp.float32)
+        out[k, 0] = product.astype(jnp.bfloat16)
+
+
+def left_multiply(place, gradient, left):
+    count, size, _ = left.shape
+    width = gradient.shape[3]
+    return pl.pallas_call(
+        left_kernel,
         grid=(count,),
         out_shape=jax.ShapeDtypeStruct((REP, count, size // REP, width), jnp.bfloat16),
-        in_specs=[SMEM, VMEM, pl.BlockSpec((1, size, size), lambda i: (first + i, 0, 0))],
+        in_specs=[SMEM, VMEM, pl.BlockSpec((1, size, size), lambda i: (i, 0, 0))],
         out_specs=pl.BlockSpec((REP, 1, size // REP, width), lambda i: (0, i, 0, 0)),
-        scratch_shapes=[pltpu.VMEM((width // 128, size, 128), jnp.float32)],
         compiler_params=pltpu.CompilerParams(vmem_limit_bytes=ROOM),
         cost_estimate=pl.CostEstimate(
             flops=count * 2 * size * size * width,
@@ -287,12 +302,13 @@
     rights = gather_over_rep(right_root[0], *passing)
     low, packed = sum_pack(source, terms)
     owned = exchange(packed)
+    ordered = order_rows(left_root[0], rows)
     adam = lax.psum(adam_squares(low, moment), "rep")
 
     def spread(sent):
         return [sent[0]] + [shift(sent[k], k) for k in (1, 2, 3)]
 
-    held = spread(left_multiply(place_ref, owned, left_root[0], 0, CAP))
+    held = spread(left_multiply(place_ref, owned, ordered))
     result, square = right_multiply(place_ref, held, rights)
     back = exchange(result)
     squares = lax.psum(jnp.sum(square, axis=(1, 2)), "rep")

time: 197 us -> 194 us (0.985)
  waiting for transfers between devices: 112 us -> 94.4 us
  Pallas kernels: 16.3 us -> 25.6 us
  starting transfers between devices: 50.8 us -> 55.5 us
    ppermute x18, waiting for transfers between devices: 61 us -> 42.5 us  [shift(): lax.ppermute(value, 'rep', [(i, (i + step) % REP) for i in range(REP)])]
    pallas_call x1 -> x2, Pallas kernels: 5.38 us -> 14.8 us  [the longest x1 10 us: order_rows(): pl.pallas_call(order_kernel, grid=(slots,), out_shape=jax.ShapeDtypeStruc...]
    ppermute x18, starting transfers between devices: 19.7 us -> 24 us  [shift(): lax.ppermute(value, 'rep', [(i, (i + step) % REP) for i in range(REP)])]
  transfers between devices with their start and end apart: 21 -> 21, of which waited for: 12 -> 14; matrix products, arithmetic and copies ran while one was open for 3% -> 3% of each run, Pallas kernels for 3% -> 8%
where the time goes in v7:
time: 194 us; the launch traced here: 193 us
  waiting for transfers between devices  94.4 us (49%)
  starting transfers between devices  55.5 us (29%)
  Pallas kernels  25.6 us (13%)
  blocking collectives  8.02 us (4%)
  local copies, waits for them, and re-layouts  5.64 us (3%)
  other arithmetic  3.38 us (2%)
    all_to_all x3, waiting for transfers between devices, exchange(): return lax.all_to_all(value, 'fsdp', split_axis=0, concat_axis=0)  51.8 us
    ppermute x18, waiting for transfers between devices, shift(): lax.ppermute(value, 'rep', [(i, (i + step) % REP) for i in range(REP)])  42.5 us
    all_to_all x3, starting transfers between devices, exchange(): return lax.all_to_all(value, 'fsdp', split_axis=0, concat_axis=0)  31.5 us
    ppermute x18, starting transfers between devices, shift(): lax.ppermute(value, 'rep', [(i, (i + step) % REP) for i in range(REP)])  24 us
    pallas_call x1, Pallas kernels, order_rows(): pl.pallas_call(order_kernel, grid=(slots,), out_shape=jax.ShapeDtypeStruc...  10 us
    psum x1, blocking collectives, shards(): squares = lax.psum(jnp.sum(square, axis=(1, 2)), 'rep')  8.02 us
    pallas_call x1, Pallas kernels, right_multiply(): pl.pallas_call(right_kernel, grid=(count,), out_shape=[jax.ShapeDtypeStru...  5.93 us
    pallas_call x1, Pallas kernels, left_multiply(): pl.pallas_call(left_kernel, grid=(count,), out_shape=jax.ShapeDtypeStruct...  4.78 us
  transfers between devices with their start and end apart: 21, of which 14 were waited for; matrix products, arithmetic and copies ran while one was open for 3% of the time, Pallas kernels for 8%

profile of v7, /device:TPU:1, one launch (start us, length us, event | category | flops | bytes accessed | tf_op | source)
XLA Modules:
  0.0 192.8 jit_solution(6498295068668037268)
XLA Ops:
  0.0 1.4 dynamic-slice_bitcast_fusion.1
  1.4 2.1 %collective-permute-start.1 = (bf16[40,16,256]{2,1,0:T(8,128)(2,1)S(1)}, bf16[40,16,256]{2,1,0:T(8,128)(2,1)S(1)}, u32[]{:S(2)}, u32[]{:S(2)}) collective-permute-start(bf16[40,16,256]{2,1,0:T(8,128)(2,1)S(1)} %get-tuple-element.24), channel_id=1, source_target_pairs={{0,1},{1,2},{2,3},{3,0},{4,5},{5,6},{6,7},{7,4},{8,9},{9,10},{10,1... | collective-permute-start | bytes 983048 | tf_op jit(solution)/shard_map/ppermute | solution.py:29
  3.5 1.4 collective-permute-start.4
  4.9 1.4 collective-permute-start
  6.5 3.4 %collective-permute-done.1 = bf16[40,16,256]{2,1,0:T(8,128)(2,1)S(1)} collective-permute-done((bf16[40,16,256]{2,1,0:T(8,128)(2,1)S(1)}, bf16[40,16,256]{2,1,0:T(8,128)(2,1)S(1)}, u32[]{:S(2)}, u32[]{:S(2)}) %collective-permute-start.1) | collective-permute-done | bytes 327712 | tf_op jit(solution)/shard_map/ppermute | solution.py:29
  9.9 1.5 collective-permute-done.4
  11.4 1.3 fusion.5
  12.7 1.6 collective-permute-start.2
  16.7 1.7 collective-permute-done.near_left
  18.4 5.8 %collective-permute-done.2.last_right = bf16[40,16,256]{2,1,0:T(8,128)(2,1)S(1)} collective-permute-done((bf16[40,16,256]{2,1,0:T(8,128)(2,1)S(1)}, bf16[40,16,256]{2,1,0:T(8,128)(2,1)S(1)}, u32[]{:S(2)}, u32[]{:S(2)}) %collective-permute-start.2) | collective-permute-done | bytes 327712 | tf_op jit(solution)/shard_map/ppermute | solution.py:29
  25.5 2.2 %sum_pack.1 = (bf16[80,16,256]{2,1,0:T(8,128)(2,1)S(1)}, bf16[64,3,16,256]{3,2,1,0:T(8,128)(2,1)}) custom-call(s32[192]{0:T(256)S(1)} %select_reduce_fusion.1.source, bf16[80,16,256]{2,1,0:T(8,128)(2,1)S(1)} %dynamic-slice_bitcast_fusion.own, bf16[40,16,256]{2,1,0:T(8,128)(2,1)S(1)} %collective-permute-done.near_left, ...), custom_call_target="tpu_custom_call" | custom-call | tf_op jit(solution)/shard_map/sum_pack/pallas_call | solution.py:79
  28.6 14.0 %all-to-all-start = ((bf16[64,3,16,256]{3,2,1,0:T(8,128)(2,1)}), bf16[64,3,16,256]{3,2,1,0:T(8,128)(2,1)S(1)}, u32[]{:S(2)}, u32[]{:S(2)}) async-start(bf16[64,3,16,256]{3,2,1,0:T(8,128)(2,1)} %get-tuple-element.13), calls=%async_computation | async-start | bytes 3145728 | tf_op jit(solution)/shard_map/all_to_all | solution.py:277
  45.0 1.5 collective-permute-start.12
  47.0 2.7 %collective-permute-start.14 = (bf16[3,512,256]{2,1,0:T(8,128)(2,1)}, bf16[3,512,256]{2,1,0:T(8,128)(2,1)}, u32[]{:S(2)}, u32[]{:S(2)}) collective-permute-start(bf16[3,512,256]{2,1,0:T(8,128)(2,1)} %get-tuple-element.14), channel_id=1, source_target_pairs={{0,3},{1,0},{2,1},{3,2},{4,7},{5,4},{6,5},{7,6},{8,11},{9,8},{10,9... | collective-permute-start | bytes 2359304 | tf_op jit(solution)/shard_map/ppermute | solution.py:29
  49.7 10.0 %order_rows.1.left = bf16[3,1024,1024]{2,1,0:T(8,128)(2,1)} custom-call(bf16[1024,1024]{1,0:T(8,128)(2,1)S(1)} %select_convert_fusion.order, bf16[3,1024,1024]{2,1,0:T(8,128)(2,1)} %bitcast.46), custom_call_target="tpu_custom_call" | custom-call | flops 6442450944 | bytes 12582912 | tf_op jit(solution)/shard_map/order_rows/pallas_call | solution.py:103
  59.7 4.2 %collective-permute-done.9.refs_5_ = bf16[3,512,256]{2,1,0:T(8,128)(2,1)S(1)} collective-permute-done((bf16[3,512,256]{2,1,0:T(8,128)(2,1)}, bf16[3,512,256]{2,1,0:T(8,128)(2,1)S(1)}, u32[]{:S(2)}, u32[]{:S(2)}) %collective-permute-start.9) | collective-permute-done | bytes 786464 | tf_op jit(solution)/shard_map/ppermute | solution.py:29
  64.0 2.6 %collective-permute-start.13 = (bf16[3,512,256]{2,1,0:T(8,128)(2,1)}, bf16[3,512,256]{2,1,0:T(8,128)(2,1)}, u32[]{:S(2)}, u32[]{:S(2)}) collective-permute-start(bf16[3,512,256]{2,1,0:T(8,128)(2,1)} %collective-permute-done.12.refs_10_), channel_id=1, source_target_pairs={{0,3},{1,0},{2,1},{3,2},{4,7},{5,4},{6,5},{7,6},{8,11},{9,8},{10,9... | collective-permute-start | bytes 2359304 | tf_op jit(solution)/shard_map/ppermute | solution.py:29
  66.6 15.8 %all-to-all-done.gradient = bf16[64,3,16,256]{3,2,1,0:T(8,128)(2,1)S(1)} async-done(((bf16[64,3,16,256]{3,2,1,0:T(8,128)(2,1)}), bf16[64,3,16,256]{3,2,1,0:T(8,128)(2,1)S(1)}, u32[]{:S(2)}, u32[]{:S(2)}) %all-to-all-start) | async-done | bytes 1572896 | tf_op jit(solution)/shard_map/all_to_all | solution.py:277
  82.4 4.8 %left_multiply.1 = bf16[4,3,256,256]{3,2,1,0:T(8,128)(2,1)S(1)} custom-call(s32[1]{0:T(128)} %bitcast.place, bf16[64,3,16,256]{3,2,1,0:T(8,128)(2,1)S(1)} %all-to-all-done.gradient, bf16[3,1024,1024]{2,1,0:T(8,128)(2,1)} %order_rows.1.left), custom_call_target="tpu_custom_call" | custom-call | flops 1610612736 | bytes 12582912 | tf_op jit(solution)/shard_map/left_multiply/pallas_call | solution.py:132
  87.3 1.3 collective-permute-start.6
  88.5 2.6 %collective-permute-start.7 = (bf16[3,256,256]{2,1,0:T(8,128)(2,1)S(1)}, bf16[3,256,256]{2,1,0:T(8,128)(2,1)S(1)}, u32[]{:S(2)}, u32[]{:S(2)}) collective-permute-start(bf16[3,256,256]{2,1,0:T(8,128)(2,1)S(1)} %get-tuple-element.30), channel_id=1, source_target_pairs={{0,2},{1,3},{2,0},{3,1},{4,6},{5,7},{6,4},{7,5},{8,10},{9,11},{10,... | collective-permute-start | bytes 1179656 | tf_op jit(solution)/shard_map/ppermute | solution.py:29
  91.9 5.9 %collective-permute-done.11.refs_7_ = bf16[3,512,256]{2,1,0:T(8,128)(2,1)} collective-permute-done((bf16[3,512,256]{2,1,0:T(8,128)(2,1)S(1)}, bf16[3,512,256]{2,1,0:T(8,128)(2,1)}, u32[]{:S(2)}, u32[]{:S(2)}) %collective-permute-start.11) | collective-permute-done | bytes 786464 | tf_op jit(solution)/shard_map/ppermute | solution.py:29
  97.7 8.3 %collective-permute-done.6.refs_1_ = bf16[3,256,256]{2,1,0:T(8,128)(2,1)S(1)} collective-permute-done((bf16[3,256,256]{2,1,0:T(8,128)(2,1)S(1)}, bf16[3,256,256]{2,1,0:T(8,128)(2,1)S(1)}, u32[]{:S(2)}, u32[]{:S(2)}) %collective-permute-start.6) | collective-permute-done | bytes 393248 | tf_op jit(solution)/shard_map/ppermute | solution.py:29
  106.0 9.6 %collective-permute-done.7.refs_2_ = bf16[3,256,256]{2,1,0:T(8,128)(2,1)S(1)} collective-permute-done((bf16[3,256,256]{2,1,0:T(8,128)(2,1)S(1)}, bf16[3,256,256]{2,1,0:T(8,128)(2,1)S(1)}, u32[]{:S(2)}, u32[]{:S(2)}) %collective-permute-start.7) | collective-permute-done | bytes 393248 | tf_op jit(solution)/shard_map/ppermute | solution.py:29
  115.6 5.9 %right_multiply.1 = (bf16[64,3,16,256]{3,2,1,0:T(8,128)(2,1)}, f32[3,1,256]{2,1,0:T(1,128)S(1)}) custom-call(s32[1]{0:T(128)} %bitcast.place, bf16[3,256,256]{2,1,0:T(8,128)(2,1)S(1)} %get-tuple-element.32.refs_0_, bf16[3,256,256]{2,1,0:T(8,128)(2,1)S(1)} %collective-permute-done.6.refs_1_, bf16[3,256,256]{2,1,0:T(8,128)(2,1)S(1)} %collective-permute-done.7.refs_2_, ...), custom_call_target="tpu_custom_call" | custom-call | flops 1610612736 | bytes 12582912 | tf_op jit(solution)/shard_map/right_multiply/pallas_call | solution.py:186
  121.6 11.4 %all-to-all-start.1 = ((bf16[64,3,16,256]{3,2,1,0:T(8,128)(2,1)}), bf16[64,3,16,256]{3,2,1,0:T(8,128)(2,1)S(1)}, u32[]{:S(2)}, u32[]{:S(2)}) async-start(bf16[64,3,16,256]{3,2,1,0:T(8,128)(2,1)} %get-tuple-element.17), calls=%async_computation.1 | async-start | bytes 3145728 | tf_op jit(solution)/shard_map/all_to_all | solution.py:277
  134.1 8.0 %all-reduce = (f32[3]{0:T(128)S(1)}, f32[80]{0:T(128)S(1)}) all-reduce(f32[3]{0:T(128)S(1)} %reduce_sum.57, f32[80]{0:T(128)S(1)} %fusion.4), channel_id=1, replica_groups=mesh['fsdp'=64,'rep'=4] {'rep'}, use_global_device_ids=true, to_apply=%region_5.6 | all-reduce | flops 83 | bytes 664 | tf_op jit(solution)/shard_map/psum | solution.py:314
  142.2 30.6 %all-to-all-done.1.back = bf16[64,3,16,256]{3,2,1,0:T(8,128)(2,1)S(1)} async-done(((bf16[64,3,16,256]{3,2,1,0:T(8,128)(2,1)}), bf16[64,3,16,256]{3,2,1,0:T(8,128)(2,1)S(1)}, u32[]{:S(2)}, u32[]{:S(2)}) %all-to-all-start.1) | async-done | bytes 1572896 | tf_op jit(solution)/shard_map/all_to_all | solution.py:277
  174.2 6.1 %all-to-all-start.2 = ((f32[64,1,128]{2,1,0:T(1,128)}), f32[64,1,128]{2,1,0:T(1,128)S(1)}, u32[]{:S(2)}, u32[]{:S(2)}) async-start(f32[64,1,128]{2,1,0:T(1,128)} %broadcast_in_dim.67), calls=%async_computation.2 | async-start | bytes 65536 | tf_op jit(solution)/shard_map/all_to_all | solution.py:277
  180.5 2.6 %collective-permute-start.16 = (bf16[20,16,256]{2,1,0:T(8,128)(2,1)S(1)}, bf16[20,16,256]{2,1,0:T(8,128)(2,1)S(1)}, u32[]{:S(2)}, u32[]{:S(2)}) collective-permute-start(bf16[20,16,256]{2,1,0:T(8,128)(2,1)S(1)} %get-tuple-element.34), channel_id=1, source_target_pairs={{0,2},{1,3},{2,0},{3,1},{4,6},{5,7},{6,4},{7,5},{8,10},{9,11},{10,... | collective-permute-start | bytes 491528 | tf_op jit(solution)/shard_map/ppermute | solution.py:29
  184.0 5.5 %all-to-all-done.2 = f32[64,1,128]{2,1,0:T(1,128)S(1)} async-done(((f32[64,1,128]{2,1,0:T(1,128)}), f32[64,1,128]{2,1,0:T(1,128)S(1)}, u32[]{:S(2)}, u32[]{:S(2)}) %all-to-all-start.2) | async-done | bytes 32800 | tf_op jit(solution)/shard_map/all_to_all | solution.py:277
  190.9 1.9 join_blocks.1
  (53 shorter events, 13.5 us)
Async XLA Ops:
  0.0 6.3 %copy-start.2 = (s32[80]{0:T(128)S(1)}, s32[80]{0:T(128)}, u32[]{:S(2)}) copy-start(s32[80]{0:T(128)} %owner.1) | copy-start | bytes 964
  1.4 8.5 %collective-permute-start.1 = (bf16[40,16,256]{2,1,0:T(8,128)(2,1)S(1)}, bf16[40,16,256]{2,1,0:T(8,128)(2,1)S(1)}, u32[]{:S(2)}, u32[]{:S(2)}) collective-permute-start(bf16[40,16,256]{2,1,0:T(8,128)(2,1)S(1)} %get-tuple-element.24), channel_id=1, source_target_pairs={{0,1},{1,2},{2,3},{3,0},{4,5},{5,6},{6,7},{7,4},{8,9},{9,10},{10,1... | collective-permute-start | bytes 983048 | tf_op jit(solution)/shard_map/ppermute | solution.py:29
  3.5 7.9 %collective-permute-start.4 = (bf16[40,16,256]{2,1,0:T(8,128)(2,1)S(1)}, bf16[40,16,256]{2,1,0:T(8,128)(2,1)S(1)}, u32[]{:S(2)}, u32[]{:S(2)}) collective-permute-start(bf16[40,16,256]{2,1,0:T(8,128)(2,1)S(1)} %get-tuple-element.23), channel_id=1, source_target_pairs={{0,3},{1,0},{2,1},{3,2},{4,7},{5,4},{6,5},{7,6},{8,11},{9,8},{10,9... | collective-permute-start | bytes 983048 | tf_op jit(solution)/shard_map/ppermute | solution.py:29
  4.9 13.6 %collective-permute-start = (bf16[40,16,256]{2,1,0:T(8,128)(2,1)S(1)}, bf16[40,16,256]{2,1,0:T(8,128)(2,1)S(1)}, u32[]{:S(2)}, u32[]{:S(2)}) collective-permute-start(bf16[40,16,256]{2,1,0:T(8,128)(2,1)S(1)} %get-tuple-element.25), channel_id=1, source_target_pairs={{0,3},{1,0},{2,1},{3,2},{4,7},{5,4},{6,5},{7,6},{8,11},{9,8},{10,9... | collective-permute-start | bytes 983048 | tf_op jit(solution)/shard_map/ppermute | solution.py:29
  6.2 12.2 %collective-permute-start.3 = (bf16[40,16,256]{2,1,0:T(8,128)(2,1)S(1)}, bf16[40,16,256]{2,1,0:T(8,128)(2,1)S(1)}, u32[]{:S(2)}, u32[]{:S(2)}) collective-permute-start(bf16[40,16,256]{2,1,0:T(8,128)(2,1)S(1)} %get-tuple-element.26), channel_id=1, source_target_pairs={{0,1},{1,2},{2,3},{3,0},{4,5},{5,6},{6,7},{7,4},{8,9},{9,10},{10,1... | collective-permute-start | bytes 983048 | tf_op jit(solution)/shard_map/ppermute | solution.py:29
  12.7 11.5 %collective-permute-start.2 = (bf16[40,16,256]{2,1,0:T(8,128)(2,1)S(1)}, bf16[40,16,256]{2,1,0:T(8,128)(2,1)S(1)}, u32[]{:S(2)}, u32[]{:S(2)}) collective-permute-start(bf16[40,16,256]{2,1,0:T(8,128)(2,1)S(1)} %get-tuple-element.22), channel_id=1, source_target_pairs={{0,1},{1,2},{2,3},{3,0},{4,5},{5,6},{6,7},{7,4},{8,9},{9,10},{10,1... | collective-permute-start | bytes 983048 | tf_op jit(solution)/shard_map/ppermute | solution.py:29
  14.3 11.1 %collective-permute-start.5 = (bf16[40,16,256]{2,1,0:T(8,128)(2,1)S(1)}, bf16[40,16,256]{2,1,0:T(8,128)(2,1)S(1)}, u32[]{:S(2)}, u32[]{:S(2)}) collective-permute-start(bf16[40,16,256]{2,1,0:T(8,128)(2,1)S(1)} %get-tuple-element.21), channel_id=1, source_target_pairs={{0,3},{1,0},{2,1},{3,2},{4,7},{5,4},{6,5},{7,6},{8,11},{9,8},{10,9... | collective-permute-start | bytes 983048 | tf_op jit(solution)/shard_map/ppermute | solution.py:29
  15.5 12.2 %copy-start.5 = (s32[80]{0:T(128)}, s32[80]{0:T(128)S(1)}, u32[]{:S(2)}) copy-start(s32[80]{0:T(128)S(1)} %multiply_add_fusion) | copy-start | bytes 964
  27.7 0.8 copy-start
  28.6 14.0 %copy-start.3 = (bf16[1,3,1024,256]{3,2,1,0:T(8,128)(2,1)S(1)}, bf16[1,3,1024,256]{3,2,1,0:T(8,128)(2,1)}, u32[]{:S(2)}) copy-start(bf16[1,3,1024,256]{3,2,1,0:T(8,128)(2,1)} %param.9) | copy-start | bytes 4718596
  28.6 53.8 %all-to-all-start = ((bf16[64,3,16,256]{3,2,1,0:T(8,128)(2,1)}), bf16[64,3,16,256]{3,2,1,0:T(8,128)(2,1)S(1)}, u32[]{:S(2)}, u32[]{:S(2)}) async-start(bf16[64,3,16,256]{3,2,1,0:T(8,128)(2,1)} %get-tuple-element.13), calls=%async_computation | async-start | bytes 3145728 | tf_op jit(solution)/shard_map/all_to_all | solution.py:277
  43.8 20.1 %collective-permute-start.9 = (bf16[3,512,256]{2,1,0:T(8,128)(2,1)}, bf16[3,512,256]{2,1,0:T(8,128)(2,1)S(1)}, u32[]{:S(2)}, u32[]{:S(2)}) collective-permute-start(bf16[3,512,256]{2,1,0:T(8,128)(2,1)} %get-tuple-element.14), channel_id=1, source_target_pairs={{0,1},{1,2},{2,3},{3,0},{4,5},{5,6},{6,7},{7,4},{8,9},{9,10},{10,1... | collective-permute-start | bytes 2359304 | tf_op jit(solution)/shard_map/ppermute | solution.py:29
  45.0 19.0 %collective-permute-start.12 = (bf16[3,512,256]{2,1,0:T(8,128)(2,1)}, bf16[3,512,256]{2,1,0:T(8,128)(2,1)}, u32[]{:S(2)}, u32[]{:S(2)}) collective-permute-start(bf16[3,512,256]{2,1,0:T(8,128)(2,1)} %get-tuple-element.15), channel_id=1, source_target_pairs={{0,3},{1,0},{2,1},{3,2},{4,7},{5,4},{6,5},{7,6},{8,11},{9,8},{10,9... | collective-permute-start | bytes 2359304 | tf_op jit(solution)/shard_map/ppermute | solution.py:29
  46.9 41.6 %collective-permute-start.10 = (bf16[3,512,256]{2,1,0:T(8,128)(2,1)}, bf16[3,512,256]{2,1,0:T(8,128)(2,1)S(1)}, u32[]{:S(2)}, u32[]{:S(2)}) collective-permute-start(bf16[3,512,256]{2,1,0:T(8,128)(2,1)} %get-tuple-element.15), channel_id=1, source_target_pairs={{0,1},{1,2},{2,3},{3,0},{4,5},{5,6},{6,7},{7,4},{8,9},{9,10},{10,1... | collective-permute-start | bytes 2359304 | tf_op jit(solution)/shard_map/ppermute | solution.py:29
  47.0 44.2 %collective-permute-start.14 = (bf16[3,512,256]{2,1,0:T(8,128)(2,1)}, bf16[3,512,256]{2,1,0:T(8,128)(2,1)}, u32[]{:S(2)}, u32[]{:S(2)}) collective-permute-start(bf16[3,512,256]{2,1,0:T(8,128)(2,1)} %get-tuple-element.14), channel_id=1, source_target_pairs={{0,3},{1,0},{2,1},{3,2},{4,7},{5,4},{6,5},{7,6},{8,11},{9,8},{10,9... | collective-permute-start | bytes 2359304 | tf_op jit(solution)/shard_map/ppermute | solution.py:29
  63.9 33.8 %collective-permute-start.11 = (bf16[3,512,256]{2,1,0:T(8,128)(2,1)S(1)}, bf16[3,512,256]{2,1,0:T(8,128)(2,1)}, u32[]{:S(2)}, u32[]{:S(2)}) collective-permute-start(bf16[3,512,256]{2,1,0:T(8,128)(2,1)S(1)} %collective-permute-done.9.refs_5_), channel_id=1, source_target_pairs={{0,1},{1,2},{2,3},{3,0},{4,5},{5,6},{6,7},{7,4},{8,9},{9,10},{10,1... | collective-permute-start | bytes 2359304 | tf_op jit(solution)/shard_map/ppermute | solution.py:29
  64.0 33.7 %collective-permute-start.13 = (bf16[3,512,256]{2,1,0:T(8,128)(2,1)}, bf16[3,512,256]{2,1,0:T(8,128)(2,1)}, u32[]{:S(2)}, u32[]{:S(2)}) collective-permute-start(bf16[3,512,256]{2,1,0:T(8,128)(2,1)} %collective-permute-done.12.refs_10_), channel_id=1, source_target_pairs={{0,3},{1,0},{2,1},{3,2},{4,7},{5,4},{6,5},{7,6},{8,11},{9,8},{10,9... | collective-permute-start | bytes 2359304 | tf_op jit(solution)/shard_map/ppermute | solution.py:29
  87.3 18.8 %collective-permute-start.6 = (bf16[3,256,256]{2,1,0:T(8,128)(2,1)S(1)}, bf16[3,256,256]{2,1,0:T(8,128)(2,1)S(1)}, u32[]{:S(2)}, u32[]{:S(2)}) collective-permute-start(bf16[3,256,256]{2,1,0:T(8,128)(2,1)S(1)} %get-tuple-element.31), channel_id=1, source_target_pairs={{0,1},{1,2},{2,3},{3,0},{4,5},{5,6},{6,7},{7,4},{8,9},{9,10},{10,1... | collective-permute-start | bytes 1179656 | tf_op jit(solution)/shard_map/ppermute | solution.py:29
  88.5 27.1 %collective-permute-start.7 = (bf16[3,256,256]{2,1,0:T(8,128)(2,1)S(1)}, bf16[3,256,256]{2,1,0:T(8,128)(2,1)S(1)}, u32[]{:S(2)}, u32[]{:S(2)}) collective-permute-start(bf16[3,256,256]{2,1,0:T(8,128)(2,1)S(1)} %get-tuple-element.30), channel_id=1, source_target_pairs={{0,2},{1,3},{2,0},{3,1},{4,6},{5,7},{6,4},{7,5},{8,10},{9,11},{10,... | collective-permute-start | bytes 1179656 | tf_op jit(solution)/shard_map/ppermute | solution.py:29
  91.2 24.5 %collective-permute-start.8 = (bf16[3,256,256]{2,1,0:T(8,128)(2,1)S(1)}, bf16[3,256,256]{2,1,0:T(8,128)(2,1)S(1)}, u32[]{:S(2)}, u32[]{:S(2)}) collective-permute-start(bf16[3,256,256]{2,1,0:T(8,128)(2,1)S(1)} %get-tuple-element.29), channel_id=1, source_target_pairs={{0,3},{1,0},{2,1},{3,2},{4,7},{5,4},{6,5},{7,6},{8,11},{9,8},{10,9... | collective-permute-start | bytes 1179656 | tf_op jit(solution)/shard_map/ppermute | solution.py:29
  121.6 11.4 %copy-start.1 = (bf16[80,16,256]{2,1,0:T(8,128)(2,1)S(1)}, bf16[80,16,256]{2,1,0:T(8,128)(2,1)}, u32[]{:S(2)}) copy-start(bf16[80,16,256]{2,1,0:T(8,128)(2,1)} %copy-done) | copy-start | bytes 1966084
  121.6 11.4 %copy-start.4 = (f32[80,16,256]{2,1,0:T(8,128)S(1)}, f32[80,16,256]{2,1,0:T(8,128)}, u32[]{:S(2)}) copy-start(f32[80,16,256]{2,1,0:T(8,128)} %param.6) | copy-start | bytes 3932164
  121.6 51.2 %all-to-all-start.1 = ((bf16[64,3,16,256]{3,2,1,0:T(8,128)(2,1)}), bf16[64,3,16,256]{3,2,1,0:T(8,128)(2,1)S(1)}, u32[]{:S(2)}, u32[]{:S(2)}) async-start(bf16[64,3,16,256]{3,2,1,0:T(8,128)(2,1)} %get-tuple-element.17), calls=%async_computation.1 | async-start | bytes 3145728 | tf_op jit(solution)/shard_map/all_to_all | solution.py:277
  142.2 47.6 %copy-start.6 = (s32[80]{0:T(128)S(1)}, s32[80]{0:T(128)}, u32[]{:S(2)}) copy-start(s32[80]{0:T(128)} %copy-done.5) | copy-start | bytes 964
  174.2 15.3 %all-to-all-start.2 = ((f32[64,1,128]{2,1,0:T(1,128)}), f32[64,1,128]{2,1,0:T(1,128)S(1)}, u32[]{:S(2)}, u32[]{:S(2)}) async-start(f32[64,1,128]{2,1,0:T(1,128)} %broadcast_in_dim.67), calls=%async_computation.2 | async-start | bytes 65536 | tf_op jit(solution)/shard_map/all_to_all | solution.py:277
  180.4 9.6 %collective-permute-start.15 = (bf16[20,16,256]{2,1,0:T(8,128)(2,1)S(1)}, bf16[20,16,256]{2,1,0:T(8,128)(2,1)S(1)}, u32[]{:S(2)}, u32[]{:S(2)}) collective-permute-start(bf16[20,16,256]{2,1,0:T(8,128)(2,1)S(1)} %get-tuple-element.35), channel_id=1, source_target_pairs={{0,1},{1,2},{2,3},{3,0},{4,5},{5,6},{6,7},{7,4},{8,9},{9,10},{10,1... | collective-permute-start | bytes 491528 | tf_op jit(solution)/shard_map/ppermute | solution.py:29
  180.5 10.0 %collective-permute-start.16 = (bf16[20,16,256]{2,1,0:T(8,128)(2,1)S(1)}, bf16[20,16,256]{2,1,0:T(8,128)(2,1)S(1)}, u32[]{:S(2)}, u32[]{:S(2)}) collective-permute-start(bf16[20,16,256]{2,1,0:T(8,128)(2,1)S(1)} %get-tuple-element.34), channel_id=1, source_target_pairs={{0,2},{1,3},{2,0},{3,1},{4,6},{5,7},{6,4},{7,5},{8,10},{9,11},{10,... | collective-permute-start | bytes 491528 | tf_op jit(solution)/shard_map/ppermute | solution.py:29
  183.1 7.7 %collective-permute-start.17 = (bf16[20,16,256]{2,1,0:T(8,128)(2,1)S(1)}, bf16[20,16,256]{2,1,0:T(8,128)(2,1)S(1)}, u32[]{:S(2)}, u32[]{:S(2)}) collective-permute-start(bf16[20,16,256]{2,1,0:T(8,128)(2,1)S(1)} %get-tuple-element.33), channel_id=1, source_target_pairs={{0,3},{1,0},{2,1},{3,2},{4,7},{5,4},{6,5},{7,6},{8,11},{9,8},{10,9... | collective-permute-start | bytes 491528 | tf_op jit(solution)/shard_map/ppermute | solution.py:29
